TPU v7x, 32 devices: a whole 2x2x4 slice. The times are simulated.
32 devices in a mesh: gx: 2 (over core), gy: 4 (over y, x), gz: 4 (over z).
Axes of the slice: x: 2, y: 2, z: 4, core: 2. Of those that a mesh axis runs over, the one named last changes fastest.
Arguments:
- field: float32 [128, 128, 2048], P('gz', 'gx', 'gy'), may hold values from -6 to 6
Outputs:
- coeffs: float32 [128, 128, 2048], P('gz', 'gx', 'gy')
All inputs are finite; a program needn't handle non-finite values.
Results may differ from a plain program's by a relative error of at most 0.000075.
Values sent between devices are 32-bit elements; how exact they have to be, the bound alone decides.
No kernel may reach another device: no remote copies, remote signals or barrier semaphores. Data moves between devices by JAX's collectives and lax.ppermute only.
A program may use at most 128 MiB of HBM per device.

v0:
```python
import functools

import jax
import jax.numpy as jnp
import ml_dtypes
import numpy as np
from jax import lax
from jax.experimental import pallas as pl
from jax.experimental.pallas import tpu as pltpu
from jax.sharding import PartitionSpec as P

lift_alpha = -1.586134342
lift_beta = -0.05298011854
lift_gamma = 0.8829110762
lift_delta = 0.4435068522
lift_zeta = 1.149604398

BF = jnp.bfloat16
F32 = jnp.float32
MIB = 1024 * 1024


def periodic_lift(u):
    s, d = u[0::2].copy(), u[1::2].copy()
    d = d + lift_alpha * (s + np.roll(s, -1, 0))
    s = s + lift_beta * (np.roll(d, 1, 0) + d)
    d = d + lift_gamma * (s + np.roll(s, -1, 0))
    s = s + lift_delta * (np.roll(d, 1, 0) + d)
    out = np.empty_like(u)
    out[0::2] = s * lift_zeta
    out[1::2] = d / lift_zeta
    return out


@functools.lru_cache(None)
def blocks(n):
    current = np.eye(4 * n)
    found = []
    for level in range(3):
        full = periodic_lift(current)
        m = n >> level
        rows = full[m : 2 * m]
        found.append((rows[:, n : 2 * n], rows[:, :n], rows[:, 2 * n : 3 * n]))
        current = full[0::2]
    return found


def row_space(outer, rank):
    _, sizes, basis = np.linalg.svd(outer, full_matrices=False)
    assert sizes[rank:].max() < 1e-10
    basis = basis[:rank].copy()
    basis[np.abs(basis) < 1e-12] = 0.0
    return basis


LEFT_RANKS = (2, 3, 4)
RIGHT_RANKS = (2, 3, 3)


@functools.lru_cache(None)
def sides(n):
    out = []
    for level, (main, left, right) in enumerate(blocks(n)):
        cl = row_space(left, LEFT_RANKS[level])
        cr = row_space(right, RIGHT_RANKS[level])
        out.append((main, cl, left @ cl.T, cr, right @ cr.T))
    return out


def nested_space(outer):
    first = row_space(outer[0], 2)
    every = np.concatenate(outer)
    rest = every - every @ first.T @ first
    return np.concatenate([first, row_space(rest, 4)])


@functools.lru_cache(None)
def joint_sides(n):
    found = blocks(n)
    cl = nested_space([b[1] for b in found])
    cr = nested_space([b[2] for b in found])
    maps = [(b[0], b[1] @ cl.T, b[2] @ cr.T) for b in found]
    return cl, cr, maps


def hi_lo(table):
    table = np.asarray(table, np.float32)
    hi = table.astype(ml_dtypes.bfloat16)
    lo = (table - hi.astype(np.float32)).astype(ml_dtypes.bfloat16)
    return hi, lo


def stack_lhs(table):
    hi, lo = hi_lo(table)
    return np.concatenate([hi, lo, hi], axis=1)


def stack_rhs(table):
    hi, lo = hi_lo(table)
    return np.concatenate([hi, hi, lo], axis=0)


def split(values):
    hi = values.astype(BF)
    return hi, (values - hi.astype(F32)).astype(BF)


def dot(a, b):
    return lax.dot_general(a, b, (((1,), (0,)), ((), ())), preferred_element_type=F32)


def dot_t(a, b):
    return lax.dot_general(a, b, (((1,), (1,)), ((), ())), preferred_element_type=F32)


def spread_columns(table, step, width):
    out = np.zeros((table.shape[0], width))
    out[:, ::step] = table
    return out


VM = pl.BlockSpec(memory_space=pltpu.VMEM)
HB = pl.BlockSpec(memory_space=pltpu.HBM)


def in_hbm(array):
    return pltpu.with_memory_space_constraint(array, pltpu.HBM)


def vmem(shape, dtype=F32):
    return pltpu.VMEM(shape, dtype)


def params(mib):
    return pltpu.CompilerParams(vmem_limit_bytes=mib * MIB)


def x_send(field):
    nz, nx, ny = field.shape
    cl, cr, _ = joint_sides(nx)
    one = np.concatenate([cl, cr])
    group = 4
    wide = np.kron(np.eye(group), one)
    hi_rows, lo_rows = hi_lo(wide)
    pair = np.concatenate([hi_rows, lo_rows])
    height = 12 * group
    step = 8
    steps = nz // step
    order = [0, steps - 1] + list(range(1, steps - 1))
    flight = 2
    _, low, _, high, _ = sides(nz)[0]
    assert np.abs(low[:, :-step]).max() == 0 and np.abs(high[:, step:]).max() == 0

    def kernel(u_hbm, c_hbm, u_ref, out_ref, up_ref, down_ref, c_ref, u_sem, c_sem):
        table_copy = pltpu.make_async_copy(c_hbm, c_ref, c_sem)
        copies = [
            pltpu.make_async_copy(
                u_hbm.at[i * step : i * step + step], u_ref.at[i * step : i * step + step], u_sem.at[i]
            )
            for i in range(steps)
        ]
        for i in order[:flight]:
            copies[i].start()
        table_copy.start()
        table_copy.wait()
        table = c_ref[...]
        for turn, i in enumerate(order):
            copies[i].wait()
            if turn + flight < steps:
                copies[order[turn + flight]].start()
            for g in range(i * step // group, (i + 1) * step // group):
                hi, lo = split(u_ref[group * g : group * g + group].reshape(group * nx, ny))
                both = dot(table, hi)
                out_ref[height * g : height * g + height, :] = (
                    both[:height] + both[height:] + dot(table[:height], lo)
                )
            if i in order[:2]:
                combos, ref = (high, down_ref) if i == 0 else (low, up_ref)
                for c in range(2):
                    ref[c * nx : c * nx + nx, :] = weighted(
                        [(combos[c, z], lambda z=z: u_ref[z]) for z in range(i * step, (i + 1) * step)]
                    )

    return pl.pallas_call(
        kernel,
        in_specs=[HB, HB],
        out_specs=[VM] * 4,
        out_shape=[vmem((nz, nx, ny)), vmem((nz * 12, ny)), vmem((2 * nx, ny)), vmem((2 * nx, ny))],
        scratch_shapes=[
            pltpu.VMEM(pair.shape, BF),
            pltpu.SemaphoreType.DMA((steps,)),
            pltpu.SemaphoreType.DMA,
        ],
        compiler_params=params(16),
        name="x_send",
    )(in_hbm(field), in_hbm(jnp.asarray(pair)))


def x_exchange(message):
    count = lax.axis_size("gx")
    right = [(i, (i + 1) % count) for i in range(count)]
    if count == 2:
        return lax.ppermute(message, "gx", right)
    left = [(j, i) for i, j in right]
    rows, ny = message.shape
    grid = message.reshape(rows // 12, 12, ny)
    from_left = lax.ppermute(grid[:, :6], "gx", right)
    from_right = lax.ppermute(grid[:, 6:], "gx", left)
    return jnp.concatenate([from_left, from_right], axis=1).reshape(rows, ny)


def x_apply(field, halo):
    nz, nx, ny = field.shape
    _, _, maps = joint_sides(nx)
    main = np.concatenate([m for m, _, _ in maps])
    outer = np.concatenate([np.concatenate([l, r], axis=1) for _, l, r in maps])
    pad = np.zeros((main.shape[0], 4))
    tables = np.stack(
        [
            stack_lhs(np.concatenate([main, outer, pad], axis=1)),
            stack_lhs(np.concatenate([main, pad, outer], axis=1)),
        ]
    )
    rows = main.shape[0]
    counts = [nx, nx // 2, nx // 4]
    step = 8
    steps = nz // step

    combos = []
    for level, (_, cl, _, cr, _) in enumerate(sides(ny)):
        both = np.zeros((8, 128))
        assert np.abs(cl[:, : ny - 64]).max() == 0 and np.abs(cr[:, 64:]).max() == 0
        both[: cl.shape[0], 64:] = cl[:, ny - 64 :]
        both[4 : 4 + cr.shape[0], :64] = cr[:, :64]
        combos.append(stack_lhs(both))
    combos = np.stack(combos)

    def kernel(u_ref, r_ref, t_ref, c_ref, x1, x2, x3, right_ref, left_ref, e1, e2, e3):
        i = pl.program_id(0)
        lanes = lax.broadcasted_iota(jnp.int32, (rows, 128), 1)
        for z in range(step):
            start = pl.multiple_of(i * (12 * step) + 24 * (z // 2) + 8 * (z % 2), 8)
            hi, lo = split(u_ref[i * step + z])
            rhi, rlo = split(r_ref[pl.ds(start, 16), :])
            stacked = jnp.concatenate([hi, rhi, hi, rhi, lo, rlo], axis=0)
            got = dot(t_ref[z % 2], stacked)
            edge = jnp.where(lanes < 64, got[:, :128], got[:, ny - 128 :])
            ehi, elo = split(edge)
            estack = jnp.concatenate([ehi, ehi, elo], axis=1)
            at = 0
            for ref, eref, n in zip((x1, x2, x3), (e1, e2, e3), counts):
                where = pl.ds(pl.multiple_of((i * step + z) * n, 16), n)
                ref[i * step + z] = got[at : at + n]
                eref[where, :] = estack[at : at + n]
                at += n

        @pl.when(i == steps - 1)
        def _():
            row = 0
            for level, (eref, n) in enumerate(zip((e1, e2, e3), counts)):
                got = dot_t(c_ref[level], eref[...])
                for j in range(nz * n // 512):
                    for c in range(LEFT_RANKS[level]):
                        right_ref[row : row + 1, :] = got[c : c + 1, 512 * j : 512 * j + 512]
                        if c < RIGHT_RANKS[level]:
                            left_ref[row : row + 1, :] = got[4 + c : 5 + c, 512 * j : 512 * j + 512]
                        else:
                            left_ref[row : row + 1, :] = jnp.zeros((1, 512), F32)
                        row += 1
            right_ref[row:, :] = jnp.zeros((24 - row, 512), F32)
            left_ref[row:, :] = jnp.zeros((24 - row, 512), F32)

    return pl.pallas_call(
        kernel,
        grid=(steps,),
        in_specs=[VM] * 4,
        out_specs=[VM] * 5,
        out_shape=[vmem((nz, n, ny)) for n in counts] + [jax.ShapeDtypeStruct((24, 512), F32)] * 2,
        scratch_shapes=[pltpu.VMEM((nz * n, 384), BF) for n in counts],
        compiler_params=params(24),
        name="x_apply",
    )(field, halo, jnp.asarray(tables), jnp.asarray(combos))


def add(a, b):
    if a is None:
        return b
    return a if b is None else a + b


def scale(a, c):
    return None if a is None else a * np.float32(c)


def open_lift(values, first, last):
    get = values.get
    low, high = first // 2 - 3, last // 2 + 4
    s = {i: get(2 * i) for i in range(low, high + 1)}
    d = {i: get(2 * i + 1) for i in range(low, high + 1)}
    pick = lambda t, i: t.get(i)
    d1 = {i: add(d[i], scale(add(s[i], pick(s, i + 1)), lift_alpha)) for i in range(low, high + 1)}
    s1 = {i: add(s[i], scale(add(pick(d1, i - 1), d1[i]), lift_beta)) for i in range(low, high + 1)}
    d2 = {i: add(d1[i], scale(add(s1[i], pick(s1, i + 1)), lift_gamma)) for i in range(low, high + 1)}
    s2 = {i: add(s1[i], scale(add(pick(d2, i - 1), d2[i]), lift_delta)) for i in range(low, high + 1)}
    out = {}
    for z in range(first, last + 1):
        if z % 2:
            out[z] = scale(d2[z // 2], 1.0 / lift_zeta)
        else:
            out[z] = scale(s2[z // 2], lift_zeta)
    return out


def lows(values, first, last):
    got = open_lift(values, 2 * first, 2 * last)
    return {i: got[2 * i] for i in range(first, last + 1) if got[2 * i] is not None}


def own_levels(values, nz, level):
    if level >= 1:
        values = lows(values, -2, nz // 2 + 1)
    if level >= 2:
        values = lows(values, -3, nz // 4 + 2)
    return open_lift(values, 0, (nz >> level) - 1)


def z_tables(nz):
    out = []
    for _, cl, pl_, cr, pr in sides(nz):
        out.append((np.concatenate([cl, cr]), np.concatenate([pl_, pr], axis=1)))
    return out


def weighted(parts):
    total = None
    for scalar, get in parts:
        if abs(scalar) < 1e-12:
            continue
        term = get() * np.float32(scalar)
        total = term if total is None else total + term
    return total


def z_first(x2, x3, halo):
    nz, _, ny = x2.shape
    tables = [t for t, _ in z_tables(nz)]
    counts = [x2.shape[1], x3.shape[1]]
    groups = ny // 128

    def kernel(x2, x3, r_ref, o2, o3, of, y2, y3):
        for level, ref, out, own, table, n in zip((1, 2), (x2, x3), (o2, o3), (y2, y3), tables[1:], counts):

            def body(k, _, level=level, ref=ref, out=out, own=own, table=table, n=n):
                row = pl.multiple_of((k // groups) * 8, 8)
                lane = pl.multiple_of((k % groups) * 128, 128)
                get = {}
                for z in range(nz):
                    get[z] = ref[z, pl.ds(row, 8), pl.ds(lane, 128)]
                for z, value in own_levels(get, nz, level).items():
                    own[z, pl.ds(row, 8), pl.ds(lane, 128)] = value
                for c in range(table.shape[0]):
                    out[pl.ds(pl.multiple_of(c * n + row, 8), 8), pl.ds(lane, 128)] = weighted(
                        [(table[c, z], lambda z=z: get[z]) for z in range(nz)]
                    )
                return 0

            lax.fori_loop(0, (n // 8) * groups, body, 0)
        for c in range(4):
            got = weighted(
                [(tables[0][c, z], lambda z=z: r_ref[12 * z : 12 * z + 12, :]) for z in range(nz)]
            )
            of[4 * c : 4 * c + 2, :] = got[0:2]
            of[4 * c + 2 : 4 * c + 4, :] = got[6:8]

    return pl.pallas_call(
        kernel,
        in_specs=[VM] * 3,
        out_specs=[VM] * 5,
        out_shape=[vmem((t.shape[0] * n, ny)) for t, n in zip(tables[1:], counts)]
        + [vmem((16, ny)), vmem((nz // 2, counts[0], ny)), vmem((nz // 4, counts[1], ny))],
        compiler_params=params(16),
        cost_estimate=pl.CostEstimate(flops=20_000_000, bytes_accessed=6_000_000, transcendentals=0),
        name="z_first",
    )(x2, x3, halo)


def y_tables(ny, spread):
    out = []
    for level, (main, _, left, _, right) in enumerate(sides(ny)):
        step = (1 << level) if spread else 1
        width = ny if spread else ny >> level
        fit = lambda t: spread_columns(t.T, step, width)
        out.append((fit(main), fit(left), fit(right)))
    return out


def halo_rows(level, chunk, nz, counts):
    start = 0
    for below in range(level):
        start += (nz * counts[below] // 512) * LEFT_RANKS[below]
    return start + chunk * LEFT_RANKS[level]


LEFT_AT, RIGHT_AT = 32, 56


def halo_base(left, right, level, nz, counts):
    base = np.zeros((128, left.shape[1]))
    for chunk in range(nz * counts[level] // 512):
        row = halo_rows(level, chunk, nz, counts)
        base[LEFT_AT + row : LEFT_AT + row + left.shape[0]] = left
        base[RIGHT_AT + row : RIGHT_AT + row + right.shape[0]] = right
    return base


def turned(left_ref, right_ref):
    wide = jnp.concatenate(
        [jnp.zeros((LEFT_AT, 512), F32), left_ref[...], right_ref[...], jnp.zeros((48, 512), F32)], axis=0
    )
    return wide.T


def band_tables(level, nz, counts, ny):
    assert ny == 512
    main, left, right = y_tables(ny, True)[level]
    base = halo_base(left, right, level, nz, counts)
    own, edge = [], []
    for j in range(2):
        cols = slice(256 * j, 256 * j + 256)
        own.append(stack_rhs(main[cols, cols]))
        tile = base[:, cols].copy()
        if j == 0:
            tile[:32] = main[256:288, cols]
            assert np.abs(main[288:, cols]).max() == 0
        else:
            tile[96:] = main[224:256, cols]
            assert np.abs(main[:224, cols]).max() == 0
        edge.append(stack_rhs(tile))
    return np.stack(own), np.stack(edge)


def three(values):
    hi, lo = split(values)
    return jnp.concatenate([hi, lo, hi], axis=1)


def banded(rows, edge, own_ref, edge_ref):
    edges = three(edge)
    out = []
    for j in range(2):
        own = three(rows[:, 256 * j : 256 * j + 256])
        out.append(dot(own, own_ref[j]) + dot(edges, edge_ref[j]))
    return jnp.concatenate(out, axis=1)


def plain_edge(rows):
    lanes = lax.broadcasted_iota(jnp.int32, (rows.shape[0], 128), 1)
    before = jnp.where(lanes >= 96, rows[:, 128:256], 0.0)
    return jnp.where(lanes < 32, rows[:, 256:384], before)


def late_rows(counts, ny):
    return [3 * counts[1] * (ny // 2) // ny, 4 * counts[2] * (ny // 4) // ny, 8, 8]


def y_messages(combined, from_left, from_right, nz, band_one):
    c2, c3, cf = combined
    ny = c2.shape[1]
    tables = z_tables(nz)
    nums = [t.shape[0] for t, _ in tables]
    counts = [2 * c2.shape[0] // nums[1], c2.shape[0] // nums[1], c3.shape[0] // nums[2]]
    mains, halos, coefs = [], [], []
    for level, (main, left, right) in enumerate(y_tables(ny, False)):
        mains.append(stack_rhs(main))
        halos.append(stack_rhs(halo_base(left, right, level, nz, counts)))
        chunks = nz * counts[level] // 512
        per = 512 // counts[level]
        table = tables[level][0]
        coef = np.zeros((nums[level], per, 128), np.float32)
        for c in range(nums[level]):
            for zz in range(per):
                for chunk in range(chunks):
                    row = halo_rows(level, chunk, nz, counts)
                    for lane in range(LEFT_RANKS[level]):
                        for base in (LEFT_AT, RIGHT_AT):
                            coef[c, zz, base + row + lane] = table[c, chunk * per + zz]
        coefs.append(coef.reshape(nums[level] * per, 128))
    heights = late_rows(counts, ny)
    height = sum(heights)

    def kernel(c2, c3, cf, fl, fr, own1, edge1, m2, m3, h2, h3, k1, k2, k3, up_ref, down_ref):
        halo = turned(fl, fr)

        def reduced(k, n, num):
            per = 512 // n
            extra = []
            for c in range(num):
                total = None
                for zz in range(per):
                    if np.abs(coefs_of[n][c * per + zz]).max() > 1e-12:
                        term = halo[zz * n : zz * n + n] * k[c * per + zz : c * per + zz + 1, :]
                        total = term if total is None else total + term
                extra.append(total)
            return extra

        coefs_of = dict(zip(counts, coefs))
        got = []
        for c_ref, m, h, k, n, num in zip((c2, c3), (m2, m3), (h2, h3), (k2, k3), counts[1:], nums[1:]):
            extra = jnp.concatenate(reduced(k, n, num), axis=0)
            got.append(dot(three(c_ref[...]), m[...]) + dot(three(extra), h[...]))
        frame = cf[...]
        frame = banded(frame, plain_edge(frame), own1, edge1)
        ones = reduced(k1, counts[0], 4)
        rows8 = lax.broadcasted_iota(jnp.int32, (8, 128), 0)
        for side, ref in enumerate((up_ref, down_ref)):
            at = 0
            for level in (1, 2):
                n, width = counts[level], ny >> level
                ranks = LEFT_RANKS if side == 0 else RIGHT_RANKS
                first = 0 if side == 0 else LEFT_RANKS[level] * n
                total = ranks[level] * n
                tall = heights[level - 1]
                for part in range(1 << level):
                    use = max(min(tall, total - part * tall), 0)
                    lanes = slice(part * width, (part + 1) * width)
                    if use > 0:
                        ref[at : at + use, lanes] = got[level - 1][
                            first + part * tall : first + part * tall + use
                        ]
                    if use < tall:
                        ref[at + use : at + tall, lanes] = jnp.zeros((tall - use, width), F32)
                at += tall
            ref[at : at + 8, :] = frame[8 * side : 8 * side + 8]
            at += 8
            turn = jnp.concatenate(ones[2 * side : 2 * side + 2], axis=0).T
            both = []
            for start in (LEFT_AT, RIGHT_AT):
                v = turn[start : start + 8]
                v = v + pltpu.roll(v, 4, 0)
                both.append(v + pltpu.roll(v, 2, 0))
            ref[at:, :128] = jnp.where(rows8 < 2, both[0], both[1])
            ref[at:, 128:] = jnp.zeros((8, ny - 128), F32)

    return pl.pallas_call(
        kernel,
        in_specs=[VM] * 14,
        out_specs=[VM] * 2,
        out_shape=[vmem((height, ny))] * 2,
        compiler_params=params(24),
        name="y_messages",
    )(
        c2,
        c3,
        cf,
        from_left,
        from_right,
        *band_one,
        *[jnp.asarray(t) for t in mains[1:]],
        *[jnp.asarray(t) for t in halos[1:]],
        *[jnp.asarray(t) for t in coefs],
    )


def touched_layers(nz):
    one, two, three = [np.abs(p).max(axis=1) > 1e-12 for _, p in z_tables(nz)]
    hit = lambda z: one[z] or (z % 2 == 0 and two[z // 2]) or (z % 4 == 0 and three[z // 4])
    return [z for z in range(nz) if hit(z)]


def main_part(xs, from_left, from_right, below, above, bands):
    nz, nx, ny = xs[0].shape
    counts = [nx, nx // 2, nx // 4]
    changed = touched_layers(nz)
    untouched = [z for z in range(nz) if z not in changed]
    groups = ny // 128
    _, _, maps = joint_sides(nx)
    x_table = stack_lhs(maps[0][0])
    masks = []
    for level in range(3):
        chunks = nz * counts[level] // 512
        per = 512 // counts[level]
        lanes_of = np.zeros((chunks, 128))
        for chunk in range(chunks):
            row = halo_rows(level, chunk, nz, counts)
            for base in (LEFT_AT, RIGHT_AT):
                lanes_of[chunk, base + row : base + row + LEFT_RANKS[level]] = 1.0
        if level == 0:
            masks.append(lanes_of)
        else:
            own = sides(nz)[level][0]
            lanes = np.einsum("ocz,cl->ozl", own.reshape(own.shape[0], chunks, per), lanes_of)
            masks.append(lanes.reshape(-1, 128))
    masks = [np.concatenate([m, np.zeros((-m.shape[0] % 8, 128))]).astype(np.float32) for m in masks]

    def kernel(x1, x2, x3, fl, fr, b1, a1, o1, e1, o2, e2, o3, e3, xt, k1, k2, k3, out_ref, w_ref, hbm, w2, halo_ref, sem):
        halo_ref[...] = turned(fl, fr)
        lanes = lax.broadcasted_iota(jnp.int32, (8, 128), 1)
        wide = lax.broadcasted_iota(jnp.int32, (32, 128), 1)
        after, before = wide < 32, wide >= 96

        def in_y(x, level, row, tall, own, edge, mk):
            n = counts[level]
            per = 512 // n
            layers = nz >> level
            values = x[:, row : row + tall, :]
            turns = [halo_ref[zz * n + row : zz * n + row + tall, :] for zz in range(per)]
            edges = []
            for z in range(layers):
                if level == 0:
                    turn = turns[z % per] * mk[z // per : z // per + 1, :]
                else:
                    turn = None
                    for zz in range(per):
                        if np.abs(masks[level][z * per + zz]).max() > 1e-12:
                            turn = add(turn, turns[zz] * mk[z * per + zz : z * per + zz + 1, :])
                edges.append(
                    jnp.where(
                        after[:tall],
                        values[z, :, 256:384],
                        jnp.where(before[:tall], values[z, :, 128:256], turn),
                    )
                )
            got = banded(
                values.reshape(layers * tall, ny), jnp.concatenate(edges, axis=0), own, edge
            )
            return {z: got[tall * z : tall * z + tall] for z in range(layers)}

        def store(to, values, row, indices, height=None):
            for z in indices:
                for q in range(groups):
                    piece = values[z][:, 128 * q : 128 * q + 128]
                    tall = piece.shape[0]
                    if height is None:
                        to[q, z, row : row + tall, :] = piece
                    else:
                        to[q, z * height + row : z * height + row + tall, :] = piece

        for row in range(0, counts[0], 16):
            got = own_levels(in_y(x1, 0, row, 16, o1, e1, k1), nz, 0)
            store(out_ref, got, row, range(nz))

        def leaving(layers):
            return [
                pltpu.make_async_copy(
                    out_ref.at[q, z], hbm.at[z, :, 128 * q : 128 * q + 128], sem.at[z]
                )
                for z in layers
                for q in range(groups)
            ]

        copies = leaving([z for z in untouched if z % 2])
        for copy in copies:
            copy.start()

        store(w2, in_y(x2, 1, 0, counts[1], o2, e2, k2), 0, range(nz // 2), counts[1])
        got = in_y(x3, 2, 0, counts[2], o3, e3, k3)
        for z in range(nz // 4):
            for row in range(0, counts[2], 8):
                where = pl.ds(2 * z * counts[1] + 2 * row, 8, stride=2)
                for q in range(groups):
                    piece = got[z][row : row + 8, 128 * q : 128 * q + 128]
                    w2[q, where, :] = jnp.where(lanes % 4 == 0, piece, w2[q, where, :])

        def merge(k, _):
            row = pl.multiple_of((k // groups) * 8, 8)
            q = k % groups
            where = pl.ds(2 * row, 8, stride=2)
            for z in range(nz // 2):
                inner = w2[q, pl.ds(pl.multiple_of(z * counts[1] + row, 8), 8), :]
                out_ref[q, 2 * z, where, :] = jnp.where(lanes % 2 == 0, inner, out_ref[q, 2 * z, where, :])
            return 0

        lax.fori_loop(0, (counts[1] // 8) * groups, merge, 0)
        more = leaving([z for z in untouched if z % 2 == 0])
        for copy in more:
            copy.start()

        early = []
        for ref in (b1, a1):
            for c in range(2):
                hi, lo = split(ref[c * nx : c * nx + nx, :])
                early.append(dot(xt[...], jnp.concatenate([hi, hi, lo], axis=0)))
        early = jnp.concatenate(early, axis=0)
        w_ref[...] = banded(early, plain_edge(early), o1, e1)

        for copy in copies + more:
            copy.wait()

    flat = [t for band in bands for t in band]
    return pl.pallas_call(
        kernel,
        in_specs=[VM] * 17,
        out_specs=[VM, VM, HB],
        out_shape=[
            vmem((groups, nz, nx, 128)),
            vmem((4 * nx, ny)),
            pltpu.HBM((nz, nx, ny), F32),
        ],
        scratch_shapes=[
            pltpu.VMEM((groups, nz // 2 * counts[1], 128), F32),
            pltpu.VMEM((512, 128), F32),
            pltpu.SemaphoreType.DMA((nz,)),
        ],
        compiler_params=params(32),
        cost_estimate=pl.CostEstimate(
            flops=8_000_000_000, bytes_accessed=20_000_000, transcendentals=0
        ),
        name="main_part",
    )(*xs, from_left, from_right, below, above, *flat, jnp.asarray(x_table), *[jnp.asarray(m) for m in masks])


def z_apply(inner, partial, early, from_left, from_right):
    groups, nz, nx, _ = inner.shape
    ny = groups * 128
    maps = [p for _, p in z_tables(nz)]
    counts = [nx, nx // 2, nx // 4]
    tables = []
    for level in (1, 2):
        width = ny >> level
        hi = spread_columns(np.eye(width), 1 << level, ny).astype(ml_dtypes.bfloat16)
        tables.append(np.concatenate([hi, hi]))
    heights = late_rows(counts, ny)
    _, _, x_maps = joint_sides(nx)
    frame = np.zeros((4 * nx, 16))
    for c in range(4):
        frame[c * nx : c * nx + nx, 4 * c : 4 * c + 2] = x_maps[0][1][:, :2]
        frame[c * nx : c * nx + nx, 4 * c + 2 : 4 * c + 4] = x_maps[0][2][:, :2]
        assert np.abs(x_maps[0][1][:, 2:]).max() < 1e-12 and np.abs(x_maps[0][2][:, 2:]).max() < 1e-12
    _, left, right = y_tables(ny, True)[0]
    side_hi, side_lo = hi_lo(np.concatenate([left, right, np.zeros((4, ny))]))
    side_rows = np.concatenate([side_hi, side_hi, side_lo, np.zeros((104, ny), side_hi.dtype)])
    touched = touched_layers(nz)

    def kernel(in_ref, base_hbm, w_ref, fl, fr, t2, t3, xf, yf, out_hbm, s1, s2, s3, buf, sem):
        del base_hbm
        s3[...] = jnp.zeros(s3.shape, F32)
        at = heights[0] + heights[1]
        hi, lo = split(jnp.concatenate([fl[at : at + 8, :], fr[at : at + 8, :]], axis=0))
        at += 8
        none = jnp.zeros((104, 128), F32)
        turn = []
        for ref in (fl, fr):
            values = ref[at : at + 8, :128]
            high = values.astype(BF).astype(F32)
            turn.append(jnp.concatenate([high, values - high, high, none], axis=0).T.astype(BF))
        left_hand = jnp.concatenate([jnp.concatenate(turn, axis=0), xf[...]], axis=1)
        first = w_ref[...] + dot(left_hand, jnp.concatenate([yf[...], hi, hi, lo], axis=0))
        for c in range(4):
            for q in range(groups):
                s1[c, q] = first[c * nx : c * nx + nx, 128 * q : 128 * q + 128]
        at = 0
        for level, table, to in ((1, t2, s2), (2, t3, s3)):
            width, tall, n = ny >> level, heights[level - 1], counts[level]
            flat = jnp.concatenate(
                [
                    ref[at : at + tall, p * width : p * width + width]
                    for ref in (fl, fr)
                    for p in range(1 << level)
                ],
                axis=0,
            )
            hi, lo = split(flat)
            got = dot(jnp.concatenate([hi, lo], axis=1), table[...])
            for c in range(LEFT_RANKS[level] + RIGHT_RANKS[level]):
                start = c * n
                if c >= LEFT_RANKS[level]:
                    start += (tall << level) - LEFT_RANKS[level] * n
                for q in range(groups):
                    piece = got[start : start + n, 128 * q : 128 * q + 128]
                    if level == 1:
                        to[c, q] = piece
                    else:
                        to[c, q, pl.ds(0, n, stride=2), :] = piece
            at += tall

        lanes = lax.broadcasted_iota(jnp.int32, (8, 128), 1)
        even_lane = lanes % 2 == 0
        third_cell = (lax.broadcasted_iota(jnp.int32, (8, 128), 0) % 2 + lanes % 4) == 0

        def summed(table_row, get):
            total = None
            for c, scalar in enumerate(table_row):
                if abs(scalar) > 1e-12:
                    total = add(total, get(c) * np.float32(scalar))
            return total

        copies = []
        for slot, z in enumerate(touched):

            for t in range(nx // 16):
                full, half = 16 * t, 8 * t
                for q in range(groups):
                    if z % 2:
                        for more in (0, 8):
                            rows = pl.ds(full + more, 8)
                            extra = summed(maps[0][z], lambda c: s1[c, q, rows, :])
                            buf[slot, q, rows, :] = add(in_ref[q, z, rows, :], extra)
                        continue
                    evens = pl.ds(16 * t, 8, stride=2)
                    odds = pl.ds(16 * t + 1, 8, stride=2)
                    extra = summed(maps[0][z], lambda c: s1[c, q, odds, :])
                    buf[slot, q, odds, :] = add(in_ref[q, z, odds, :], extra)
                    rows = pl.ds(half, 8)
                    extra = summed(maps[1][z // 2], lambda c: s2[c, q, rows, :])
                    if z % 4 == 0:
                        third = summed(maps[2][z // 4], lambda c: s3[c, q, rows, :])
                        third = 0.0 if third is None else third
                        extra = jnp.where(third_cell, third, 0.0 if extra is None else extra)
                    one = summed(maps[0][z], lambda c: s1[c, q, evens, :])
                    if one is not None:
                        extra = jnp.where(even_lane, 0.0 if extra is None else extra, one)
                    buf[slot, q, evens, :] = add(in_ref[q, z, evens, :], extra)
            for q in range(groups):
                copy = pltpu.make_async_copy(
                    buf.at[slot, q], out_hbm.at[z, :, 128 * q : 128 * q + 128], sem.at[slot]
                )
                copy.start()
                copies.append(copy)
        for copy in copies:
            copy.wait()

    return pl.pallas_call(
        kernel,
        in_specs=[VM, HB] + [VM] * 7,
        out_specs=HB,
        out_shape=jax.ShapeDtypeStruct((nz, nx, ny), F32),
        input_output_aliases={1: 0},
        scratch_shapes=[
            pltpu.VMEM((4, groups, nx, 128), F32),
            pltpu.VMEM((maps[1].shape[1], groups, nx // 2, 128), F32),
            pltpu.VMEM((maps[2].shape[1], groups, nx // 2, 128), F32),
            pltpu.VMEM((len(touched), groups, nx, 128), F32),
            pltpu.SemaphoreType.DMA((len(touched),)),
        ],
        compiler_params=params(24),
        name="z_apply",
    )(
        inner,
        partial,
        early,
        from_left,
        from_right,
        *[jnp.asarray(t) for t in tables],
        jnp.asarray(stack_lhs(frame)),
        jnp.asarray(side_rows),
    )


def swap(to_right, to_left, axis):
    count = lax.axis_size(axis)
    right = [(i, (i + 1) % count) for i in range(count)]
    left = [(j, i) for i, j in right]
    return lax.ppermute(to_right, axis, right), lax.ppermute(to_left, axis, left)


def local(field):
    nz, nx, ny = field.shape
    counts = [nx, nx // 2, nx // 4]
    bands = [[jnp.asarray(t) for t in band_tables(level, nz, counts, ny)] for level in range(3)]
    field, message, up, down = x_send(field)
    halo = x_exchange(message)
    below, above = swap(up, down, "gz")
    x1, x2, x3, to_right, to_left = x_apply(field, halo)
    from_left, from_right = swap(to_right, to_left, "gy")
    *combined, own2, own3 = z_first(x2, x3, halo)
    up, down = y_messages(combined, from_left, from_right, nz, bands[0])
    late_below, late_above = swap(up, down, "gz")
    inner, early, partial = main_part((x1, own2, own3), from_left, from_right, below, above, bands)
    return z_apply(inner, partial, early, late_below, late_above)


def solution(mesh):
    placed = (P("gz", "gx", "gy"),)
    return jax.shard_map(
        local, mesh=mesh, in_specs=placed, out_specs=P("gz", "gx", "gy"), check_vma=False
    )
```

profile of v0, /device:TPU:0, one launch (start us, length us, event | category | flops | bytes accessed | tf_op | source)
XLA Modules:
  0.0 31.5 jit_solution(17405971319738553721)
XLA Ops:
  0.0 3.5 %x_send.1 = (f32[32,64,512]{2,1,0:T(8,128)S(1)}, f32[384,512]{1,0:T(8,128)S(1)}, f32[128,512]{1,0:T(8,128)S(1)}, f32[128,512]{1,0:T(8,128)S(1)}) custom-call(f32[32,64,512]{2,1,0:T(8,128)} %u_hbm.1, bf16[96,256]{1,0:T(8,128)(2,1)} %constant.54.clone.c_hbm), custom_call_target="tpu_custom_call" | custom-call | tf_op jit(solution)/shard_map/x_send/pallas_call | solution.py:184
  3.5 0.5 %collective-permute-start = (f32[384,512]{1,0:T(8,128)S(1)}, f32[384,512]{1,0:T(8,128)S(1)}, u32[]{:S(2)}, u32[]{:S(2)}) collective-permute-start(f32[384,512]{1,0:T(8,128)S(1)} %get-tuple-element.25), channel_id=1, source_target_pairs={{0,16},{16,0},{1,17},{17,1},{2,18},{18,2},{3,19},{19,3},{4,20},{20... | collective-permute-start | bytes 2359304 | tf_op jit(solution)/shard_map/ppermute | solution.py:203
  4.0 2.6 %collective-permute-start.3 = (f32[128,512]{1,0:T(8,128)S(1)}, f32[128,512]{1,0:T(8,128)S(1)}, u32[]{:S(2)}, u32[]{:S(2)}) collective-permute-start(f32[128,512]{1,0:T(8,128)S(1)} %get-tuple-element.33), channel_id=1, source_target_pairs={{0,1},{1,2},{2,3},{3,0},{4,5},{5,6},{6,7},{7,4},{8,9},{9,10},{10,1... | collective-permute-start | bytes 786440 | tf_op jit(solution)/shard_map/ppermute | solution.py:853
  6.7 2.1 %collective-permute-start.4 = (f32[128,512]{1,0:T(8,128)S(1)}, f32[128,512]{1,0:T(8,128)S(1)}, u32[]{:S(2)}, u32[]{:S(2)}) collective-permute-start(f32[128,512]{1,0:T(8,128)S(1)} %get-tuple-element.34), channel_id=1, source_target_pairs={{1,0},{2,1},{3,2},{0,3},{5,4},{6,5},{7,6},{4,7},{9,8},{10,9},{11,1... | collective-permute-start | bytes 786440 | tf_op jit(solution)/shard_map/ppermute | solution.py:853
  8.8 0.0 collective-permute-done.r_ref
  8.8 0.0 copy-done.13
  8.8 0.0 copy-done.9
  8.8 0.0 copy-start
  8.8 0.0 copy-start.1
  8.8 0.0 copy-start.3
  8.8 0.0 copy-start.4
  8.9 0.0 copy-start.6
  8.9 0.0 copy-start.8
  8.9 0.0 copy-start.10
  8.9 0.0 copy-start.12
  8.9 0.0 copy-start.14
  8.9 2.6 %x_apply.1 = (f32[32,64,512]{2,1,0:T(8,128)S(1)}, f32[32,32,512]{2,1,0:T(8,128)S(1)}, f32[32,16,512]{2,1,0:T(8,128)S(1)}, f32[24,512]{1,0:T(8,128)S(1)}, f32[24,512]{1,0:T(8,128)S(1)}) custom-call(f32[32,64,512]{2,1,0:T(8,128)S(1)} %get-tuple-element.24.u_ref, f32[384,512]{1,0:T(8,128)S(1)} %collective-permute-done.r_ref, ...), custom_call_target="tpu_custom_call" | custom-call | tf_op jit(solution)/shard_map/x_apply/pallas_call | solution.py:273
  11.6 0.0 copy-start.16
  11.6 0.0 copy-start.17
  11.6 0.0 copy-start.18
  11.6 0.0 copy-start.19
  11.6 0.0 copy-start.20
  11.6 0.0 copy-start.21
  11.6 0.0 copy-start.22
  11.7 1.7 %collective-permute-start.1 = (f32[24,512]{1,0:T(8,128)S(1)}, f32[24,512]{1,0:T(8,128)S(1)}, u32[]{:S(2)}, u32[]{:S(2)}) collective-permute-start(f32[24,512]{1,0:T(8,128)S(1)} %get-tuple-element.31), channel_id=1, source_target_pairs={{0,4},{4,8},{8,12},{12,0},{1,5},{5,9},{9,13},{13,1},{2,6},{6,10},{... | collective-permute-start | bytes 147464 | tf_op jit(solution)/shard_map/ppermute | solution.py:853
  13.3 1.3 %collective-permute-start.2 = (f32[24,512]{1,0:T(8,128)S(1)}, f32[24,512]{1,0:T(8,128)S(1)}, u32[]{:S(2)}, u32[]{:S(2)}) collective-permute-start(f32[24,512]{1,0:T(8,128)S(1)} %get-tuple-element.32), channel_id=1, source_target_pairs={{4,0},{8,4},{12,8},{0,12},{5,1},{9,5},{13,9},{1,13},{6,2},{10,6},{... | collective-permute-start | bytes 147464 | tf_op jit(solution)/shard_map/ppermute | solution.py:853
  14.6 2.4 %z_first.1 = (f32[192,512]{1,0:T(8,128)S(1)}, f32[112,512]{1,0:T(8,128)S(1)}, f32[16,512]{1,0:T(8,128)S(1)}, f32[16,32,512]{2,1,0:T(8,128)S(1)}, f32[8,16,512]{2,1,0:T(8,128)S(1)}) custom-call(f32[32,32,512]{2,1,0:T(8,128)S(1)} %get-tuple-element.27.x2, f32[32,16,512]{2,1,0:T(8,128)S(1)} %get-tuple-element.28.x3, f32[384,512]{1,0:T(8,128)S(1)} %collective-permute-done.r_ref), custom_call_target="tpu_custom_call" | custom-call | flops 20000000 | bytes 6000000 | tf_op jit(solution)/shard_map/z_first/pallas_call | solution.py:375
  17.0 0.0 collective-permute-done.1.fl
  17.0 0.4 %collective-permute-done.2.fr = f32[24,512]{1,0:T(8,128)S(1)} collective-permute-done((f32[24,512]{1,0:T(8,128)S(1)}, f32[24,512]{1,0:T(8,128)S(1)}, u32[]{:S(2)}, u32[]{:S(2)}) %collective-permute-start.2) | collective-permute-done | bytes 49184 | tf_op jit(solution)/shard_map/ppermute | solution.py:853
  17.5 0.0 copy-done.4
  17.5 0.0 copy-done.6
  17.5 0.0 copy-done.8
  17.5 0.0 copy-done.10
  17.5 0.0 copy-done.12
  17.5 0.0 copy-done.14
  17.5 0.9 %y_messages.1 = (f32[80,512]{1,0:T(8,128)S(1)}, f32[80,512]{1,0:T(8,128)S(1)}) custom-call(f32[192,512]{1,0:T(8,128)S(1)} %get-tuple-element.38.c2, f32[112,512]{1,0:T(8,128)S(1)} %get-tuple-element.39.c3, f32[16,512]{1,0:T(8,128)S(1)} %get-tuple-element.40.cf, f32[24,512]{1,0:T(8,128)S(1)} %collective-permute-done.1.fl, ...), custom_call_target="tpu_custom_call" | custom-call | tf_op jit(solution)/shard_map/y_messages/pallas_call | solution.py:544
  18.4 0.2 collective-permute-start.5
  18.6 3.7 %collective-permute-start.6 = (f32[80,512]{1,0:T(8,128)S(1)}, f32[80,512]{1,0:T(8,128)S(1)}, u32[]{:S(2)}, u32[]{:S(2)}) collective-permute-start(f32[80,512]{1,0:T(8,128)S(1)} %get-tuple-element.42), channel_id=1, source_target_pairs={{1,0},{2,1},{3,2},{0,3},{5,4},{6,5},{7,6},{4,7},{9,8},{10,9},{11,1... | collective-permute-start | bytes 491528 | tf_op jit(solution)/shard_map/ppermute | solution.py:853
  22.3 0.0 collective-permute-done.3.b1
  22.3 0.0 collective-permute-done.4.a1
  22.3 0.0 copy-start.2
  22.3 0.0 copy-start.5
  22.4 0.0 copy-start.7
  22.4 0.0 copy-start.11
  22.4 6.8 %main_part.1 = (f32[4,32,64,128]{3,2,1,0:T(8,128)S(1)}, f32[256,512]{1,0:T(8,128)S(1)}, f32[32,64,512]{2,1,0:T(8,128)}) custom-call(f32[32,64,512]{2,1,0:T(8,128)S(1)} %get-tuple-element.26.x1, f32[16,32,512]{2,1,0:T(8,128)S(1)} %get-tuple-element.29.x2, f32[8,16,512]{2,1,0:T(8,128)S(1)} %get-tuple-element.30.x3, f32[24,512]{1,0:T(8,128)S(1)} %collective-permute-done.1.fl, ...), custom_call_target="tpu_custom_call" | custom-call | flops 8000000000 | bytes 20000000 | tf_op jit(solution)/shard_map/main_part/pallas_call | solution.py:690
  29.2 0.0 collective-permute-done.5.fl
  29.2 0.0 collective-permute-done.6.fr
  29.2 2.2 %z_apply.1 = f32[32,64,512]{2,1,0:T(8,128)} custom-call(f32[4,32,64,128]{3,2,1,0:T(8,128)S(1)} %get-tuple-element.35.in_ref, f32[32,64,512]{2,1,0:T(8,128)} %get-tuple-element.36.base_hbm, f32[256,512]{1,0:T(8,128)S(1)} %get-tuple-element.37.w_ref, f32[80,512]{1,0:T(8,128)S(1)} %collective-permute-done.5.fl, ...), custom_call_target="tpu_custom_call", output_to_operand_aliasing={{}: (1, {})} | custom-call | tf_op jit(solution)/shard_map/z_apply/pallas_call | solution.py:822
  (18 shorter events, 0.0 us)
Async XLA Ops:
  0.0 8.8 %copy-start.13 = (bf16[3,8,384]{2,1,0:T(8,128)(2,1)S(1)}, bf16[3,8,384]{2,1,0:T(8,128)(2,1)}, u32[]{:S(2)}) copy-start(bf16[3,8,384]{2,1,0:T(8,128)(2,1)} %constant.56.clone.c_ref) | copy-start | bytes 55300
  0.0 8.8 %copy-start.9 = (bf16[2,112,240]{2,1,0:T(8,128)(2,1)S(1)}, bf16[2,112,240]{2,1,0:T(8,128)(2,1)}, u32[]{:S(2)}) copy-start(bf16[2,112,240]{2,1,0:T(8,128)(2,1)} %constant.55.clone.t_ref) | copy-start | bytes 322564
  3.5 5.3 %collective-permute-start = (f32[384,512]{1,0:T(8,128)S(1)}, f32[384,512]{1,0:T(8,128)S(1)}, u32[]{:S(2)}, u32[]{:S(2)}) collective-permute-start(f32[384,512]{1,0:T(8,128)S(1)} %get-tuple-element.25), channel_id=1, source_target_pairs={{0,16},{16,0},{1,17},{17,1},{2,18},{18,2},{3,19},{19,3},{4,20},{20... | collective-permute-start | bytes 2359304 | tf_op jit(solution)/shard_map/ppermute | solution.py:203
  4.0 18.2 %collective-permute-start.3 = (f32[128,512]{1,0:T(8,128)S(1)}, f32[128,512]{1,0:T(8,128)S(1)}, u32[]{:S(2)}, u32[]{:S(2)}) collective-permute-start(f32[128,512]{1,0:T(8,128)S(1)} %get-tuple-element.33), channel_id=1, source_target_pairs={{0,1},{1,2},{2,3},{3,0},{4,5},{5,6},{6,7},{7,4},{8,9},{9,10},{10,1... | collective-permute-start | bytes 786440 | tf_op jit(solution)/shard_map/ppermute | solution.py:853
  6.7 15.6 %collective-permute-start.4 = (f32[128,512]{1,0:T(8,128)S(1)}, f32[128,512]{1,0:T(8,128)S(1)}, u32[]{:S(2)}, u32[]{:S(2)}) collective-permute-start(f32[128,512]{1,0:T(8,128)S(1)} %get-tuple-element.34), channel_id=1, source_target_pairs={{1,0},{2,1},{3,2},{0,3},{5,4},{6,5},{7,6},{4,7},{9,8},{10,9},{11,1... | collective-permute-start | bytes 786440 | tf_op jit(solution)/shard_map/ppermute | solution.py:853
  8.8 8.7 %copy-start = (bf16[2,768,256]{2,1,0:T(8,128)(2,1)S(1)}, bf16[2,768,256]{2,1,0:T(8,128)(2,1)}, u32[]{:S(2)}) copy-start(bf16[2,768,256]{2,1,0:T(8,128)(2,1)} %constant.48.clone.o1.own1) | copy-start | bytes 2359300
  8.8 8.6 %copy-start.1 = (bf16[1536,256]{1,0:T(8,128)(2,1)S(1)}, bf16[1536,256]{1,0:T(8,128)(2,1)}, u32[]{:S(2)}) copy-start(bf16[1536,256]{1,0:T(8,128)(2,1)} %constant.57.clone.m2) | copy-start | bytes 2359300
  8.8 8.6 %copy-start.3 = (bf16[2,384,256]{2,1,0:T(8,128)(2,1)S(1)}, bf16[2,384,256]{2,1,0:T(8,128)(2,1)}, u32[]{:S(2)}) copy-start(bf16[2,384,256]{2,1,0:T(8,128)(2,1)} %constant.49.clone.e1.edge1) | copy-start | bytes 1179652
  8.8 8.6 %copy-start.4 = (bf16[1536,128]{1,0:T(8,128)(2,1)S(1)}, bf16[1536,128]{1,0:T(8,128)(2,1)}, u32[]{:S(2)}) copy-start(bf16[1536,128]{1,0:T(8,128)(2,1)} %constant.58.clone.m3) | copy-start | bytes 1179652
  8.9 8.6 %copy-start.6 = (bf16[384,256]{1,0:T(8,128)(2,1)S(1)}, bf16[384,256]{1,0:T(8,128)(2,1)}, u32[]{:S(2)}) copy-start(bf16[384,256]{1,0:T(8,128)(2,1)} %constant.59.clone.h2) | copy-start | bytes 589828
  8.9 8.6 %copy-start.8 = (f32[224,128]{1,0:T(8,128)S(1)}, f32[224,128]{1,0:T(8,128)}, u32[]{:S(2)}) copy-start(f32[224,128]{1,0:T(8,128)} %constant.63.clone.k3) | copy-start | bytes 344068
  8.9 8.6 %copy-start.10 = (bf16[384,128]{1,0:T(8,128)(2,1)S(1)}, bf16[384,128]{1,0:T(8,128)(2,1)}, u32[]{:S(2)}) copy-start(bf16[384,128]{1,0:T(8,128)(2,1)} %constant.60.clone.h3) | copy-start | bytes 294916
  8.9 8.6 %copy-start.12 = (f32[96,128]{1,0:T(8,128)S(1)}, f32[96,128]{1,0:T(8,128)}, u32[]{:S(2)}) copy-start(f32[96,128]{1,0:T(8,128)} %constant.62.clone.k2) | copy-start | bytes 147460
  8.9 8.6 %copy-start.14 = (f32[32,128]{1,0:T(8,128)S(1)}, f32[32,128]{1,0:T(8,128)}, u32[]{:S(2)}) copy-start(f32[32,128]{1,0:T(8,128)} %constant.61.clone.k1) | copy-start | bytes 49156
  11.6 10.7 %copy-start.15 = (bf16[2,768,256]{2,1,0:T(8,128)(2,1)S(1)}, bf16[2,768,256]{2,1,0:T(8,128)(2,1)}, u32[]{:S(2)}) copy-start(bf16[2,768,256]{2,1,0:T(8,128)(2,1)} %constant.52.clone.o3) | copy-start | bytes 2359300
  11.6 10.7 %copy-start.16 = (bf16[2,768,256]{2,1,0:T(8,128)(2,1)S(1)}, bf16[2,768,256]{2,1,0:T(8,128)(2,1)}, u32[]{:S(2)}) copy-start(bf16[2,768,256]{2,1,0:T(8,128)(2,1)} %constant.50.clone.o2) | copy-start | bytes 2359300
  11.6 10.7 %copy-start.17 = (bf16[2,384,256]{2,1,0:T(8,128)(2,1)S(1)}, bf16[2,384,256]{2,1,0:T(8,128)(2,1)}, u32[]{:S(2)}) copy-start(bf16[2,384,256]{2,1,0:T(8,128)(2,1)} %constant.53.clone.e3) | copy-start | bytes 1179652
  11.6 10.7 %copy-start.18 = (bf16[2,384,256]{2,1,0:T(8,128)(2,1)S(1)}, bf16[2,384,256]{2,1,0:T(8,128)(2,1)}, u32[]{:S(2)}) copy-start(bf16[2,384,256]{2,1,0:T(8,128)(2,1)} %constant.51.clone.e2) | copy-start | bytes 1179652
  11.6 10.7 %copy-start.19 = (f32[256,128]{1,0:T(8,128)S(1)}, f32[256,128]{1,0:T(8,128)}, u32[]{:S(2)}) copy-start(f32[256,128]{1,0:T(8,128)} %constant.67.clone.k3) | copy-start | bytes 393220
  11.6 10.7 %copy-start.20 = (f32[256,128]{1,0:T(8,128)S(1)}, f32[256,128]{1,0:T(8,128)}, u32[]{:S(2)}) copy-start(f32[256,128]{1,0:T(8,128)} %constant.66.clone.k2) | copy-start | bytes 393220
  11.6 10.7 %copy-start.21 = (bf16[64,192]{1,0:T(8,128)(2,1)S(1)}, bf16[64,192]{1,0:T(8,128)(2,1)}, u32[]{:S(2)}) copy-start(bf16[64,192]{1,0:T(8,128)(2,1)} %constant.64.clone.xt) | copy-start | bytes 73732
  11.6 10.7 %copy-start.22 = (f32[8,128]{1,0:T(8,128)S(1)}, f32[8,128]{1,0:T(8,128)}, u32[]{:S(2)}) copy-start(f32[8,128]{1,0:T(8,128)} %constant.65.clone.k1) | copy-start | bytes 12292
  11.7 5.3 %collective-permute-start.1 = (f32[24,512]{1,0:T(8,128)S(1)}, f32[24,512]{1,0:T(8,128)S(1)}, u32[]{:S(2)}, u32[]{:S(2)}) collective-permute-start(f32[24,512]{1,0:T(8,128)S(1)} %get-tuple-element.31), channel_id=1, source_target_pairs={{0,4},{4,8},{8,12},{12,0},{1,5},{5,9},{9,13},{13,1},{2,6},{6,10},{... | collective-permute-start | bytes 147464 | tf_op jit(solution)/shard_map/ppermute | solution.py:853
  13.3 4.1 %collective-permute-start.2 = (f32[24,512]{1,0:T(8,128)S(1)}, f32[24,512]{1,0:T(8,128)S(1)}, u32[]{:S(2)}, u32[]{:S(2)}) collective-permute-start(f32[24,512]{1,0:T(8,128)S(1)} %get-tuple-element.32), channel_id=1, source_target_pairs={{4,0},{8,4},{12,8},{0,12},{5,1},{9,5},{13,9},{1,13},{6,2},{10,6},{... | collective-permute-start | bytes 147464 | tf_op jit(solution)/shard_map/ppermute | solution.py:853
  18.4 10.8 %collective-permute-start.5 = (f32[80,512]{1,0:T(8,128)S(1)}, f32[80,512]{1,0:T(8,128)S(1)}, u32[]{:S(2)}, u32[]{:S(2)}) collective-permute-start(f32[80,512]{1,0:T(8,128)S(1)} %get-tuple-element.41), channel_id=1, source_target_pairs={{0,1},{1,2},{2,3},{3,0},{4,5},{5,6},{6,7},{7,4},{8,9},{9,10},{10,1... | collective-permute-start | bytes 491528 | tf_op jit(solution)/shard_map/ppermute | solution.py:853
  18.6 10.6 %collective-permute-start.6 = (f32[80,512]{1,0:T(8,128)S(1)}, f32[80,512]{1,0:T(8,128)S(1)}, u32[]{:S(2)}, u32[]{:S(2)}) collective-permute-start(f32[80,512]{1,0:T(8,128)S(1)} %get-tuple-element.42), channel_id=1, source_target_pairs={{1,0},{2,1},{3,2},{0,3},{5,4},{6,5},{7,6},{4,7},{9,8},{10,9},{11,1... | collective-permute-start | bytes 491528 | tf_op jit(solution)/shard_map/ppermute | solution.py:853
  22.3 6.9 %copy-start.2 = (bf16[512,512]{1,0:T(8,128)(2,1)S(1)}, bf16[512,512]{1,0:T(8,128)(2,1)}, u32[]{:S(2)}) copy-start(bf16[512,512]{1,0:T(8,128)(2,1)} %constant.68.clone.t2) | copy-start | bytes 1572868
  22.3 6.9 %copy-start.5 = (bf16[256,512]{1,0:T(8,128)(2,1)S(1)}, bf16[256,512]{1,0:T(8,128)(2,1)}, u32[]{:S(2)}) copy-start(bf16[256,512]{1,0:T(8,128)(2,1)} %constant.69.clone.t3) | copy-start | bytes 786436
  22.4 6.9 %copy-start.7 = (bf16[128,512]{1,0:T(8,128)(2,1)S(1)}, bf16[128,512]{1,0:T(8,128)(2,1)}, u32[]{:S(2)}) copy-start(bf16[128,512]{1,0:T(8,128)(2,1)} %constant.71.clone.yf) | copy-start | bytes 393220
  22.4 6.8 %copy-start.11 = (bf16[256,48]{1,0:T(8,128)(2,1)S(1)}, bf16[256,48]{1,0:T(8,128)(2,1)}, u32[]{:S(2)}) copy-start(bf16[256,48]{1,0:T(8,128)(2,1)} %constant.70.clone.xf) | copy-start | bytes 73732
where the time goes:
time: 31.6 us; the launch traced here: 31.5 us
  Pallas kernels  18.4 us (58%)
  starting transfers between devices  12.1 us (38%)
  waiting for transfers between devices  0.46 us (1%)
  between operations  0.36 us (1%)
    ppermute x3, starting transfers between devices, swap(): lax.ppermute(to_left, axis, left)  7.09 us
    pallas_call x1, Pallas kernels, main_part(): pl.pallas_call(kernel, in_specs=[VM] * 17, out_specs=[VM, VM, HB], out_sh...  6.77 us
    ppermute x3, starting transfers between devices, swap(): lax.ppermute(to_right, axis, right)  4.5 us
    pallas_call x1, Pallas kernels, x_send(): pl.pallas_call(kernel, in_specs=[HB, HB], out_specs=[VM] * 4, out_shape=[...  3.51 us
    pallas_call x1, Pallas kernels, x_apply(): pl.pallas_call(kernel, grid=(steps,), in_specs=[VM] * 4, out_specs=[VM] *...  2.64 us
    pallas_call x1, Pallas kernels, z_first(): pl.pallas_call(kernel, in_specs=[VM] * 3, out_specs=[VM] * 5, out_shape=[...  2.35 us
    pallas_call x1, Pallas kernels, z_apply(): pl.pallas_call(kernel, in_specs=[VM, HB] + [VM] * 7, out_specs=HB, out_sh...  2.24 us
    pallas_call x1, Pallas kernels, y_messages(): pl.pallas_call(kernel, in_specs=[VM] * 14, out_specs=[VM] * 2, out_shape=...  0.86 us
  transfers between devices with their start and end apart: 7, of which 1 were waited for; matrix products, arithmetic and copies ran while one was open for 0% of the time, Pallas kernels for 40%

commit v1 on v0

--- a/solution.py
+++ b/solution.py
@@ -144,10 +144,10 @@
     hi_rows, lo_rows = hi_lo(wide)
     pair = np.concatenate([hi_rows, lo_rows])
     height = 12 * group
-    step = 8
+    step = 4
     steps = nz // step
     order = [0, steps - 1] + list(range(1, steps - 1))
-    flight = 2
+    flight = 4
     _, low, _, high, _ = sides(nz)[0]
     assert np.abs(low[:, :-step]).max() == 0 and np.abs(high[:, step:]).max() == 0
 
@@ -459,8 +459,10 @@
     return jnp.where(lanes < 32, rows[:, 256:384], before)
 
 
-def late_rows(counts, ny):
-    return [3 * counts[1] * (ny // 2) // ny, 4 * counts[2] * (ny // 4) // ny, 8, 8]
+def late_rows(side, counts, ny):
+    ranks = LEFT_RANKS if side == 0 else RIGHT_RANKS
+    parts = [ranks[1] * counts[1] * ny // 256, ranks[2] * counts[2] * ny // 512, ny // 16, 8]
+    return [0] + [int(n) for n in np.cumsum(parts)]
 
 
 def y_messages(combined, from_left, from_right, nz, band_one):
@@ -485,8 +487,7 @@
                         for base in (LEFT_AT, RIGHT_AT):
                             coef[c, zz, base + row + lane] = table[c, chunk * per + zz]
         coefs.append(coef.reshape(nums[level] * per, 128))
-    heights = late_rows(counts, ny)
-    height = sum(heights)
+    places = [late_rows(side, counts, ny) for side in (0, 1)]
 
     def kernel(c2, c3, cf, fl, fr, own1, edge1, m2, m3, h2, h3, k1, k2, k3, up_ref, down_ref):
         halo = turned(fl, fr)
@@ -513,39 +514,35 @@
         ones = reduced(k1, counts[0], 4)
         rows8 = lax.broadcasted_iota(jnp.int32, (8, 128), 0)
         for side, ref in enumerate((up_ref, down_ref)):
-            at = 0
+            at = places[side]
             for level in (1, 2):
-                n, width = counts[level], ny >> level
+                n, lane_groups = counts[level], (ny >> level) // 128
                 ranks = LEFT_RANKS if side == 0 else RIGHT_RANKS
                 first = 0 if side == 0 else LEFT_RANKS[level] * n
-                total = ranks[level] * n
-                tall = heights[level - 1]
-                for part in range(1 << level):
-                    use = max(min(tall, total - part * tall), 0)
-                    lanes = slice(part * width, (part + 1) * width)
-                    if use > 0:
-                        ref[at : at + use, lanes] = got[level - 1][
-                            first + part * tall : first + part * tall + use
+                row = at[level - 1]
+                for c in range(ranks[level]):
+                    for p in range(lane_groups):
+                        ref[row : row + n, :] = got[level - 1][
+                            first + c * n : first + c * n + n, 128 * p : 128 * p + 128
                         ]
-                    if use < tall:
-                        ref[at + use : at + tall, lanes] = jnp.zeros((tall - use, width), F32)
-                at += tall
-            ref[at : at + 8, :] = frame[8 * side : 8 * side + 8]
-            at += 8
+                        row += n
+            for p in range(ny // 128):
+                ref[at[2] + 8 * p : at[2] + 8 * p + 8, :] = frame[
+                    8 * side : 8 * side + 8, 128 * p : 128 * p + 128
+                ]
             turn = jnp.concatenate(ones[2 * side : 2 * side + 2], axis=0).T
             both = []
             for start in (LEFT_AT, RIGHT_AT):
                 v = turn[start : start + 8]
                 v = v + pltpu.roll(v, 4, 0)
                 both.append(v + pltpu.roll(v, 2, 0))
-            ref[at:, :128] = jnp.where(rows8 < 2, both[0], both[1])
-            ref[at:, 128:] = jnp.zeros((8, ny - 128), F32)
+            ref[at[3] : at[4], :] = jnp.where(rows8 < 2, both[0], both[1])
 
     return pl.pallas_call(
         kernel,
         in_specs=[VM] * 14,
         out_specs=[VM] * 2,
-        out_shape=[vmem((height, ny))] * 2,
+        out_shape=[vmem((at[-1], 128)) for at in places],
         compiler_params=params(24),
         name="y_messages",
     )(
@@ -719,7 +716,7 @@
         width = ny >> level
         hi = spread_columns(np.eye(width), 1 << level, ny).astype(ml_dtypes.bfloat16)
         tables.append(np.concatenate([hi, hi]))
-    heights = late_rows(counts, ny)
+    places = [late_rows(side, counts, ny) for side in (0, 1)]
     _, _, x_maps = joint_sides(nx)
     frame = np.zeros((4 * nx, 16))
     for c in range(4):
@@ -734,13 +731,15 @@
     def kernel(in_ref, base_hbm, w_ref, fl, fr, t2, t3, xf, yf, out_hbm, s1, s2, s3, buf, sem):
         del base_hbm
         s3[...] = jnp.zeros(s3.shape, F32)
-        at = heights[0] + heights[1]
-        hi, lo = split(jnp.concatenate([fl[at : at + 8, :], fr[at : at + 8, :]], axis=0))
-        at += 8
+        halos = [
+            jnp.concatenate([ref[at[2] + 8 * p : at[2] + 8 * p + 8, :] for p in range(groups)], axis=1)
+            for ref, at in zip((fl, fr), places)
+        ]
+        hi, lo = split(jnp.concatenate(halos, axis=0))
         none = jnp.zeros((104, 128), F32)
         turn = []
-        for ref in (fl, fr):
-            values = ref[at : at + 8, :128]
+        for ref, at in zip((fl, fr), places):
+            values = ref[at[3] : at[4], :]
             high = values.astype(BF).astype(F32)
             turn.append(jnp.concatenate([high, values - high, high, none], axis=0).T.astype(BF))
         left_hand = jnp.concatenate([jnp.concatenate(turn, axis=0), xf[...]], axis=1)
@@ -748,30 +747,29 @@
         for c in range(4):
             for q in range(groups):
                 s1[c, q] = first[c * nx : c * nx + nx, 128 * q : 128 * q + 128]
-        at = 0
         for level, table, to in ((1, t2, s2), (2, t3, s3)):
-            width, tall, n = ny >> level, heights[level - 1], counts[level]
-            flat = jnp.concatenate(
-                [
-                    ref[at : at + tall, p * width : p * width + width]
-                    for ref in (fl, fr)
-                    for p in range(1 << level)
-                ],
-                axis=0,
-            )
+            n, lane_groups = counts[level], (ny >> level) // 128
+            pieces = []
+            for side, ref in enumerate((fl, fr)):
+                row = places[side][level - 1]
+                for c in range((LEFT_RANKS, RIGHT_RANKS)[side][level]):
+                    pieces.append(
+                        jnp.concatenate(
+                            [ref[row + p * n : row + p * n + n, :] for p in range(lane_groups)], axis=1
+                        )
+                    )
+                    row += lane_groups * n
+            flat = jnp.concatenate(pieces, axis=0)
             hi, lo = split(flat)
             got = dot(jnp.concatenate([hi, lo], axis=1), table[...])
             for c in range(LEFT_RANKS[level] + RIGHT_RANKS[level]):
                 start = c * n
-                if c >= LEFT_RANKS[level]:
-                    start += (tall << level) - LEFT_RANKS[level] * n
                 for q in range(groups):
                     piece = got[start : start + n, 128 * q : 128 * q + 128]
                     if level == 1:
                         to[c, q] = piece
                     else:
                         to[c, q, pl.ds(0, n, stride=2), :] = piece
-            at += tall
 
         lanes = lax.broadcasted_iota(jnp.int32, (8, 128), 1)
         even_lane = lanes % 2 == 0

time: 31.6 us -> 30.7 us (0.972)
  starting transfers between devices: 12.1 us -> 10.5 us
  waiting for transfers between devices: 0.46 us -> 1.01 us
    ppermute x3, starting transfers between devices: 7.09 us -> 5.62 us  [swap(): lax.ppermute(to_left, axis, left)]
    ppermute x3, waiting for transfers between devices: 0.45 us -> 1 us  [swap(): lax.ppermute(to_left, axis, left)]
  transfers between devices with their start and end apart: 7 -> 7, of which waited for: 1 -> 2; matrix products, arithmetic and copies ran while one was open for 0% -> 0% of each run, Pallas kernels for 40% -> 41%
where the time goes in v1:
time: 30.7 us; the launch traced here: 30.6 us
  Pallas kernels  18.6 us (61%)
  starting transfers between devices  10.5 us (34%)
  waiting for transfers between devices  1.01 us (3%)
  between operations  0.34 us (1%)
    pallas_call x1, Pallas kernels, main_part(): pl.pallas_call(kernel, in_specs=[VM] * 17, out_specs=[VM, VM, HB], out_sh...  6.76 us
    ppermute x3, starting transfers between devices, swap(): lax.ppermute(to_left, axis, left)  5.62 us
    ppermute x3, starting transfers between devices, swap(): lax.ppermute(to_right, axis, right)  4.32 us
    pallas_call x1, Pallas kernels, x_send(): pl.pallas_call(kernel, in_specs=[HB, HB], out_specs=[VM] * 4, out_shape=[...  3.73 us
    pallas_call x1, Pallas kernels, x_apply(): pl.pallas_call(kernel, grid=(steps,), in_specs=[VM] * 4, out_specs=[VM] *...  2.64 us
    pallas_call x1, Pallas kernels, z_first(): pl.pallas_call(kernel, in_specs=[VM] * 3, out_specs=[VM] * 5, out_shape=[...  2.35 us
    pallas_call x1, Pallas kernels, z_apply(): pl.pallas_call(kernel, in_specs=[VM, HB] + [VM] * 7, out_specs=HB, out_sh...  2.25 us
    ppermute x3, waiting for transfers between devices, swap(): lax.ppermute(to_left, axis, left)  1 us
  transfers between devices with their start and end apart: 7, of which 2 were waited for; matrix products, arithmetic and copies ran while one was open for 0% of the time, Pallas kernels for 41%

profile of v1, /device:TPU:0, one launch (start us, length us, event | category | flops | bytes accessed | tf_op | source)
XLA Modules:
  0.0 30.6 jit_solution(7476952390903120149)
XLA Ops:
  0.0 3.7 %x_send.1 = (f32[32,64,512]{2,1,0:T(8,128)S(1)}, f32[384,512]{1,0:T(8,128)S(1)}, f32[128,512]{1,0:T(8,128)S(1)}, f32[128,512]{1,0:T(8,128)S(1)}) custom-call(f32[32,64,512]{2,1,0:T(8,128)} %u_hbm.1, bf16[96,256]{1,0:T(8,128)(2,1)} %constant.54.clone.c_hbm), custom_call_target="tpu_custom_call" | custom-call | tf_op jit(solution)/shard_map/x_send/pallas_call | solution.py:184
  3.7 0.5 %collective-permute-start = (f32[384,512]{1,0:T(8,128)S(1)}, f32[384,512]{1,0:T(8,128)S(1)}, u32[]{:S(2)}, u32[]{:S(2)}) collective-permute-start(f32[384,512]{1,0:T(8,128)S(1)} %get-tuple-element.25), channel_id=1, source_target_pairs={{0,16},{16,0},{1,17},{17,1},{2,18},{18,2},{3,19},{19,3},{4,20},{20... | collective-permute-start | bytes 2359304 | tf_op jit(solution)/shard_map/ppermute | solution.py:203
  4.3 2.6 %collective-permute-start.3 = (f32[128,512]{1,0:T(8,128)S(1)}, f32[128,512]{1,0:T(8,128)S(1)}, u32[]{:S(2)}, u32[]{:S(2)}) collective-permute-start(f32[128,512]{1,0:T(8,128)S(1)} %get-tuple-element.33), channel_id=1, source_target_pairs={{0,1},{1,2},{2,3},{3,0},{4,5},{5,6},{6,7},{7,4},{8,9},{9,10},{10,1... | collective-permute-start | bytes 786440 | tf_op jit(solution)/shard_map/ppermute | solution.py:851
  6.9 2.1 %collective-permute-start.4 = (f32[128,512]{1,0:T(8,128)S(1)}, f32[128,512]{1,0:T(8,128)S(1)}, u32[]{:S(2)}, u32[]{:S(2)}) collective-permute-start(f32[128,512]{1,0:T(8,128)S(1)} %get-tuple-element.34), channel_id=1, source_target_pairs={{1,0},{2,1},{3,2},{0,3},{5,4},{6,5},{7,6},{4,7},{9,8},{10,9},{11,1... | collective-permute-start | bytes 786440 | tf_op jit(solution)/shard_map/ppermute | solution.py:851
  9.0 0.0 collective-permute-done.r_ref
  9.0 0.0 copy-done.13
  9.0 0.0 copy-done.9
  9.0 0.0 copy-start
  9.0 0.0 copy-start.1
  9.0 0.0 copy-start.3
  9.1 0.0 copy-start.4
  9.1 0.0 copy-start.6
  9.1 0.0 copy-start.8
  9.1 0.0 copy-start.10
  9.1 0.0 copy-start.12
  9.1 0.0 copy-start.14
  9.1 2.6 %x_apply.1 = (f32[32,64,512]{2,1,0:T(8,128)S(1)}, f32[32,32,512]{2,1,0:T(8,128)S(1)}, f32[32,16,512]{2,1,0:T(8,128)S(1)}, f32[24,512]{1,0:T(8,128)S(1)}, f32[24,512]{1,0:T(8,128)S(1)}) custom-call(f32[32,64,512]{2,1,0:T(8,128)S(1)} %get-tuple-element.24.u_ref, f32[384,512]{1,0:T(8,128)S(1)} %collective-permute-done.r_ref, ...), custom_call_target="tpu_custom_call" | custom-call | tf_op jit(solution)/shard_map/x_apply/pallas_call | solution.py:273
  11.8 0.0 copy-start.16
  11.8 0.0 copy-start.17
  11.8 0.0 copy-start.18
  11.8 0.0 copy-start.19
  11.8 0.0 copy-start.20
  11.9 0.0 copy-start.21
  11.9 0.0 copy-start.22
  11.9 1.7 %collective-permute-start.1 = (f32[24,512]{1,0:T(8,128)S(1)}, f32[24,512]{1,0:T(8,128)S(1)}, u32[]{:S(2)}, u32[]{:S(2)}) collective-permute-start(f32[24,512]{1,0:T(8,128)S(1)} %get-tuple-element.31), channel_id=1, source_target_pairs={{0,4},{4,8},{8,12},{12,0},{1,5},{5,9},{9,13},{13,1},{2,6},{6,10},{... | collective-permute-start | bytes 147464 | tf_op jit(solution)/shard_map/ppermute | solution.py:851
  13.6 1.3 %collective-permute-start.2 = (f32[24,512]{1,0:T(8,128)S(1)}, f32[24,512]{1,0:T(8,128)S(1)}, u32[]{:S(2)}, u32[]{:S(2)}) collective-permute-start(f32[24,512]{1,0:T(8,128)S(1)} %get-tuple-element.32), channel_id=1, source_target_pairs={{4,0},{8,4},{12,8},{0,12},{5,1},{9,5},{13,9},{1,13},{6,2},{10,6},{... | collective-permute-start | bytes 147464 | tf_op jit(solution)/shard_map/ppermute | solution.py:851
  14.9 2.4 %z_first.1 = (f32[192,512]{1,0:T(8,128)S(1)}, f32[112,512]{1,0:T(8,128)S(1)}, f32[16,512]{1,0:T(8,128)S(1)}, f32[16,32,512]{2,1,0:T(8,128)S(1)}, f32[8,16,512]{2,1,0:T(8,128)S(1)}) custom-call(f32[32,32,512]{2,1,0:T(8,128)S(1)} %get-tuple-element.27.x2, f32[32,16,512]{2,1,0:T(8,128)S(1)} %get-tuple-element.28.x3, f32[384,512]{1,0:T(8,128)S(1)} %collective-permute-done.r_ref), custom_call_target="tpu_custom_call" | custom-call | flops 20000000 | bytes 6000000 | tf_op jit(solution)/shard_map/z_first/pallas_call | solution.py:375
  17.2 0.0 collective-permute-done.1.fl
  17.2 0.4 %collective-permute-done.2.fr = f32[24,512]{1,0:T(8,128)S(1)} collective-permute-done((f32[24,512]{1,0:T(8,128)S(1)}, f32[24,512]{1,0:T(8,128)S(1)}, u32[]{:S(2)}, u32[]{:S(2)}) %collective-permute-start.2) | collective-permute-done | bytes 49184 | tf_op jit(solution)/shard_map/ppermute | solution.py:851
  17.7 0.0 copy-done
  17.7 0.0 copy-done.1
  17.7 0.0 copy-done.3
  17.7 0.0 copy-done.4
  17.7 0.0 copy-done.6
  17.7 0.9 %y_messages.1 = (f32[296,128]{1,0:T(8,128)S(1)}, f32[280,128]{1,0:T(8,128)S(1)}) custom-call(f32[192,512]{1,0:T(8,128)S(1)} %get-tuple-element.38.c2, f32[112,512]{1,0:T(8,128)S(1)} %get-tuple-element.39.c3, f32[16,512]{1,0:T(8,128)S(1)} %get-tuple-element.40.cf, f32[24,512]{1,0:T(8,128)S(1)} %collective-permute-done.1.fl, ...), custom_call_target="tpu_custom_call" | custom-call | tf_op jit(solution)/shard_map/y_messages/pallas_call | solution.py:541
  18.6 2.2 %collective-permute-start.6 = (f32[280,128]{1,0:T(8,128)S(1)}, f32[280,128]{1,0:T(8,128)S(1)}, u32[]{:S(2)}, u32[]{:S(2)}) collective-permute-start(f32[280,128]{1,0:T(8,128)S(1)} %get-tuple-element.42), channel_id=1, source_target_pairs={{1,0},{2,1},{3,2},{0,3},{5,4},{6,5},{7,6},{4,7},{9,8},{10,9},{11,1... | collective-permute-start | bytes 430088 | tf_op jit(solution)/shard_map/ppermute | solution.py:851
  20.8 0.0 collective-permute-start.5
  20.8 0.0 collective-permute-done.3.b1
  20.8 0.6 %collective-permute-done.4.a1 = f32[128,512]{1,0:T(8,128)S(1)} collective-permute-done((f32[128,512]{1,0:T(8,128)S(1)}, f32[128,512]{1,0:T(8,128)S(1)}, u32[]{:S(2)}, u32[]{:S(2)}) %collective-permute-start.4) | collective-permute-done | bytes 262176 | tf_op jit(solution)/shard_map/ppermute | solution.py:851
  21.4 0.0 copy-done.16
  21.4 0.0 copy-start.2
  21.4 0.0 copy-start.5
  21.5 0.0 copy-start.7
  21.5 0.0 copy-start.11
  21.5 6.8 %main_part.1 = (f32[4,32,64,128]{3,2,1,0:T(8,128)S(1)}, f32[256,512]{1,0:T(8,128)S(1)}, f32[32,64,512]{2,1,0:T(8,128)}) custom-call(f32[32,64,512]{2,1,0:T(8,128)S(1)} %get-tuple-element.26.x1, f32[16,32,512]{2,1,0:T(8,128)S(1)} %get-tuple-element.29.x2, f32[8,16,512]{2,1,0:T(8,128)S(1)} %get-tuple-element.30.x3, f32[24,512]{1,0:T(8,128)S(1)} %collective-permute-done.1.fl, ...), custom_call_target="tpu_custom_call" | custom-call | flops 8000000000 | bytes 20000000 | tf_op jit(solution)/shard_map/main_part/pallas_call | solution.py:687
  28.2 0.0 collective-permute-done.6.fr
  28.3 0.0 collective-permute-done.5.fl
  28.3 2.2 %z_apply.1 = f32[32,64,512]{2,1,0:T(8,128)} custom-call(f32[4,32,64,128]{3,2,1,0:T(8,128)S(1)} %get-tuple-element.35.in_ref, f32[32,64,512]{2,1,0:T(8,128)} %get-tuple-element.36.base_hbm, f32[256,512]{1,0:T(8,128)S(1)} %get-tuple-element.37.w_ref, f32[296,128]{1,0:T(8,128)S(1)} %collective-permute-done.5.fl, ...), custom_call_target="tpu_custom_call", output_to_operand_aliasing={{}: (1, {})} | custom-call | tf_op jit(solution)/shard_map/z_apply/pallas_call | solution.py:820
  (18 shorter events, 0.0 us)
Async XLA Ops:
  0.0 9.0 %copy-start.13 = (bf16[3,8,384]{2,1,0:T(8,128)(2,1)S(1)}, bf16[3,8,384]{2,1,0:T(8,128)(2,1)}, u32[]{:S(2)}) copy-start(bf16[3,8,384]{2,1,0:T(8,128)(2,1)} %constant.56.clone.c_ref) | copy-start | bytes 55300
  0.0 9.0 %copy-start.9 = (bf16[2,112,240]{2,1,0:T(8,128)(2,1)S(1)}, bf16[2,112,240]{2,1,0:T(8,128)(2,1)}, u32[]{:S(2)}) copy-start(bf16[2,112,240]{2,1,0:T(8,128)(2,1)} %constant.55.clone.t_ref) | copy-start | bytes 322564
  3.7 5.3 %collective-permute-start = (f32[384,512]{1,0:T(8,128)S(1)}, f32[384,512]{1,0:T(8,128)S(1)}, u32[]{:S(2)}, u32[]{:S(2)}) collective-permute-start(f32[384,512]{1,0:T(8,128)S(1)} %get-tuple-element.25), channel_id=1, source_target_pairs={{0,16},{16,0},{1,17},{17,1},{2,18},{18,2},{3,19},{19,3},{4,20},{20... | collective-permute-start | bytes 2359304 | tf_op jit(solution)/shard_map/ppermute | solution.py:203
  4.3 16.6 %collective-permute-start.3 = (f32[128,512]{1,0:T(8,128)S(1)}, f32[128,512]{1,0:T(8,128)S(1)}, u32[]{:S(2)}, u32[]{:S(2)}) collective-permute-start(f32[128,512]{1,0:T(8,128)S(1)} %get-tuple-element.33), channel_id=1, source_target_pairs={{0,1},{1,2},{2,3},{3,0},{4,5},{5,6},{6,7},{7,4},{8,9},{9,10},{10,1... | collective-permute-start | bytes 786440 | tf_op jit(solution)/shard_map/ppermute | solution.py:851
  6.9 14.5 %collective-permute-start.4 = (f32[128,512]{1,0:T(8,128)S(1)}, f32[128,512]{1,0:T(8,128)S(1)}, u32[]{:S(2)}, u32[]{:S(2)}) collective-permute-start(f32[128,512]{1,0:T(8,128)S(1)} %get-tuple-element.34), channel_id=1, source_target_pairs={{1,0},{2,1},{3,2},{0,3},{5,4},{6,5},{7,6},{4,7},{9,8},{10,9},{11,1... | collective-permute-start | bytes 786440 | tf_op jit(solution)/shard_map/ppermute | solution.py:851
  9.0 8.7 %copy-start = (bf16[2,768,256]{2,1,0:T(8,128)(2,1)S(1)}, bf16[2,768,256]{2,1,0:T(8,128)(2,1)}, u32[]{:S(2)}) copy-start(bf16[2,768,256]{2,1,0:T(8,128)(2,1)} %constant.48.clone.o1.own1) | copy-start | bytes 2359300
  9.0 8.6 %copy-start.1 = (bf16[1536,256]{1,0:T(8,128)(2,1)S(1)}, bf16[1536,256]{1,0:T(8,128)(2,1)}, u32[]{:S(2)}) copy-start(bf16[1536,256]{1,0:T(8,128)(2,1)} %constant.57.clone.m2) | copy-start | bytes 2359300
  9.0 8.6 %copy-start.3 = (bf16[2,384,256]{2,1,0:T(8,128)(2,1)S(1)}, bf16[2,384,256]{2,1,0:T(8,128)(2,1)}, u32[]{:S(2)}) copy-start(bf16[2,384,256]{2,1,0:T(8,128)(2,1)} %constant.49.clone.e1.edge1) | copy-start | bytes 1179652
  9.1 8.6 %copy-start.4 = (bf16[1536,128]{1,0:T(8,128)(2,1)S(1)}, bf16[1536,128]{1,0:T(8,128)(2,1)}, u32[]{:S(2)}) copy-start(bf16[1536,128]{1,0:T(8,128)(2,1)} %constant.58.clone.m3) | copy-start | bytes 1179652
  9.1 8.6 %copy-start.6 = (bf16[384,256]{1,0:T(8,128)(2,1)S(1)}, bf16[384,256]{1,0:T(8,128)(2,1)}, u32[]{:S(2)}) copy-start(bf16[384,256]{1,0:T(8,128)(2,1)} %constant.59.clone.h2) | copy-start | bytes 589828
  9.1 8.6 %copy-start.8 = (f32[224,128]{1,0:T(8,128)S(1)}, f32[224,128]{1,0:T(8,128)}, u32[]{:S(2)}) copy-start(f32[224,128]{1,0:T(8,128)} %constant.63.clone.k3) | copy-start | bytes 344068
  9.1 8.6 %copy-start.10 = (bf16[384,128]{1,0:T(8,128)(2,1)S(1)}, bf16[384,128]{1,0:T(8,128)(2,1)}, u32[]{:S(2)}) copy-start(bf16[384,128]{1,0:T(8,128)(2,1)} %constant.60.clone.h3) | copy-start | bytes 294916
  9.1 8.6 %copy-start.12 = (f32[96,128]{1,0:T(8,128)S(1)}, f32[96,128]{1,0:T(8,128)}, u32[]{:S(2)}) copy-start(f32[96,128]{1,0:T(8,128)} %constant.62.clone.k2) | copy-start | bytes 147460
  9.1 8.6 %copy-start.14 = (f32[32,128]{1,0:T(8,128)S(1)}, f32[32,128]{1,0:T(8,128)}, u32[]{:S(2)}) copy-start(f32[32,128]{1,0:T(8,128)} %constant.61.clone.k1) | copy-start | bytes 49156
  11.8 9.6 %copy-start.15 = (bf16[2,768,256]{2,1,0:T(8,128)(2,1)S(1)}, bf16[2,768,256]{2,1,0:T(8,128)(2,1)}, u32[]{:S(2)}) copy-start(bf16[2,768,256]{2,1,0:T(8,128)(2,1)} %constant.52.clone.o3) | copy-start | bytes 2359300
  11.8 9.6 %copy-start.16 = (bf16[2,768,256]{2,1,0:T(8,128)(2,1)S(1)}, bf16[2,768,256]{2,1,0:T(8,128)(2,1)}, u32[]{:S(2)}) copy-start(bf16[2,768,256]{2,1,0:T(8,128)(2,1)} %constant.50.clone.o2) | copy-start | bytes 2359300
  11.8 9.6 %copy-start.17 = (bf16[2,384,256]{2,1,0:T(8,128)(2,1)S(1)}, bf16[2,384,256]{2,1,0:T(8,128)(2,1)}, u32[]{:S(2)}) copy-start(bf16[2,384,256]{2,1,0:T(8,128)(2,1)} %constant.53.clone.e3) | copy-start | bytes 1179652
  11.8 9.6 %copy-start.18 = (bf16[2,384,256]{2,1,0:T(8,128)(2,1)S(1)}, bf16[2,384,256]{2,1,0:T(8,128)(2,1)}, u32[]{:S(2)}) copy-start(bf16[2,384,256]{2,1,0:T(8,128)(2,1)} %constant.51.clone.e2) | copy-start | bytes 1179652
  11.8 9.6 %copy-start.19 = (f32[256,128]{1,0:T(8,128)S(1)}, f32[256,128]{1,0:T(8,128)}, u32[]{:S(2)}) copy-start(f32[256,128]{1,0:T(8,128)} %constant.67.clone.k3) | copy-start | bytes 393220
  11.8 9.6 %copy-start.20 = (f32[256,128]{1,0:T(8,128)S(1)}, f32[256,128]{1,0:T(8,128)}, u32[]{:S(2)}) copy-start(f32[256,128]{1,0:T(8,128)} %constant.66.clone.k2) | copy-start | bytes 393220
  11.9 9.6 %copy-start.21 = (bf16[64,192]{1,0:T(8,128)(2,1)S(1)}, bf16[64,192]{1,0:T(8,128)(2,1)}, u32[]{:S(2)}) copy-start(bf16[64,192]{1,0:T(8,128)(2,1)} %constant.64.clone.xt) | copy-start | bytes 73732
  11.9 9.6 %copy-start.22 = (f32[8,128]{1,0:T(8,128)S(1)}, f32[8,128]{1,0:T(8,128)}, u32[]{:S(2)}) copy-start(f32[8,128]{1,0:T(8,128)} %constant.65.clone.k1) | copy-start | bytes 12292
  11.9 5.3 %collective-permute-start.1 = (f32[24,512]{1,0:T(8,128)S(1)}, f32[24,512]{1,0:T(8,128)S(1)}, u32[]{:S(2)}, u32[]{:S(2)}) collective-permute-start(f32[24,512]{1,0:T(8,128)S(1)} %get-tuple-element.31), channel_id=1, source_target_pairs={{0,4},{4,8},{8,12},{12,0},{1,5},{5,9},{9,13},{13,1},{2,6},{6,10},{... | collective-permute-start | bytes 147464 | tf_op jit(solution)/shard_map/ppermute | solution.py:851
  13.6 4.1 %collective-permute-start.2 = (f32[24,512]{1,0:T(8,128)S(1)}, f32[24,512]{1,0:T(8,128)S(1)}, u32[]{:S(2)}, u32[]{:S(2)}) collective-permute-start(f32[24,512]{1,0:T(8,128)S(1)} %get-tuple-element.32), channel_id=1, source_target_pairs={{4,0},{8,4},{12,8},{0,12},{5,1},{9,5},{13,9},{1,13},{6,2},{10,6},{... | collective-permute-start | bytes 147464 | tf_op jit(solution)/shard_map/ppermute | solution.py:851
  18.6 9.7 %collective-permute-start.6 = (f32[280,128]{1,0:T(8,128)S(1)}, f32[280,128]{1,0:T(8,128)S(1)}, u32[]{:S(2)}, u32[]{:S(2)}) collective-permute-start(f32[280,128]{1,0:T(8,128)S(1)} %get-tuple-element.42), channel_id=1, source_target_pairs={{1,0},{2,1},{3,2},{0,3},{5,4},{6,5},{7,6},{4,7},{9,8},{10,9},{11,1... | collective-permute-start | bytes 430088 | tf_op jit(solution)/shard_map/ppermute | solution.py:851
  20.8 7.5 %collective-permute-start.5 = (f32[296,128]{1,0:T(8,128)S(1)}, f32[296,128]{1,0:T(8,128)S(1)}, u32[]{:S(2)}, u32[]{:S(2)}) collective-permute-start(f32[296,128]{1,0:T(8,128)S(1)} %get-tuple-element.41), channel_id=1, source_target_pairs={{0,1},{1,2},{2,3},{3,0},{4,5},{5,6},{6,7},{7,4},{8,9},{9,10},{10,1... | collective-permute-start | bytes 454664 | tf_op jit(solution)/shard_map/ppermute | solution.py:851
  21.4 6.8 %copy-start.2 = (bf16[512,512]{1,0:T(8,128)(2,1)S(1)}, bf16[512,512]{1,0:T(8,128)(2,1)}, u32[]{:S(2)}) copy-start(bf16[512,512]{1,0:T(8,128)(2,1)} %constant.68.clone.t2) | copy-start | bytes 1572868
  21.4 6.8 %copy-start.5 = (bf16[256,512]{1,0:T(8,128)(2,1)S(1)}, bf16[256,512]{1,0:T(8,128)(2,1)}, u32[]{:S(2)}) copy-start(bf16[256,512]{1,0:T(8,128)(2,1)} %constant.69.clone.t3) | copy-start | bytes 786436
  21.5 6.8 %copy-start.7 = (bf16[128,512]{1,0:T(8,128)(2,1)S(1)}, bf16[128,512]{1,0:T(8,128)(2,1)}, u32[]{:S(2)}) copy-start(bf16[128,512]{1,0:T(8,128)(2,1)} %constant.71.clone.yf) | copy-start | bytes 393220
  21.5 6.8 %copy-start.11 = (bf16[256,48]{1,0:T(8,128)(2,1)S(1)}, bf16[256,48]{1,0:T(8,128)(2,1)}, u32[]{:S(2)}) copy-start(bf16[256,48]{1,0:T(8,128)(2,1)} %constant.70.clone.xf) | copy-start | bytes 73732

commit v2 on v1

--- a/solution.py
+++ b/solution.py
@@ -121,6 +121,7 @@
 
 VM = pl.BlockSpec(memory_space=pltpu.VMEM)
 HB = pl.BlockSpec(memory_space=pltpu.HBM)
+SHORT = pl.CostEstimate(flops=1000, bytes_accessed=1000, transcendentals=0)
 
 
 def in_hbm(array):
@@ -144,10 +145,9 @@
     hi_rows, lo_rows = hi_lo(wide)
     pair = np.concatenate([hi_rows, lo_rows])
     height = 12 * group
-    step = 4
+    step = 8
     steps = nz // step
     order = [0, steps - 1] + list(range(1, steps - 1))
-    flight = 4
     _, low, _, high, _ = sides(nz)[0]
     assert np.abs(low[:, :-step]).max() == 0 and np.abs(high[:, step:]).max() == 0
 
@@ -159,15 +159,13 @@
             )
             for i in range(steps)
         ]
-        for i in order[:flight]:
+        table_copy.start()
+        for i in order:
             copies[i].start()
-        table_copy.start()
         table_copy.wait()
         table = c_ref[...]
-        for turn, i in enumerate(order):
+        for i in order:
             copies[i].wait()
-            if turn + flight < steps:
-                copies[order[turn + flight]].start()
             for g in range(i * step // group, (i + 1) * step // group):
                 hi, lo = split(u_ref[group * g : group * g + group].reshape(group * nx, ny))
                 both = dot(table, hi)
@@ -192,6 +190,7 @@
             pltpu.SemaphoreType.DMA,
         ],
         compiler_params=params(16),
+        cost_estimate=SHORT,
         name="x_send",
     )(in_hbm(field), in_hbm(jnp.asarray(pair)))
 
@@ -278,6 +277,7 @@
         out_shape=[vmem((nz, n, ny)) for n in counts] + [jax.ShapeDtypeStruct((24, 512), F32)] * 2,
         scratch_shapes=[pltpu.VMEM((nz * n, 384), BF) for n in counts],
         compiler_params=params(24),
+        cost_estimate=SHORT,
         name="x_apply",
     )(field, halo, jnp.asarray(tables), jnp.asarray(combos))
 
@@ -379,7 +379,7 @@
         out_shape=[vmem((t.shape[0] * n, ny)) for t, n in zip(tables[1:], counts)]
         + [vmem((16, ny)), vmem((nz // 2, counts[0], ny)), vmem((nz // 4, counts[1], ny))],
         compiler_params=params(16),
-        cost_estimate=pl.CostEstimate(flops=20_000_000, bytes_accessed=6_000_000, transcendentals=0),
+        cost_estimate=SHORT,
         name="z_first",
     )(x2, x3, halo)
 
@@ -544,6 +544,7 @@
         out_specs=[VM] * 2,
         out_shape=[vmem((at[-1], 128)) for at in places],
         compiler_params=params(24),
+        cost_estimate=SHORT,
         name="y_messages",
     )(
         c2,
@@ -564,14 +565,12 @@
     return [z for z in range(nz) if hit(z)]
 
 
-def main_part(xs, from_left, from_right, below, above, bands):
+def main_part(xs, from_left, from_right, bands):
     nz, nx, ny = xs[0].shape
     counts = [nx, nx // 2, nx // 4]
     changed = touched_layers(nz)
     untouched = [z for z in range(nz) if z not in changed]
     groups = ny // 128
-    _, _, maps = joint_sides(nx)
-    x_table = stack_lhs(maps[0][0])
     masks = []
     for level in range(3):
         chunks = nz * counts[level] // 512
@@ -589,7 +588,7 @@
             masks.append(lanes.reshape(-1, 128))
     masks = [np.concatenate([m, np.zeros((-m.shape[0] % 8, 128))]).astype(np.float32) for m in masks]
 
-    def kernel(x1, x2, x3, fl, fr, b1, a1, o1, e1, o2, e2, o3, e3, xt, k1, k2, k3, out_ref, w_ref, hbm, w2, halo_ref, sem):
+    def kernel(x1, x2, x3, fl, fr, o1, e1, o2, e2, o3, e3, k1, k2, k3, out_ref, done_ref, hbm, w2, halo_ref, sem):
         halo_ref[...] = turned(fl, fr)
         lanes = lax.broadcasted_iota(jnp.int32, (8, 128), 1)
         wide = lax.broadcasted_iota(jnp.int32, (32, 128), 1)
@@ -672,25 +671,18 @@
         for copy in more:
             copy.start()
 
-        early = []
-        for ref in (b1, a1):
-            for c in range(2):
-                hi, lo = split(ref[c * nx : c * nx + nx, :])
-                early.append(dot(xt[...], jnp.concatenate([hi, hi, lo], axis=0)))
-        early = jnp.concatenate(early, axis=0)
-        w_ref[...] = banded(early, plain_edge(early), o1, e1)
-
+        done_ref[...] = jnp.zeros((8, 128), F32)
         for copy in copies + more:
             copy.wait()
 
     flat = [t for band in bands for t in band]
     return pl.pallas_call(
         kernel,
-        in_specs=[VM] * 17,
+        in_specs=[VM] * 14,
         out_specs=[VM, VM, HB],
         out_shape=[
             vmem((groups, nz, nx, 128)),
-            vmem((4 * nx, ny)),
+            vmem((8, 128)),
             pltpu.HBM((nz, nx, ny), F32),
         ],
         scratch_shapes=[
@@ -699,11 +691,34 @@
             pltpu.SemaphoreType.DMA((nz,)),
         ],
         compiler_params=params(32),
-        cost_estimate=pl.CostEstimate(
-            flops=8_000_000_000, bytes_accessed=20_000_000, transcendentals=0
-        ),
+        cost_estimate=SHORT,
         name="main_part",
-    )(*xs, from_left, from_right, below, above, *flat, jnp.asarray(x_table), *[jnp.asarray(m) for m in masks])
+    )(*xs, from_left, from_right, *flat, *[jnp.asarray(m) for m in masks])
+
+
+def early_part(below, above, band, after):
+    nx, ny = below.shape[0] // 2, below.shape[1]
+    _, _, maps = joint_sides(nx)
+
+    def kernel(b1, a1, o1, e1, xt, after_ref, w_ref):
+        del after_ref
+        early = []
+        for ref in (b1, a1):
+            for c in range(2):
+                hi, lo = split(ref[c * nx : c * nx + nx, :])
+                early.append(dot(xt[...], jnp.concatenate([hi, hi, lo], axis=0)))
+        early = jnp.concatenate(early, axis=0)
+        w_ref[...] = banded(early, plain_edge(early), o1, e1)
+
+    return pl.pallas_call(
+        kernel,
+        in_specs=[VM] * 6,
+        out_specs=VM,
+        out_shape=vmem((4 * nx, ny)),
+        compiler_params=params(16),
+        cost_estimate=SHORT,
+        name="early_part",
+    )(below, above, *band, jnp.asarray(stack_lhs(maps[0][0])), after)
 
 
 def z_apply(inner, partial, early, from_left, from_right):
@@ -726,7 +741,7 @@
     _, left, right = y_tables(ny, True)[0]
     side_hi, side_lo = hi_lo(np.concatenate([left, right, np.zeros((4, ny))]))
     side_rows = np.concatenate([side_hi, side_hi, side_lo, np.zeros((104, ny), side_hi.dtype)])
-    touched = touched_layers(nz)
+    touched = sorted(touched_layers(nz), key=lambda z: np.abs(maps[0][z]).max() > 1e-12)
 
     def kernel(in_ref, base_hbm, w_ref, fl, fr, t2, t3, xf, yf, out_hbm, s1, s2, s3, buf, sem):
         del base_hbm
@@ -863,7 +878,8 @@
     *combined, own2, own3 = z_first(x2, x3, halo)
     up, down = y_messages(combined, from_left, from_right, nz, bands[0])
     late_below, late_above = swap(up, down, "gz")
-    inner, early, partial = main_part((x1, own2, own3), from_left, from_right, below, above, bands)
+    inner, done, partial = main_part((x1, own2, own3), from_left, from_right, bands)
+    early = early_part(below, above, bands[0], done)
     return z_apply(inner, partial, early, late_below, late_above)
 
 

time: 30.7 us -> 31.6 us (1.029)
  starting transfers between devices: 10.5 us -> 12.1 us
  waiting for transfers between devices: 1.01 us -> 0.46 us
    ppermute x3, starting transfers between devices: 5.62 us -> 7.09 us  [swap(): lax.ppermute(to_left, axis, left)]
    ppermute x3, waiting for transfers between devices: 1 us -> 0.45 us  [swap(): lax.ppermute(to_left, axis, left)]
    pallas_call x1, Pallas kernels: 3.73 us -> 3.25 us  [x_send(): pl.pallas_call(kernel, in_specs=[HB, HB], out_specs=[VM] * 4, out_shape=[...]
    pallas_call x1 -> x2, Pallas kernels: 6.76 us -> 7 us  [the longest x1 6.31 us: main_part(): pl.pallas_call(kernel, in_specs=[VM] * 14, out_specs=[VM, VM, HB], out_sh...]
  transfers between devices with their start and end apart: 7 -> 7, of which waited for: 2 -> 1; matrix products, arithmetic and copies ran while one was open for 0% -> 0% of each run, Pallas kernels for 41% -> 41%
where the time goes in v2:
time: 31.6 us; the launch traced here: 31.5 us
  Pallas kernels  18.4 us (58%)
  starting transfers between devices  12.1 us (38%)
  waiting for transfers between devices  0.46 us (1%)
  between operations  0.36 us (1%)
    ppermute x3, starting transfers between devices, swap(): lax.ppermute(to_left, axis, left)  7.09 us
    pallas_call x1, Pallas kernels, main_part(): pl.pallas_call(kernel, in_specs=[VM] * 14, out_specs=[VM, VM, HB], out_sh...  6.31 us
    ppermute x3, starting transfers between devices, swap(): lax.ppermute(to_right, axis, right)  4.51 us
    pallas_call x1, Pallas kernels, x_send(): pl.pallas_call(kernel, in_specs=[HB, HB], out_specs=[VM] * 4, out_shape=[...  3.25 us
    pallas_call x1, Pallas kernels, x_apply(): pl.pallas_call(kernel, grid=(steps,), in_specs=[VM] * 4, out_specs=[VM] *...  2.64 us
    pallas_call x1, Pallas kernels, z_first(): pl.pallas_call(kernel, in_specs=[VM] * 3, out_specs=[VM] * 5, out_shape=[...  2.35 us
    pallas_call x1, Pallas kernels, z_apply(): pl.pallas_call(kernel, in_specs=[VM, HB] + [VM] * 7, out_specs=HB, out_sh...  2.31 us
    pallas_call x1, Pallas kernels, y_messages(): pl.pallas_call(kernel, in_specs=[VM] * 14, out_specs=[VM] * 2, out_shape=...  0.85 us
  transfers between devices with their start and end apart: 7, of which 1 were waited for; matrix products, arithmetic and copies ran while one was open for 0% of the time, Pallas kernels for 41%

profile of v2, /device:TPU:0, one launch (start us, length us, event | category | flops | bytes accessed | tf_op | source)
XLA Modules:
  0.0 31.5 jit_solution(14682347677209885116)
XLA Ops:
  0.0 3.2 %x_send.1 = (f32[32,64,512]{2,1,0:T(8,128)S(1)}, f32[384,512]{1,0:T(8,128)S(1)}, f32[128,512]{1,0:T(8,128)S(1)}, f32[128,512]{1,0:T(8,128)S(1)}) custom-call(f32[32,64,512]{2,1,0:T(8,128)} %u_hbm.1, bf16[96,256]{1,0:T(8,128)(2,1)} %constant.54.clone.c_hbm), custom_call_target="tpu_custom_call" | custom-call | flops 1000 | bytes 1000 | tf_op jit(solution)/shard_map/x_send/pallas_call | solution.py:182
  3.3 0.5 %collective-permute-start = (f32[384,512]{1,0:T(8,128)S(1)}, f32[384,512]{1,0:T(8,128)S(1)}, u32[]{:S(2)}, u32[]{:S(2)}) collective-permute-start(f32[384,512]{1,0:T(8,128)S(1)} %get-tuple-element.25), channel_id=1, source_target_pairs={{0,16},{16,0},{1,17},{17,1},{2,18},{18,2},{3,19},{19,3},{4,20},{20... | collective-permute-start | bytes 2359304 | tf_op jit(solution)/shard_map/ppermute | solution.py:202
  3.8 2.6 %collective-permute-start.3 = (f32[128,512]{1,0:T(8,128)S(1)}, f32[128,512]{1,0:T(8,128)S(1)}, u32[]{:S(2)}, u32[]{:S(2)}) collective-permute-start(f32[128,512]{1,0:T(8,128)S(1)} %get-tuple-element.35), channel_id=1, source_target_pairs={{0,1},{1,2},{2,3},{3,0},{4,5},{5,6},{6,7},{7,4},{8,9},{9,10},{10,1... | collective-permute-start | bytes 786440 | tf_op jit(solution)/shard_map/ppermute | solution.py:866
  6.4 2.1 %collective-permute-start.4 = (f32[128,512]{1,0:T(8,128)S(1)}, f32[128,512]{1,0:T(8,128)S(1)}, u32[]{:S(2)}, u32[]{:S(2)}) collective-permute-start(f32[128,512]{1,0:T(8,128)S(1)} %get-tuple-element.36), channel_id=1, source_target_pairs={{1,0},{2,1},{3,2},{0,3},{5,4},{6,5},{7,6},{4,7},{9,8},{10,9},{11,1... | collective-permute-start | bytes 786440 | tf_op jit(solution)/shard_map/ppermute | solution.py:866
  8.5 0.0 collective-permute-done.r_ref
  8.5 0.0 copy-done.15
  8.5 0.0 copy-start
  8.6 0.0 copy-start.1
  8.6 0.0 copy-start.4
  8.6 0.0 copy-start.8
  8.6 0.0 copy-start.10
  8.6 0.0 copy-start.14
  8.6 0.0 copy-start.16
  8.6 0.0 copy-start.18
  8.6 0.0 copy-start.21
  8.7 2.6 %x_apply.1 = (f32[32,64,512]{2,1,0:T(8,128)S(1)}, f32[32,32,512]{2,1,0:T(8,128)S(1)}, f32[32,16,512]{2,1,0:T(8,128)S(1)}, f32[24,512]{1,0:T(8,128)S(1)}, f32[24,512]{1,0:T(8,128)S(1)}) custom-call(f32[32,64,512]{2,1,0:T(8,128)S(1)} %get-tuple-element.24.u_ref, f32[384,512]{1,0:T(8,128)S(1)} %collective-permute-done.r_ref, ...), custom_call_target="tpu_custom_call" | custom-call | flops 1000 | bytes 1000 | tf_op jit(solution)/shard_map/x_apply/pallas_call | solution.py:272
  11.3 0.0 copy-start.3
  11.3 0.0 copy-start.6
  11.3 0.0 copy-start.7
  11.3 0.0 copy-start.12
  11.4 0.0 copy-start.13
  11.4 0.0 copy-start.22
  11.4 1.7 %collective-permute-start.1 = (f32[24,512]{1,0:T(8,128)S(1)}, f32[24,512]{1,0:T(8,128)S(1)}, u32[]{:S(2)}, u32[]{:S(2)}) collective-permute-start(f32[24,512]{1,0:T(8,128)S(1)} %get-tuple-element.31), channel_id=1, source_target_pairs={{0,4},{4,8},{8,12},{12,0},{1,5},{5,9},{9,13},{13,1},{2,6},{6,10},{... | collective-permute-start | bytes 147464 | tf_op jit(solution)/shard_map/ppermute | solution.py:866
  13.1 1.3 %collective-permute-start.2 = (f32[24,512]{1,0:T(8,128)S(1)}, f32[24,512]{1,0:T(8,128)S(1)}, u32[]{:S(2)}, u32[]{:S(2)}) collective-permute-start(f32[24,512]{1,0:T(8,128)S(1)} %get-tuple-element.32), channel_id=1, source_target_pairs={{4,0},{8,4},{12,8},{0,12},{5,1},{9,5},{13,9},{1,13},{6,2},{10,6},{... | collective-permute-start | bytes 147464 | tf_op jit(solution)/shard_map/ppermute | solution.py:866
  14.4 2.4 %z_first.1 = (f32[192,512]{1,0:T(8,128)S(1)}, f32[112,512]{1,0:T(8,128)S(1)}, f32[16,512]{1,0:T(8,128)S(1)}, f32[16,32,512]{2,1,0:T(8,128)S(1)}, f32[8,16,512]{2,1,0:T(8,128)S(1)}) custom-call(f32[32,32,512]{2,1,0:T(8,128)S(1)} %get-tuple-element.27.x2, f32[32,16,512]{2,1,0:T(8,128)S(1)} %get-tuple-element.28.x3, f32[384,512]{1,0:T(8,128)S(1)} %collective-permute-done.r_ref), custom_call_target="tpu_custom_call" | custom-call | flops 1000 | bytes 1000 | tf_op jit(solution)/shard_map/z_first/pallas_call | solution.py:375
  16.7 0.0 collective-permute-done.1.fl
  16.7 0.4 %collective-permute-done.2.fr = f32[24,512]{1,0:T(8,128)S(1)} collective-permute-done((f32[24,512]{1,0:T(8,128)S(1)}, f32[24,512]{1,0:T(8,128)S(1)}, u32[]{:S(2)}, u32[]{:S(2)}) %collective-permute-start.2) | collective-permute-done | bytes 49184 | tf_op jit(solution)/shard_map/ppermute | solution.py:866
  17.2 0.0 copy-done.1
  17.2 0.9 %y_messages.1 = (f32[296,128]{1,0:T(8,128)S(1)}, f32[280,128]{1,0:T(8,128)S(1)}) custom-call(f32[192,512]{1,0:T(8,128)S(1)} %get-tuple-element.38.c2, f32[112,512]{1,0:T(8,128)S(1)} %get-tuple-element.39.c3, f32[16,512]{1,0:T(8,128)S(1)} %get-tuple-element.40.cf, f32[24,512]{1,0:T(8,128)S(1)} %collective-permute-done.1.fl, ...), custom_call_target="tpu_custom_call" | custom-call | flops 1000 | bytes 1000 | tf_op jit(solution)/shard_map/y_messages/pallas_call | solution.py:541
  18.1 0.2 collective-permute-start.5
  18.3 3.7 %collective-permute-start.6 = (f32[280,128]{1,0:T(8,128)S(1)}, f32[280,128]{1,0:T(8,128)S(1)}, u32[]{:S(2)}, u32[]{:S(2)}) collective-permute-start(f32[280,128]{1,0:T(8,128)S(1)} %get-tuple-element.42), channel_id=1, source_target_pairs={{1,0},{2,1},{3,2},{0,3},{5,4},{6,5},{7,6},{4,7},{9,8},{10,9},{11,1... | collective-permute-start | bytes 430088 | tf_op jit(solution)/shard_map/ppermute | solution.py:866
  22.0 0.0 copy-done.2
  22.0 0.0 copy-done.12
  22.0 0.0 copy-done.13
  22.0 0.0 copy-done.22
  22.0 0.0 copy-start.19
  22.0 0.0 copy-start.5
  22.0 0.0 copy-start.9
  22.0 0.0 copy-start.11
  22.1 0.0 copy-start.17
  22.1 6.3 %main_part.1 = (f32[4,32,64,128]{3,2,1,0:T(8,128)S(1)}, f32[8,128]{1,0:T(8,128)S(1)}, f32[32,64,512]{2,1,0:T(8,128)}) custom-call(f32[32,64,512]{2,1,0:T(8,128)S(1)} %get-tuple-element.26.x1, f32[16,32,512]{2,1,0:T(8,128)S(1)} %get-tuple-element.29.x2, f32[8,16,512]{2,1,0:T(8,128)S(1)} %get-tuple-element.30.x3, f32[24,512]{1,0:T(8,128)S(1)} %collective-permute-done.1.fl, ...), custom_call_target="tpu_custom_call" | custom-call | flops 1000 | bytes 1000 | tf_op jit(solution)/shard_map/main_part/pallas_call | solution.py:679
  28.4 0.0 collective-permute-done.3.b1
  28.4 0.0 collective-permute-done.4.a1
  28.4 0.0 copy-done.19
  28.4 0.7 %early_part.1.w_ref = f32[256,512]{1,0:T(8,128)S(1)} custom-call(f32[128,512]{1,0:T(8,128)S(1)} %collective-permute-done.3.b1, f32[128,512]{1,0:T(8,128)S(1)} %collective-permute-done.4.a1, bf16[2,768,256]{2,1,0:T(8,128)(2,1)S(1)} %copy-done, bf16[2,384,256]{2,1,0:T(8,128)(2,1)S(1)} %copy-done.1, bf16[64,192]{1,0:T(8,128)(2,1)S(1)} %copy-done.19, ...), custom_call_target="tpu_custom_call" | custom-call | flops 1000 | bytes 1000 | tf_op jit(solution)/shard_map/early_part/pallas_call | solution.py:713
  29.1 0.0 collective-permute-done.6.fr
  29.1 0.0 collective-permute-done.5.fl
  29.2 2.3 %z_apply.1 = f32[32,64,512]{2,1,0:T(8,128)} custom-call(f32[4,32,64,128]{3,2,1,0:T(8,128)S(1)} %get-tuple-element.33.in_ref, f32[32,64,512]{2,1,0:T(8,128)} %get-tuple-element.34.base_hbm, f32[256,512]{1,0:T(8,128)S(1)} %early_part.1.w_ref, f32[296,128]{1,0:T(8,128)S(1)} %collective-permute-done.5.fl, ...), custom_call_target="tpu_custom_call", output_to_operand_aliasing={{}: (1, {})} | custom-call | tf_op jit(solution)/shard_map/z_apply/pallas_call | solution.py:835
  (19 shorter events, 0.0 us)
Async XLA Ops:
  0.0 8.5 %copy-start.20 = (bf16[3,8,384]{2,1,0:T(8,128)(2,1)S(1)}, bf16[3,8,384]{2,1,0:T(8,128)(2,1)}, u32[]{:S(2)}) copy-start(bf16[3,8,384]{2,1,0:T(8,128)(2,1)} %constant.56.clone.c_ref) | copy-start | bytes 55300
  0.0 8.5 %copy-start.15 = (bf16[2,112,240]{2,1,0:T(8,128)(2,1)S(1)}, bf16[2,112,240]{2,1,0:T(8,128)(2,1)}, u32[]{:S(2)}) copy-start(bf16[2,112,240]{2,1,0:T(8,128)(2,1)} %constant.55.clone.t_ref) | copy-start | bytes 322564
  3.3 5.3 %collective-permute-start = (f32[384,512]{1,0:T(8,128)S(1)}, f32[384,512]{1,0:T(8,128)S(1)}, u32[]{:S(2)}, u32[]{:S(2)}) collective-permute-start(f32[384,512]{1,0:T(8,128)S(1)} %get-tuple-element.25), channel_id=1, source_target_pairs={{0,16},{16,0},{1,17},{17,1},{2,18},{18,2},{3,19},{19,3},{4,20},{20... | collective-permute-start | bytes 2359304 | tf_op jit(solution)/shard_map/ppermute | solution.py:202
  3.8 24.6 %collective-permute-start.3 = (f32[128,512]{1,0:T(8,128)S(1)}, f32[128,512]{1,0:T(8,128)S(1)}, u32[]{:S(2)}, u32[]{:S(2)}) collective-permute-start(f32[128,512]{1,0:T(8,128)S(1)} %get-tuple-element.35), channel_id=1, source_target_pairs={{0,1},{1,2},{2,3},{3,0},{4,5},{5,6},{6,7},{7,4},{8,9},{9,10},{10,1... | collective-permute-start | bytes 786440 | tf_op jit(solution)/shard_map/ppermute | solution.py:866
  6.4 22.0 %collective-permute-start.4 = (f32[128,512]{1,0:T(8,128)S(1)}, f32[128,512]{1,0:T(8,128)S(1)}, u32[]{:S(2)}, u32[]{:S(2)}) collective-permute-start(f32[128,512]{1,0:T(8,128)S(1)} %get-tuple-element.36), channel_id=1, source_target_pairs={{1,0},{2,1},{3,2},{0,3},{5,4},{6,5},{7,6},{4,7},{9,8},{10,9},{11,1... | collective-permute-start | bytes 786440 | tf_op jit(solution)/shard_map/ppermute | solution.py:866
  8.5 8.6 %copy-start = (bf16[2,768,256]{2,1,0:T(8,128)(2,1)S(1)}, bf16[2,768,256]{2,1,0:T(8,128)(2,1)}, u32[]{:S(2)}) copy-start(bf16[2,768,256]{2,1,0:T(8,128)(2,1)} %constant.48.clone.o1.own1) | copy-start | bytes 2359300
  8.6 8.6 %copy-start.1 = (bf16[2,384,256]{2,1,0:T(8,128)(2,1)S(1)}, bf16[2,384,256]{2,1,0:T(8,128)(2,1)}, u32[]{:S(2)}) copy-start(bf16[2,384,256]{2,1,0:T(8,128)(2,1)} %constant.49.clone.e1.edge1) | copy-start | bytes 1179652
  8.6 8.6 %copy-start.4 = (bf16[1536,256]{1,0:T(8,128)(2,1)S(1)}, bf16[1536,256]{1,0:T(8,128)(2,1)}, u32[]{:S(2)}) copy-start(bf16[1536,256]{1,0:T(8,128)(2,1)} %constant.57.clone.m2) | copy-start | bytes 2359300
  8.6 8.6 %copy-start.8 = (bf16[1536,128]{1,0:T(8,128)(2,1)S(1)}, bf16[1536,128]{1,0:T(8,128)(2,1)}, u32[]{:S(2)}) copy-start(bf16[1536,128]{1,0:T(8,128)(2,1)} %constant.58.clone.m3) | copy-start | bytes 1179652
  8.6 8.6 %copy-start.10 = (bf16[384,256]{1,0:T(8,128)(2,1)S(1)}, bf16[384,256]{1,0:T(8,128)(2,1)}, u32[]{:S(2)}) copy-start(bf16[384,256]{1,0:T(8,128)(2,1)} %constant.59.clone.h2) | copy-start | bytes 589828
  8.6 8.6 %copy-start.14 = (f32[224,128]{1,0:T(8,128)S(1)}, f32[224,128]{1,0:T(8,128)}, u32[]{:S(2)}) copy-start(f32[224,128]{1,0:T(8,128)} %constant.63.clone.k3) | copy-start | bytes 344068
  8.6 8.6 %copy-start.16 = (bf16[384,128]{1,0:T(8,128)(2,1)S(1)}, bf16[384,128]{1,0:T(8,128)(2,1)}, u32[]{:S(2)}) copy-start(bf16[384,128]{1,0:T(8,128)(2,1)} %constant.60.clone.h3) | copy-start | bytes 294916
  8.6 8.6 %copy-start.18 = (f32[96,128]{1,0:T(8,128)S(1)}, f32[96,128]{1,0:T(8,128)}, u32[]{:S(2)}) copy-start(f32[96,128]{1,0:T(8,128)} %constant.62.clone.k2) | copy-start | bytes 147460
  8.6 8.6 %copy-start.21 = (f32[32,128]{1,0:T(8,128)S(1)}, f32[32,128]{1,0:T(8,128)}, u32[]{:S(2)}) copy-start(f32[32,128]{1,0:T(8,128)} %constant.61.clone.k1) | copy-start | bytes 49156
  11.3 10.7 %copy-start.2 = (bf16[2,768,256]{2,1,0:T(8,128)(2,1)S(1)}, bf16[2,768,256]{2,1,0:T(8,128)(2,1)}, u32[]{:S(2)}) copy-start(bf16[2,768,256]{2,1,0:T(8,128)(2,1)} %constant.52.clone.o3) | copy-start | bytes 2359300
  11.3 10.7 %copy-start.3 = (bf16[2,768,256]{2,1,0:T(8,128)(2,1)S(1)}, bf16[2,768,256]{2,1,0:T(8,128)(2,1)}, u32[]{:S(2)}) copy-start(bf16[2,768,256]{2,1,0:T(8,128)(2,1)} %constant.50.clone.o2) | copy-start | bytes 2359300
  11.3 10.7 %copy-start.6 = (bf16[2,384,256]{2,1,0:T(8,128)(2,1)S(1)}, bf16[2,384,256]{2,1,0:T(8,128)(2,1)}, u32[]{:S(2)}) copy-start(bf16[2,384,256]{2,1,0:T(8,128)(2,1)} %constant.53.clone.e3) | copy-start | bytes 1179652
  11.3 10.7 %copy-start.7 = (bf16[2,384,256]{2,1,0:T(8,128)(2,1)S(1)}, bf16[2,384,256]{2,1,0:T(8,128)(2,1)}, u32[]{:S(2)}) copy-start(bf16[2,384,256]{2,1,0:T(8,128)(2,1)} %constant.51.clone.e2) | copy-start | bytes 1179652
  11.3 10.6 %copy-start.12 = (f32[256,128]{1,0:T(8,128)S(1)}, f32[256,128]{1,0:T(8,128)}, u32[]{:S(2)}) copy-start(f32[256,128]{1,0:T(8,128)} %constant.66.clone.k3) | copy-start | bytes 393220
  11.4 10.6 %copy-start.13 = (f32[256,128]{1,0:T(8,128)S(1)}, f32[256,128]{1,0:T(8,128)}, u32[]{:S(2)}) copy-start(f32[256,128]{1,0:T(8,128)} %constant.65.clone.k2) | copy-start | bytes 393220
  11.4 10.6 %copy-start.22 = (f32[8,128]{1,0:T(8,128)S(1)}, f32[8,128]{1,0:T(8,128)}, u32[]{:S(2)}) copy-start(f32[8,128]{1,0:T(8,128)} %constant.64.clone.k1) | copy-start | bytes 12292
  11.4 5.3 %collective-permute-start.1 = (f32[24,512]{1,0:T(8,128)S(1)}, f32[24,512]{1,0:T(8,128)S(1)}, u32[]{:S(2)}, u32[]{:S(2)}) collective-permute-start(f32[24,512]{1,0:T(8,128)S(1)} %get-tuple-element.31), channel_id=1, source_target_pairs={{0,4},{4,8},{8,12},{12,0},{1,5},{5,9},{9,13},{13,1},{2,6},{6,10},{... | collective-permute-start | bytes 147464 | tf_op jit(solution)/shard_map/ppermute | solution.py:866
  13.1 4.1 %collective-permute-start.2 = (f32[24,512]{1,0:T(8,128)S(1)}, f32[24,512]{1,0:T(8,128)S(1)}, u32[]{:S(2)}, u32[]{:S(2)}) collective-permute-start(f32[24,512]{1,0:T(8,128)S(1)} %get-tuple-element.32), channel_id=1, source_target_pairs={{4,0},{8,4},{12,8},{0,12},{5,1},{9,5},{13,9},{1,13},{6,2},{10,6},{... | collective-permute-start | bytes 147464 | tf_op jit(solution)/shard_map/ppermute | solution.py:866
  18.1 11.0 %collective-permute-start.5 = (f32[296,128]{1,0:T(8,128)S(1)}, f32[296,128]{1,0:T(8,128)S(1)}, u32[]{:S(2)}, u32[]{:S(2)}) collective-permute-start(f32[296,128]{1,0:T(8,128)S(1)} %get-tuple-element.41), channel_id=1, source_target_pairs={{0,1},{1,2},{2,3},{3,0},{4,5},{5,6},{6,7},{7,4},{8,9},{9,10},{10,1... | collective-permute-start | bytes 454664 | tf_op jit(solution)/shard_map/ppermute | solution.py:866
  18.3 10.8 %collective-permute-start.6 = (f32[280,128]{1,0:T(8,128)S(1)}, f32[280,128]{1,0:T(8,128)S(1)}, u32[]{:S(2)}, u32[]{:S(2)}) collective-permute-start(f32[280,128]{1,0:T(8,128)S(1)} %get-tuple-element.42), channel_id=1, source_target_pairs={{1,0},{2,1},{3,2},{0,3},{5,4},{6,5},{7,6},{4,7},{9,8},{10,9},{11,1... | collective-permute-start | bytes 430088 | tf_op jit(solution)/shard_map/ppermute | solution.py:866
  22.0 6.4 %copy-start.19 = (bf16[64,192]{1,0:T(8,128)(2,1)S(1)}, bf16[64,192]{1,0:T(8,128)(2,1)}, u32[]{:S(2)}) copy-start(bf16[64,192]{1,0:T(8,128)(2,1)} %constant.67.clone.xt) | copy-start | bytes 73732
  22.0 7.1 %copy-start.5 = (bf16[512,512]{1,0:T(8,128)(2,1)S(1)}, bf16[512,512]{1,0:T(8,128)(2,1)}, u32[]{:S(2)}) copy-start(bf16[512,512]{1,0:T(8,128)(2,1)} %constant.68.clone.t2) | copy-start | bytes 1572868
  22.0 7.1 %copy-start.9 = (bf16[256,512]{1,0:T(8,128)(2,1)S(1)}, bf16[256,512]{1,0:T(8,128)(2,1)}, u32[]{:S(2)}) copy-start(bf16[256,512]{1,0:T(8,128)(2,1)} %constant.69.clone.t3) | copy-start | bytes 786436
  22.0 7.1 %copy-start.11 = (bf16[128,512]{1,0:T(8,128)(2,1)S(1)}, bf16[128,512]{1,0:T(8,128)(2,1)}, u32[]{:S(2)}) copy-start(bf16[128,512]{1,0:T(8,128)(2,1)} %constant.71.clone.yf) | copy-start | bytes 393220
  22.1 7.1 %copy-start.17 = (bf16[256,48]{1,0:T(8,128)(2,1)S(1)}, bf16[256,48]{1,0:T(8,128)(2,1)}, u32[]{:S(2)}) copy-start(bf16[256,48]{1,0:T(8,128)(2,1)} %constant.70.clone.xf) | copy-start | bytes 73732

commit v3 on v2

--- a/solution.py
+++ b/solution.py
@@ -465,6 +465,11 @@
     return [0] + [int(n) for n in np.cumsum(parts)]
 
 
+def late_heights(counts, ny):
+    up, down = [late_rows(side, counts, ny)[-1] for side in (0, 1)]
+    return up, max(down, up + 8)
+
+
 def y_messages(combined, from_left, from_right, nz, band_one):
     c2, c3, cf = combined
     ny = c2.shape[1]
@@ -488,8 +493,9 @@
                             coef[c, zz, base + row + lane] = table[c, chunk * per + zz]
         coefs.append(coef.reshape(nums[level] * per, 128))
     places = [late_rows(side, counts, ny) for side in (0, 1)]
-
-    def kernel(c2, c3, cf, fl, fr, own1, edge1, m2, m3, h2, h3, k1, k2, k3, up_ref, down_ref):
+    heights = late_heights(counts, ny)
+
+    def kernel(c2, c3, cf, fl, fr, own1, edge1, m2, m3, h2, h3, k1, k2, k3, down_ref, up_ref):
         halo = turned(fl, fr)
 
         def reduced(k, n, num):
@@ -537,12 +543,14 @@
                 v = v + pltpu.roll(v, 4, 0)
                 both.append(v + pltpu.roll(v, 2, 0))
             ref[at[3] : at[4], :] = jnp.where(rows8 < 2, both[0], both[1])
+            if heights[side] > at[4]:
+                ref[at[4] :, :] = jnp.zeros((heights[side] - at[4], 128), F32)
 
     return pl.pallas_call(
         kernel,
         in_specs=[VM] * 14,
         out_specs=[VM] * 2,
-        out_shape=[vmem((at[-1], 128)) for at in places],
+        out_shape=[vmem((height, 128)) for height in reversed(heights)],
         compiler_params=params(24),
         cost_estimate=SHORT,
         name="y_messages",
@@ -876,7 +884,7 @@
     x1, x2, x3, to_right, to_left = x_apply(field, halo)
     from_left, from_right = swap(to_right, to_left, "gy")
     *combined, own2, own3 = z_first(x2, x3, halo)
-    up, down = y_messages(combined, from_left, from_right, nz, bands[0])
+    down, up = y_messages(combined, from_left, from_right, nz, bands[0])
     late_below, late_above = swap(up, down, "gz")
     inner, done, partial = main_part((x1, own2, own3), from_left, from_right, bands)
     early = early_part(below, above, bands[0], done)

time: 31.6 us -> 30 us (0.949)
  starting transfers between devices: 12.1 us -> 10.5 us
    ppermute x3, starting transfers between devices: 7.09 us -> 5.62 us  [swap(): lax.ppermute(to_left, axis, left)]
  transfers between devices with their start and end apart: 7 -> 7, of which waited for: 1 -> 2; matrix products, arithmetic and copies ran while one was open for 0% -> 0% of each run, Pallas kernels for 41% -> 43%
where the time goes in v3:
time: 30 us; the launch traced here: 29.9 us
  Pallas kernels  18.4 us (61%)
  starting transfers between devices  10.5 us (35%)
  waiting for transfers between devices  0.56 us (2%)
  between operations  0.35 us (1%)
    pallas_call x1, Pallas kernels, main_part(): pl.pallas_call(kernel, in_specs=[VM] * 14, out_specs=[VM, VM, HB], out_sh...  6.33 us
    ppermute x3, starting transfers between devices, swap(): lax.ppermute(to_left, axis, left)  5.62 us
    ppermute x3, starting transfers between devices, swap(): lax.ppermute(to_right, axis, right)  4.32 us
    pallas_call x1, Pallas kernels, x_send(): pl.pallas_call(kernel, in_specs=[HB, HB], out_specs=[VM] * 4, out_shape=[...  3.25 us
    pallas_call x1, Pallas kernels, x_apply(): pl.pallas_call(kernel, grid=(steps,), in_specs=[VM] * 4, out_specs=[VM] *...  2.64 us
    pallas_call x1, Pallas kernels, z_first(): pl.pallas_call(kernel, in_specs=[VM] * 3, out_specs=[VM] * 5, out_shape=[...  2.35 us
    pallas_call x1, Pallas kernels, z_apply(): pl.pallas_call(kernel, in_specs=[VM, HB] + [VM] * 7, out_specs=HB, out_sh...  2.27 us
    pallas_call x1, Pallas kernels, y_messages(): pl.pallas_call(kernel, in_specs=[VM] * 14, out_specs=[VM] * 2, out_shape=...  0.85 us
  transfers between devices with their start and end apart: 7, of which 2 were waited for; matrix products, arithmetic and copies ran while one was open for 0% of the time, Pallas kernels for 43%

profile of v3, /device:TPU:0, one launch (start us, length us, event | category | flops | bytes accessed | tf_op | source)
XLA Modules:
  0.0 29.9 jit_solution(4997112116859797021)
XLA Ops:
  0.0 3.2 %x_send.1 = (f32[32,64,512]{2,1,0:T(8,128)S(1)}, f32[384,512]{1,0:T(8,128)S(1)}, f32[128,512]{1,0:T(8,128)S(1)}, f32[128,512]{1,0:T(8,128)S(1)}) custom-call(f32[32,64,512]{2,1,0:T(8,128)} %u_hbm.1, bf16[96,256]{1,0:T(8,128)(2,1)} %constant.54.clone.c_hbm), custom_call_target="tpu_custom_call" | custom-call | flops 1000 | bytes 1000 | tf_op jit(solution)/shard_map/x_send/pallas_call | solution.py:182
  3.3 0.5 %collective-permute-start = (f32[384,512]{1,0:T(8,128)S(1)}, f32[384,512]{1,0:T(8,128)S(1)}, u32[]{:S(2)}, u32[]{:S(2)}) collective-permute-start(f32[384,512]{1,0:T(8,128)S(1)} %get-tuple-element.25), channel_id=1, source_target_pairs={{0,16},{16,0},{1,17},{17,1},{2,18},{18,2},{3,19},{19,3},{4,20},{20... | collective-permute-start | bytes 2359304 | tf_op jit(solution)/shard_map/ppermute | solution.py:202
  3.8 2.6 %collective-permute-start.3 = (f32[128,512]{1,0:T(8,128)S(1)}, f32[128,512]{1,0:T(8,128)S(1)}, u32[]{:S(2)}, u32[]{:S(2)}) collective-permute-start(f32[128,512]{1,0:T(8,128)S(1)} %get-tuple-element.35), channel_id=1, source_target_pairs={{0,1},{1,2},{2,3},{3,0},{4,5},{5,6},{6,7},{7,4},{8,9},{9,10},{10,1... | collective-permute-start | bytes 786440 | tf_op jit(solution)/shard_map/ppermute | solution.py:874
  6.4 2.1 %collective-permute-start.4 = (f32[128,512]{1,0:T(8,128)S(1)}, f32[128,512]{1,0:T(8,128)S(1)}, u32[]{:S(2)}, u32[]{:S(2)}) collective-permute-start(f32[128,512]{1,0:T(8,128)S(1)} %get-tuple-element.36), channel_id=1, source_target_pairs={{1,0},{2,1},{3,2},{0,3},{5,4},{6,5},{7,6},{4,7},{9,8},{10,9},{11,1... | collective-permute-start | bytes 786440 | tf_op jit(solution)/shard_map/ppermute | solution.py:874
  8.5 0.0 collective-permute-done.r_ref
  8.5 0.0 copy-done.20
  8.5 0.0 copy-start
  8.6 0.0 copy-start.1
  8.6 0.0 copy-start.4
  8.6 0.0 copy-start.8
  8.6 0.0 copy-start.10
  8.6 0.0 copy-start.14
  8.6 0.0 copy-start.16
  8.6 0.0 copy-start.18
  8.6 0.0 copy-start.21
  8.7 2.6 %x_apply.1 = (f32[32,64,512]{2,1,0:T(8,128)S(1)}, f32[32,32,512]{2,1,0:T(8,128)S(1)}, f32[32,16,512]{2,1,0:T(8,128)S(1)}, f32[24,512]{1,0:T(8,128)S(1)}, f32[24,512]{1,0:T(8,128)S(1)}) custom-call(f32[32,64,512]{2,1,0:T(8,128)S(1)} %get-tuple-element.24.u_ref, f32[384,512]{1,0:T(8,128)S(1)} %collective-permute-done.r_ref, ...), custom_call_target="tpu_custom_call" | custom-call | flops 1000 | bytes 1000 | tf_op jit(solution)/shard_map/x_apply/pallas_call | solution.py:272
  11.3 0.0 copy-start.3
  11.3 0.0 copy-start.6
  11.3 0.0 copy-start.7
  11.3 0.0 copy-start.11
  11.4 0.0 copy-start.12
  11.4 0.0 copy-start.22
  11.4 1.7 %collective-permute-start.1 = (f32[24,512]{1,0:T(8,128)S(1)}, f32[24,512]{1,0:T(8,128)S(1)}, u32[]{:S(2)}, u32[]{:S(2)}) collective-permute-start(f32[24,512]{1,0:T(8,128)S(1)} %get-tuple-element.31), channel_id=1, source_target_pairs={{0,4},{4,8},{8,12},{12,0},{1,5},{5,9},{9,13},{13,1},{2,6},{6,10},{... | collective-permute-start | bytes 147464 | tf_op jit(solution)/shard_map/ppermute | solution.py:874
  13.1 1.3 %collective-permute-start.2 = (f32[24,512]{1,0:T(8,128)S(1)}, f32[24,512]{1,0:T(8,128)S(1)}, u32[]{:S(2)}, u32[]{:S(2)}) collective-permute-start(f32[24,512]{1,0:T(8,128)S(1)} %get-tuple-element.32), channel_id=1, source_target_pairs={{4,0},{8,4},{12,8},{0,12},{5,1},{9,5},{13,9},{1,13},{6,2},{10,6},{... | collective-permute-start | bytes 147464 | tf_op jit(solution)/shard_map/ppermute | solution.py:874
  14.4 2.4 %z_first.1 = (f32[192,512]{1,0:T(8,128)S(1)}, f32[112,512]{1,0:T(8,128)S(1)}, f32[16,512]{1,0:T(8,128)S(1)}, f32[16,32,512]{2,1,0:T(8,128)S(1)}, f32[8,16,512]{2,1,0:T(8,128)S(1)}) custom-call(f32[32,32,512]{2,1,0:T(8,128)S(1)} %get-tuple-element.27.x2, f32[32,16,512]{2,1,0:T(8,128)S(1)} %get-tuple-element.28.x3, f32[384,512]{1,0:T(8,128)S(1)} %collective-permute-done.r_ref), custom_call_target="tpu_custom_call" | custom-call | flops 1000 | bytes 1000 | tf_op jit(solution)/shard_map/z_first/pallas_call | solution.py:375
  16.7 0.0 collective-permute-done.1.fl
  16.7 0.4 %collective-permute-done.2.fr = f32[24,512]{1,0:T(8,128)S(1)} collective-permute-done((f32[24,512]{1,0:T(8,128)S(1)}, f32[24,512]{1,0:T(8,128)S(1)}, u32[]{:S(2)}, u32[]{:S(2)}) %collective-permute-start.2) | collective-permute-done | bytes 49184 | tf_op jit(solution)/shard_map/ppermute | solution.py:874
  17.2 0.0 copy-done
  17.2 0.9 %y_messages.1 = (f32[304,128]{1,0:T(8,128)S(1)}, f32[296,128]{1,0:T(8,128)S(1)}) custom-call(f32[192,512]{1,0:T(8,128)S(1)} %get-tuple-element.38.c2, f32[112,512]{1,0:T(8,128)S(1)} %get-tuple-element.39.c3, f32[16,512]{1,0:T(8,128)S(1)} %get-tuple-element.40.cf, f32[24,512]{1,0:T(8,128)S(1)} %collective-permute-done.1.fl, ...), custom_call_target="tpu_custom_call" | custom-call | flops 1000 | bytes 1000 | tf_op jit(solution)/shard_map/y_messages/pallas_call | solution.py:549
  18.1 2.2 %collective-permute-start.6 = (f32[304,128]{1,0:T(8,128)S(1)}, f32[304,128]{1,0:T(8,128)S(1)}, u32[]{:S(2)}, u32[]{:S(2)}) collective-permute-start(f32[304,128]{1,0:T(8,128)S(1)} %get-tuple-element.42), channel_id=1, source_target_pairs={{1,0},{2,1},{3,2},{0,3},{5,4},{6,5},{7,6},{4,7},{9,8},{10,9},{11,1... | collective-permute-start | bytes 466952 | tf_op jit(solution)/shard_map/ppermute | solution.py:874
  20.3 0.0 collective-permute-start.5
  20.3 0.0 copy-done.6
  20.3 0.0 copy-done.7
  20.3 0.0 copy-done.11
  20.4 0.0 copy-done.12
  20.4 0.0 copy-done.22
  20.4 0.0 copy-start.19
  20.4 0.0 copy-start.5
  20.4 0.0 copy-start.9
  20.4 0.0 copy-start.13
  20.4 0.0 copy-start.17
  20.4 6.3 %main_part.1 = (f32[4,32,64,128]{3,2,1,0:T(8,128)S(1)}, f32[8,128]{1,0:T(8,128)S(1)}, f32[32,64,512]{2,1,0:T(8,128)}) custom-call(f32[32,64,512]{2,1,0:T(8,128)S(1)} %get-tuple-element.26.x1, f32[16,32,512]{2,1,0:T(8,128)S(1)} %get-tuple-element.29.x2, f32[8,16,512]{2,1,0:T(8,128)S(1)} %get-tuple-element.30.x3, f32[24,512]{1,0:T(8,128)S(1)} %collective-permute-done.1.fl, ...), custom_call_target="tpu_custom_call" | custom-call | flops 1000 | bytes 1000 | tf_op jit(solution)/shard_map/main_part/pallas_call | solution.py:687
  26.8 0.0 collective-permute-done.3.b1
  26.8 0.0 collective-permute-done.4.a1
  26.8 0.7 %early_part.1.w_ref = f32[256,512]{1,0:T(8,128)S(1)} custom-call(f32[128,512]{1,0:T(8,128)S(1)} %collective-permute-done.3.b1, f32[128,512]{1,0:T(8,128)S(1)} %collective-permute-done.4.a1, bf16[2,768,256]{2,1,0:T(8,128)(2,1)S(1)} %copy-done, bf16[2,384,256]{2,1,0:T(8,128)(2,1)S(1)} %copy-done.1, bf16[64,192]{1,0:T(8,128)(2,1)S(1)} %copy-done.19, ...), custom_call_target="tpu_custom_call" | custom-call | flops 1000 | bytes 1000 | tf_op jit(solution)/shard_map/early_part/pallas_call | solution.py:721
  27.5 0.1 collective-permute-done.5.fl
  27.6 0.0 collective-permute-done.6.fr
  27.6 2.3 %z_apply.1 = f32[32,64,512]{2,1,0:T(8,128)} custom-call(f32[4,32,64,128]{3,2,1,0:T(8,128)S(1)} %get-tuple-element.33.in_ref, f32[32,64,512]{2,1,0:T(8,128)} %get-tuple-element.34.base_hbm, f32[256,512]{1,0:T(8,128)S(1)} %early_part.1.w_ref, f32[296,128]{1,0:T(8,128)S(1)} %collective-permute-done.5.fl, ...), custom_call_target="tpu_custom_call", output_to_operand_aliasing={{}: (1, {})} | custom-call | tf_op jit(solution)/shard_map/z_apply/pallas_call | solution.py:843
  (19 shorter events, 0.0 us)
Async XLA Ops:
  0.0 8.5 %copy-start.20 = (bf16[3,8,384]{2,1,0:T(8,128)(2,1)S(1)}, bf16[3,8,384]{2,1,0:T(8,128)(2,1)}, u32[]{:S(2)}) copy-start(bf16[3,8,384]{2,1,0:T(8,128)(2,1)} %constant.56.clone.c_ref) | copy-start | bytes 55300
  0.0 8.5 %copy-start.15 = (bf16[2,112,240]{2,1,0:T(8,128)(2,1)S(1)}, bf16[2,112,240]{2,1,0:T(8,128)(2,1)}, u32[]{:S(2)}) copy-start(bf16[2,112,240]{2,1,0:T(8,128)(2,1)} %constant.55.clone.t_ref) | copy-start | bytes 322564
  3.3 5.3 %collective-permute-start = (f32[384,512]{1,0:T(8,128)S(1)}, f32[384,512]{1,0:T(8,128)S(1)}, u32[]{:S(2)}, u32[]{:S(2)}) collective-permute-start(f32[384,512]{1,0:T(8,128)S(1)} %get-tuple-element.25), channel_id=1, source_target_pairs={{0,16},{16,0},{1,17},{17,1},{2,18},{18,2},{3,19},{19,3},{4,20},{20... | collective-permute-start | bytes 2359304 | tf_op jit(solution)/shard_map/ppermute | solution.py:202
  3.8 23.0 %collective-permute-start.3 = (f32[128,512]{1,0:T(8,128)S(1)}, f32[128,512]{1,0:T(8,128)S(1)}, u32[]{:S(2)}, u32[]{:S(2)}) collective-permute-start(f32[128,512]{1,0:T(8,128)S(1)} %get-tuple-element.35), channel_id=1, source_target_pairs={{0,1},{1,2},{2,3},{3,0},{4,5},{5,6},{6,7},{7,4},{8,9},{9,10},{10,1... | collective-permute-start | bytes 786440 | tf_op jit(solution)/shard_map/ppermute | solution.py:874
  6.4 20.4 %collective-permute-start.4 = (f32[128,512]{1,0:T(8,128)S(1)}, f32[128,512]{1,0:T(8,128)S(1)}, u32[]{:S(2)}, u32[]{:S(2)}) collective-permute-start(f32[128,512]{1,0:T(8,128)S(1)} %get-tuple-element.36), channel_id=1, source_target_pairs={{1,0},{2,1},{3,2},{0,3},{5,4},{6,5},{7,6},{4,7},{9,8},{10,9},{11,1... | collective-permute-start | bytes 786440 | tf_op jit(solution)/shard_map/ppermute | solution.py:874
  8.5 8.6 %copy-start = (bf16[2,768,256]{2,1,0:T(8,128)(2,1)S(1)}, bf16[2,768,256]{2,1,0:T(8,128)(2,1)}, u32[]{:S(2)}) copy-start(bf16[2,768,256]{2,1,0:T(8,128)(2,1)} %constant.48.clone.o1.own1) | copy-start | bytes 2359300
  8.6 8.6 %copy-start.1 = (bf16[2,384,256]{2,1,0:T(8,128)(2,1)S(1)}, bf16[2,384,256]{2,1,0:T(8,128)(2,1)}, u32[]{:S(2)}) copy-start(bf16[2,384,256]{2,1,0:T(8,128)(2,1)} %constant.49.clone.e1.edge1) | copy-start | bytes 1179652
  8.6 8.6 %copy-start.4 = (bf16[1536,256]{1,0:T(8,128)(2,1)S(1)}, bf16[1536,256]{1,0:T(8,128)(2,1)}, u32[]{:S(2)}) copy-start(bf16[1536,256]{1,0:T(8,128)(2,1)} %constant.57.clone.m2) | copy-start | bytes 2359300
  8.6 8.6 %copy-start.8 = (bf16[1536,128]{1,0:T(8,128)(2,1)S(1)}, bf16[1536,128]{1,0:T(8,128)(2,1)}, u32[]{:S(2)}) copy-start(bf16[1536,128]{1,0:T(8,128)(2,1)} %constant.58.clone.m3) | copy-start | bytes 1179652
  8.6 8.6 %copy-start.10 = (bf16[384,256]{1,0:T(8,128)(2,1)S(1)}, bf16[384,256]{1,0:T(8,128)(2,1)}, u32[]{:S(2)}) copy-start(bf16[384,256]{1,0:T(8,128)(2,1)} %constant.59.clone.h2) | copy-start | bytes 589828
  8.6 8.6 %copy-start.14 = (f32[224,128]{1,0:T(8,128)S(1)}, f32[224,128]{1,0:T(8,128)}, u32[]{:S(2)}) copy-start(f32[224,128]{1,0:T(8,128)} %constant.63.clone.k3) | copy-start | bytes 344068
  8.6 8.6 %copy-start.16 = (bf16[384,128]{1,0:T(8,128)(2,1)S(1)}, bf16[384,128]{1,0:T(8,128)(2,1)}, u32[]{:S(2)}) copy-start(bf16[384,128]{1,0:T(8,128)(2,1)} %constant.60.clone.h3) | copy-start | bytes 294916
  8.6 8.6 %copy-start.18 = (f32[96,128]{1,0:T(8,128)S(1)}, f32[96,128]{1,0:T(8,128)}, u32[]{:S(2)}) copy-start(f32[96,128]{1,0:T(8,128)} %constant.62.clone.k2) | copy-start | bytes 147460
  8.6 8.6 %copy-start.21 = (f32[32,128]{1,0:T(8,128)S(1)}, f32[32,128]{1,0:T(8,128)}, u32[]{:S(2)}) copy-start(f32[32,128]{1,0:T(8,128)} %constant.61.clone.k1) | copy-start | bytes 49156
  11.3 9.0 %copy-start.2 = (bf16[2,768,256]{2,1,0:T(8,128)(2,1)S(1)}, bf16[2,768,256]{2,1,0:T(8,128)(2,1)}, u32[]{:S(2)}) copy-start(bf16[2,768,256]{2,1,0:T(8,128)(2,1)} %constant.52.clone.o3) | copy-start | bytes 2359300
  11.3 9.0 %copy-start.3 = (bf16[2,768,256]{2,1,0:T(8,128)(2,1)S(1)}, bf16[2,768,256]{2,1,0:T(8,128)(2,1)}, u32[]{:S(2)}) copy-start(bf16[2,768,256]{2,1,0:T(8,128)(2,1)} %constant.50.clone.o2) | copy-start | bytes 2359300
  11.3 9.0 %copy-start.6 = (bf16[2,384,256]{2,1,0:T(8,128)(2,1)S(1)}, bf16[2,384,256]{2,1,0:T(8,128)(2,1)}, u32[]{:S(2)}) copy-start(bf16[2,384,256]{2,1,0:T(8,128)(2,1)} %constant.53.clone.e3) | copy-start | bytes 1179652
  11.3 9.0 %copy-start.7 = (bf16[2,384,256]{2,1,0:T(8,128)(2,1)S(1)}, bf16[2,384,256]{2,1,0:T(8,128)(2,1)}, u32[]{:S(2)}) copy-start(bf16[2,384,256]{2,1,0:T(8,128)(2,1)} %constant.51.clone.e2) | copy-start | bytes 1179652
  11.3 9.0 %copy-start.11 = (f32[256,128]{1,0:T(8,128)S(1)}, f32[256,128]{1,0:T(8,128)}, u32[]{:S(2)}) copy-start(f32[256,128]{1,0:T(8,128)} %constant.66.clone.k3) | copy-start | bytes 393220
  11.4 9.0 %copy-start.12 = (f32[256,128]{1,0:T(8,128)S(1)}, f32[256,128]{1,0:T(8,128)}, u32[]{:S(2)}) copy-start(f32[256,128]{1,0:T(8,128)} %constant.65.clone.k2) | copy-start | bytes 393220
  11.4 9.0 %copy-start.22 = (f32[8,128]{1,0:T(8,128)S(1)}, f32[8,128]{1,0:T(8,128)}, u32[]{:S(2)}) copy-start(f32[8,128]{1,0:T(8,128)} %constant.64.clone.k1) | copy-start | bytes 12292
  11.4 5.3 %collective-permute-start.1 = (f32[24,512]{1,0:T(8,128)S(1)}, f32[24,512]{1,0:T(8,128)S(1)}, u32[]{:S(2)}, u32[]{:S(2)}) collective-permute-start(f32[24,512]{1,0:T(8,128)S(1)} %get-tuple-element.31), channel_id=1, source_target_pairs={{0,4},{4,8},{8,12},{12,0},{1,5},{5,9},{9,13},{13,1},{2,6},{6,10},{... | collective-permute-start | bytes 147464 | tf_op jit(solution)/shard_map/ppermute | solution.py:874
  13.1 4.1 %collective-permute-start.2 = (f32[24,512]{1,0:T(8,128)S(1)}, f32[24,512]{1,0:T(8,128)S(1)}, u32[]{:S(2)}, u32[]{:S(2)}) collective-permute-start(f32[24,512]{1,0:T(8,128)S(1)} %get-tuple-element.32), channel_id=1, source_target_pairs={{4,0},{8,4},{12,8},{0,12},{5,1},{9,5},{13,9},{1,13},{6,2},{10,6},{... | collective-permute-start | bytes 147464 | tf_op jit(solution)/shard_map/ppermute | solution.py:874
  18.1 9.5 %collective-permute-start.6 = (f32[304,128]{1,0:T(8,128)S(1)}, f32[304,128]{1,0:T(8,128)S(1)}, u32[]{:S(2)}, u32[]{:S(2)}) collective-permute-start(f32[304,128]{1,0:T(8,128)S(1)} %get-tuple-element.42), channel_id=1, source_target_pairs={{1,0},{2,1},{3,2},{0,3},{5,4},{6,5},{7,6},{4,7},{9,8},{10,9},{11,1... | collective-permute-start | bytes 466952 | tf_op jit(solution)/shard_map/ppermute | solution.py:874
  20.3 7.3 %collective-permute-start.5 = (f32[296,128]{1,0:T(8,128)S(1)}, f32[296,128]{1,0:T(8,128)S(1)}, u32[]{:S(2)}, u32[]{:S(2)}) collective-permute-start(f32[296,128]{1,0:T(8,128)S(1)} %get-tuple-element.41), channel_id=1, source_target_pairs={{0,1},{1,2},{2,3},{3,0},{4,5},{5,6},{6,7},{7,4},{8,9},{9,10},{10,1... | collective-permute-start | bytes 454664 | tf_op jit(solution)/shard_map/ppermute | solution.py:874
  20.4 6.4 %copy-start.19 = (bf16[64,192]{1,0:T(8,128)(2,1)S(1)}, bf16[64,192]{1,0:T(8,128)(2,1)}, u32[]{:S(2)}) copy-start(bf16[64,192]{1,0:T(8,128)(2,1)} %constant.67.clone.xt) | copy-start | bytes 73732
  20.4 7.2 %copy-start.5 = (bf16[512,512]{1,0:T(8,128)(2,1)S(1)}, bf16[512,512]{1,0:T(8,128)(2,1)}, u32[]{:S(2)}) copy-start(bf16[512,512]{1,0:T(8,128)(2,1)} %constant.68.clone.t2) | copy-start | bytes 1572868
  20.4 7.2 %copy-start.9 = (bf16[256,512]{1,0:T(8,128)(2,1)S(1)}, bf16[256,512]{1,0:T(8,128)(2,1)}, u32[]{:S(2)}) copy-start(bf16[256,512]{1,0:T(8,128)(2,1)} %constant.69.clone.t3) | copy-start | bytes 786436
  20.4 7.2 %copy-start.13 = (bf16[128,512]{1,0:T(8,128)(2,1)S(1)}, bf16[128,512]{1,0:T(8,128)(2,1)}, u32[]{:S(2)}) copy-start(bf16[128,512]{1,0:T(8,128)(2,1)} %constant.71.clone.yf) | copy-start | bytes 393220
  20.4 7.2 %copy-start.17 = (bf16[256,48]{1,0:T(8,128)(2,1)S(1)}, bf16[256,48]{1,0:T(8,128)(2,1)}, u32[]{:S(2)}) copy-start(bf16[256,48]{1,0:T(8,128)(2,1)} %constant.70.clone.xf) | copy-start | bytes 73732

commit v4 on v3

--- a/solution.py
+++ b/solution.py
@@ -466,8 +466,7 @@
 
 
 def late_heights(counts, ny):
-    up, down = [late_rows(side, counts, ny)[-1] for side in (0, 1)]
-    return up, max(down, up + 8)
+    return (max(late_rows(side, counts, ny)[-1] for side in (0, 1)),) * 2
 
 
 def y_messages(combined, from_left, from_right, nz, band_one):
@@ -708,7 +707,7 @@
     nx, ny = below.shape[0] // 2, below.shape[1]
     _, _, maps = joint_sides(nx)
 
-    def kernel(b1, a1, o1, e1, xt, after_ref, w_ref):
+    def kernel(a1, b1, o1, e1, xt, after_ref, w_ref):
         del after_ref
         early = []
         for ref in (b1, a1):
@@ -726,7 +725,7 @@
         compiler_params=params(16),
         cost_estimate=SHORT,
         name="early_part",
-    )(below, above, *band, jnp.asarray(stack_lhs(maps[0][0])), after)
+    )(above, below, *band, jnp.asarray(stack_lhs(maps[0][0])), after)
 
 
 def z_apply(inner, partial, early, from_left, from_right):
@@ -751,7 +750,7 @@
     side_rows = np.concatenate([side_hi, side_hi, side_lo, np.zeros((104, ny), side_hi.dtype)])
     touched = sorted(touched_layers(nz), key=lambda z: np.abs(maps[0][z]).max() > 1e-12)
 
-    def kernel(in_ref, base_hbm, w_ref, fl, fr, t2, t3, xf, yf, out_hbm, s1, s2, s3, buf, sem):
+    def kernel(in_ref, base_hbm, w_ref, fr, fl, t2, t3, xf, yf, out_hbm, s1, s2, s3, buf, sem):
         del base_hbm
         s3[...] = jnp.zeros(s3.shape, F32)
         halos = [
@@ -859,8 +858,8 @@
         inner,
         partial,
         early,
+        from_right,
         from_left,
-        from_right,
         *[jnp.asarray(t) for t in tables],
         jnp.asarray(stack_lhs(frame)),
         jnp.asarray(side_rows),

time: 30 us -> 31.4 us (1.047)
  starting transfers between devices: 10.5 us -> 11.8 us
    ppermute x3, starting transfers between devices: 5.62 us -> 9.72 us  [swap(): lax.ppermute(to_left, axis, left)]
    ppermute x3, starting transfers between devices: 4.32 us -> 1.55 us  [swap(): lax.ppermute(to_right, axis, right)]
  transfers between devices with their start and end apart: 7 -> 7, of which waited for: 2 -> 1; matrix products, arithmetic and copies ran while one was open for 0% -> 0% of each run, Pallas kernels for 43% -> 41%
where the time goes in v4:
time: 31.4 us; the launch traced here: 31.3 us
  Pallas kernels  18.4 us (59%)
  starting transfers between devices  11.8 us (38%)
  waiting for transfers between devices  0.54 us (2%)
  between operations  0.38 us (1%)
    ppermute x3, starting transfers between devices, swap(): lax.ppermute(to_left, axis, left)  9.72 us
    pallas_call x1, Pallas kernels, main_part(): pl.pallas_call(kernel, in_specs=[VM] * 14, out_specs=[VM, VM, HB], out_sh...  6.31 us
    pallas_call x1, Pallas kernels, x_send(): pl.pallas_call(kernel, in_specs=[HB, HB], out_specs=[VM] * 4, out_shape=[...  3.25 us
    pallas_call x1, Pallas kernels, x_apply(): pl.pallas_call(kernel, grid=(steps,), in_specs=[VM] * 4, out_specs=[VM] *...  2.64 us
    pallas_call x1, Pallas kernels, z_first(): pl.pallas_call(kernel, in_specs=[VM] * 3, out_specs=[VM] * 5, out_shape=[...  2.35 us
    pallas_call x1, Pallas kernels, z_apply(): pl.pallas_call(kernel, in_specs=[VM, HB] + [VM] * 7, out_specs=HB, out_sh...  2.31 us
    ppermute x3, starting transfers between devices, swap(): lax.ppermute(to_right, axis, right)  1.55 us
    pallas_call x1, Pallas kernels, y_messages(): pl.pallas_call(kernel, in_specs=[VM] * 14, out_specs=[VM] * 2, out_shape=...  0.86 us
  transfers between devices with their start and end apart: 7, of which 1 were waited for; matrix products, arithmetic and copies ran while one was open for 0% of the time, Pallas kernels for 41%

profile of v4, /device:TPU:0, one launch (start us, length us, event | category | flops | bytes accessed | tf_op | source)
XLA Modules:
  0.0 31.3 jit_solution(1742597776976807561)
XLA Ops:
  0.0 3.2 %x_send.1 = (f32[32,64,512]{2,1,0:T(8,128)S(1)}, f32[384,512]{1,0:T(8,128)S(1)}, f32[128,512]{1,0:T(8,128)S(1)}, f32[128,512]{1,0:T(8,128)S(1)}) custom-call(f32[32,64,512]{2,1,0:T(8,128)} %u_hbm.1, bf16[96,256]{1,0:T(8,128)(2,1)} %constant.54.clone.c_hbm), custom_call_target="tpu_custom_call" | custom-call | flops 1000 | bytes 1000 | tf_op jit(solution)/shard_map/x_send/pallas_call | solution.py:182
  3.3 0.5 %collective-permute-start = (f32[384,512]{1,0:T(8,128)S(1)}, f32[384,512]{1,0:T(8,128)S(1)}, u32[]{:S(2)}, u32[]{:S(2)}) collective-permute-start(f32[384,512]{1,0:T(8,128)S(1)} %get-tuple-element.25), channel_id=1, source_target_pairs={{0,16},{16,0},{1,17},{17,1},{2,18},{18,2},{3,19},{19,3},{4,20},{20... | collective-permute-start | bytes 2359304 | tf_op jit(solution)/shard_map/ppermute | solution.py:202
  3.8 4.7 %collective-permute-start.3 = (f32[128,512]{1,0:T(8,128)S(1)}, f32[128,512]{1,0:T(8,128)S(1)}, u32[]{:S(2)}, u32[]{:S(2)}) collective-permute-start(f32[128,512]{1,0:T(8,128)S(1)} %get-tuple-element.35), channel_id=1, source_target_pairs={{1,0},{2,1},{3,2},{0,3},{5,4},{6,5},{7,6},{4,7},{9,8},{10,9},{11,1... | collective-permute-start | bytes 786440 | tf_op jit(solution)/shard_map/ppermute | solution.py:873
  8.4 0.0 collective-permute-start.4
  8.4 0.0 collective-permute-done.r_ref
  8.4 0.0 copy-done.20
  8.5 0.0 copy-done.15
  8.5 0.0 copy-start
  8.5 0.0 copy-start.1
  8.5 0.0 copy-start.4
  8.5 0.0 copy-start.8
  8.5 0.0 copy-start.10
  8.5 0.0 copy-start.14
  8.5 0.0 copy-start.16
  8.6 0.0 copy-start.18
  8.6 0.0 copy-start.21
  8.6 2.6 %x_apply.1 = (f32[32,64,512]{2,1,0:T(8,128)S(1)}, f32[32,32,512]{2,1,0:T(8,128)S(1)}, f32[32,16,512]{2,1,0:T(8,128)S(1)}, f32[24,512]{1,0:T(8,128)S(1)}, f32[24,512]{1,0:T(8,128)S(1)}) custom-call(f32[32,64,512]{2,1,0:T(8,128)S(1)} %get-tuple-element.24.u_ref, f32[384,512]{1,0:T(8,128)S(1)} %collective-permute-done.r_ref, ...), custom_call_target="tpu_custom_call" | custom-call | flops 1000 | bytes 1000 | tf_op jit(solution)/shard_map/x_apply/pallas_call | solution.py:272
  11.2 0.0 copy-start.3
  11.2 0.0 copy-start.6
  11.3 0.0 copy-start.7
  11.3 0.0 copy-start.12
  11.3 0.0 copy-start.13
  11.3 0.0 copy-start.22
  11.3 1.5 %collective-permute-start.1 = (f32[24,512]{1,0:T(8,128)S(1)}, f32[24,512]{1,0:T(8,128)S(1)}, u32[]{:S(2)}, u32[]{:S(2)}) collective-permute-start(f32[24,512]{1,0:T(8,128)S(1)} %get-tuple-element.31), channel_id=1, source_target_pairs={{0,4},{4,8},{8,12},{12,0},{1,5},{5,9},{9,13},{13,1},{2,6},{6,10},{... | collective-permute-start | bytes 147464 | tf_op jit(solution)/shard_map/ppermute | solution.py:873
  12.8 1.4 %collective-permute-start.2 = (f32[24,512]{1,0:T(8,128)S(1)}, f32[24,512]{1,0:T(8,128)S(1)}, u32[]{:S(2)}, u32[]{:S(2)}) collective-permute-start(f32[24,512]{1,0:T(8,128)S(1)} %get-tuple-element.32), channel_id=1, source_target_pairs={{4,0},{8,4},{12,8},{0,12},{5,1},{9,5},{13,9},{1,13},{6,2},{10,6},{... | collective-permute-start | bytes 147464 | tf_op jit(solution)/shard_map/ppermute | solution.py:873
  14.3 2.4 %z_first.1 = (f32[192,512]{1,0:T(8,128)S(1)}, f32[112,512]{1,0:T(8,128)S(1)}, f32[16,512]{1,0:T(8,128)S(1)}, f32[16,32,512]{2,1,0:T(8,128)S(1)}, f32[8,16,512]{2,1,0:T(8,128)S(1)}) custom-call(f32[32,32,512]{2,1,0:T(8,128)S(1)} %get-tuple-element.27.x2, f32[32,16,512]{2,1,0:T(8,128)S(1)} %get-tuple-element.28.x3, f32[384,512]{1,0:T(8,128)S(1)} %collective-permute-done.r_ref), custom_call_target="tpu_custom_call" | custom-call | flops 1000 | bytes 1000 | tf_op jit(solution)/shard_map/z_first/pallas_call | solution.py:375
  16.6 0.0 collective-permute-done.1.fl
  16.7 0.5 %collective-permute-done.2.fr = f32[24,512]{1,0:T(8,128)S(1)} collective-permute-done((f32[24,512]{1,0:T(8,128)S(1)}, f32[24,512]{1,0:T(8,128)S(1)}, u32[]{:S(2)}, u32[]{:S(2)}) %collective-permute-start.2) | collective-permute-done | bytes 49184 | tf_op jit(solution)/shard_map/ppermute | solution.py:873
  17.2 0.0 copy-done
  17.2 0.0 copy-done.1
  17.2 0.0 copy-done.4
  17.2 0.0 copy-done.8
  17.2 0.0 copy-done.10
  17.2 0.9 %y_messages.1 = (f32[296,128]{1,0:T(8,128)S(1)}, f32[296,128]{1,0:T(8,128)S(1)}) custom-call(f32[192,512]{1,0:T(8,128)S(1)} %get-tuple-element.38.c2, f32[112,512]{1,0:T(8,128)S(1)} %get-tuple-element.39.c3, f32[16,512]{1,0:T(8,128)S(1)} %get-tuple-element.40.cf, f32[24,512]{1,0:T(8,128)S(1)} %collective-permute-done.1.fl, ...), custom_call_target="tpu_custom_call" | custom-call | flops 1000 | bytes 1000 | tf_op jit(solution)/shard_map/y_messages/pallas_call | solution.py:548
  18.1 3.6 %collective-permute-start.5 = (f32[296,128]{1,0:T(8,128)S(1)}, f32[296,128]{1,0:T(8,128)S(1)}, u32[]{:S(2)}, u32[]{:S(2)}) collective-permute-start(f32[296,128]{1,0:T(8,128)S(1)} %get-tuple-element.41), channel_id=1, source_target_pairs={{1,0},{2,1},{3,2},{0,3},{5,4},{6,5},{7,6},{4,7},{9,8},{10,9},{11,1... | collective-permute-start | bytes 454664 | tf_op jit(solution)/shard_map/ppermute | solution.py:873
  21.7 0.0 collective-permute-start.6
  21.8 0.0 copy-start.19
  21.8 0.0 copy-start.5
  21.8 0.0 copy-start.9
  21.8 0.0 copy-start.11
  21.8 0.0 copy-start.17
  21.9 6.3 %main_part.1 = (f32[4,32,64,128]{3,2,1,0:T(8,128)S(1)}, f32[8,128]{1,0:T(8,128)S(1)}, f32[32,64,512]{2,1,0:T(8,128)}) custom-call(f32[32,64,512]{2,1,0:T(8,128)S(1)} %get-tuple-element.26.x1, f32[16,32,512]{2,1,0:T(8,128)S(1)} %get-tuple-element.29.x2, f32[8,16,512]{2,1,0:T(8,128)S(1)} %get-tuple-element.30.x3, f32[24,512]{1,0:T(8,128)S(1)} %collective-permute-done.1.fl, ...), custom_call_target="tpu_custom_call" | custom-call | flops 1000 | bytes 1000 | tf_op jit(solution)/shard_map/main_part/pallas_call | solution.py:686
  28.2 0.0 collective-permute-done.3.a1
  28.2 0.0 collective-permute-done.4.b1
  28.2 0.7 %early_part.1.w_ref = f32[256,512]{1,0:T(8,128)S(1)} custom-call(f32[128,512]{1,0:T(8,128)S(1)} %collective-permute-done.3.a1, f32[128,512]{1,0:T(8,128)S(1)} %collective-permute-done.4.b1, bf16[2,768,256]{2,1,0:T(8,128)(2,1)S(1)} %copy-done, bf16[2,384,256]{2,1,0:T(8,128)(2,1)S(1)} %copy-done.1, bf16[64,192]{1,0:T(8,128)(2,1)S(1)} %copy-done.19, ...), custom_call_target="tpu_custom_call" | custom-call | flops 1000 | bytes 1000 | tf_op jit(solution)/shard_map/early_part/pallas_call | solution.py:720
  28.9 0.0 collective-permute-done.5.fr
  28.9 0.0 collective-permute-done.6.fl
  29.0 2.3 %z_apply.1 = f32[32,64,512]{2,1,0:T(8,128)} custom-call(f32[4,32,64,128]{3,2,1,0:T(8,128)S(1)} %get-tuple-element.33.in_ref, f32[32,64,512]{2,1,0:T(8,128)} %get-tuple-element.34.base_hbm, f32[256,512]{1,0:T(8,128)S(1)} %early_part.1.w_ref, f32[296,128]{1,0:T(8,128)S(1)} %collective-permute-done.5.fr, ...), custom_call_target="tpu_custom_call", output_to_operand_aliasing={{}: (1, {})} | custom-call | tf_op jit(solution)/shard_map/z_apply/pallas_call | solution.py:842
  (19 shorter events, 0.0 us)
Async XLA Ops:
  0.0 8.4 %copy-start.20 = (bf16[3,8,384]{2,1,0:T(8,128)(2,1)S(1)}, bf16[3,8,384]{2,1,0:T(8,128)(2,1)}, u32[]{:S(2)}) copy-start(bf16[3,8,384]{2,1,0:T(8,128)(2,1)} %constant.56.clone.c_ref) | copy-start | bytes 55300
  0.0 8.5 %copy-start.15 = (bf16[2,112,240]{2,1,0:T(8,128)(2,1)S(1)}, bf16[2,112,240]{2,1,0:T(8,128)(2,1)}, u32[]{:S(2)}) copy-start(bf16[2,112,240]{2,1,0:T(8,128)(2,1)} %constant.55.clone.t_ref) | copy-start | bytes 322564
  3.3 5.2 %collective-permute-start = (f32[384,512]{1,0:T(8,128)S(1)}, f32[384,512]{1,0:T(8,128)S(1)}, u32[]{:S(2)}, u32[]{:S(2)}) collective-permute-start(f32[384,512]{1,0:T(8,128)S(1)} %get-tuple-element.25), channel_id=1, source_target_pairs={{0,16},{16,0},{1,17},{17,1},{2,18},{18,2},{3,19},{19,3},{4,20},{20... | collective-permute-start | bytes 2359304 | tf_op jit(solution)/shard_map/ppermute | solution.py:202
  3.8 24.4 %collective-permute-start.3 = (f32[128,512]{1,0:T(8,128)S(1)}, f32[128,512]{1,0:T(8,128)S(1)}, u32[]{:S(2)}, u32[]{:S(2)}) collective-permute-start(f32[128,512]{1,0:T(8,128)S(1)} %get-tuple-element.35), channel_id=1, source_target_pairs={{1,0},{2,1},{3,2},{0,3},{5,4},{6,5},{7,6},{4,7},{9,8},{10,9},{11,1... | collective-permute-start | bytes 786440 | tf_op jit(solution)/shard_map/ppermute | solution.py:873
  8.4 19.7 %collective-permute-start.4 = (f32[128,512]{1,0:T(8,128)S(1)}, f32[128,512]{1,0:T(8,128)S(1)}, u32[]{:S(2)}, u32[]{:S(2)}) collective-permute-start(f32[128,512]{1,0:T(8,128)S(1)} %get-tuple-element.36), channel_id=1, source_target_pairs={{0,1},{1,2},{2,3},{3,0},{4,5},{5,6},{6,7},{7,4},{8,9},{9,10},{10,1... | collective-permute-start | bytes 786440 | tf_op jit(solution)/shard_map/ppermute | solution.py:873
  8.5 8.7 %copy-start = (bf16[2,768,256]{2,1,0:T(8,128)(2,1)S(1)}, bf16[2,768,256]{2,1,0:T(8,128)(2,1)}, u32[]{:S(2)}) copy-start(bf16[2,768,256]{2,1,0:T(8,128)(2,1)} %constant.48.clone.o1.own1) | copy-start | bytes 2359300
  8.5 8.7 %copy-start.1 = (bf16[2,384,256]{2,1,0:T(8,128)(2,1)S(1)}, bf16[2,384,256]{2,1,0:T(8,128)(2,1)}, u32[]{:S(2)}) copy-start(bf16[2,384,256]{2,1,0:T(8,128)(2,1)} %constant.49.clone.e1.edge1) | copy-start | bytes 1179652
  8.5 8.7 %copy-start.4 = (bf16[1536,256]{1,0:T(8,128)(2,1)S(1)}, bf16[1536,256]{1,0:T(8,128)(2,1)}, u32[]{:S(2)}) copy-start(bf16[1536,256]{1,0:T(8,128)(2,1)} %constant.57.clone.m2) | copy-start | bytes 2359300
  8.5 8.7 %copy-start.8 = (bf16[1536,128]{1,0:T(8,128)(2,1)S(1)}, bf16[1536,128]{1,0:T(8,128)(2,1)}, u32[]{:S(2)}) copy-start(bf16[1536,128]{1,0:T(8,128)(2,1)} %constant.58.clone.m3) | copy-start | bytes 1179652
  8.5 8.7 %copy-start.10 = (bf16[384,256]{1,0:T(8,128)(2,1)S(1)}, bf16[384,256]{1,0:T(8,128)(2,1)}, u32[]{:S(2)}) copy-start(bf16[384,256]{1,0:T(8,128)(2,1)} %constant.59.clone.h2) | copy-start | bytes 589828
  8.5 8.7 %copy-start.14 = (f32[224,128]{1,0:T(8,128)S(1)}, f32[224,128]{1,0:T(8,128)}, u32[]{:S(2)}) copy-start(f32[224,128]{1,0:T(8,128)} %constant.63.clone.k3) | copy-start | bytes 344068
  8.5 8.7 %copy-start.16 = (bf16[384,128]{1,0:T(8,128)(2,1)S(1)}, bf16[384,128]{1,0:T(8,128)(2,1)}, u32[]{:S(2)}) copy-start(bf16[384,128]{1,0:T(8,128)(2,1)} %constant.60.clone.h3) | copy-start | bytes 294916
  8.6 8.7 %copy-start.18 = (f32[96,128]{1,0:T(8,128)S(1)}, f32[96,128]{1,0:T(8,128)}, u32[]{:S(2)}) copy-start(f32[96,128]{1,0:T(8,128)} %constant.62.clone.k2) | copy-start | bytes 147460
  8.6 8.7 %copy-start.21 = (f32[32,128]{1,0:T(8,128)S(1)}, f32[32,128]{1,0:T(8,128)}, u32[]{:S(2)}) copy-start(f32[32,128]{1,0:T(8,128)} %constant.61.clone.k1) | copy-start | bytes 49156
  11.2 10.5 %copy-start.2 = (bf16[2,768,256]{2,1,0:T(8,128)(2,1)S(1)}, bf16[2,768,256]{2,1,0:T(8,128)(2,1)}, u32[]{:S(2)}) copy-start(bf16[2,768,256]{2,1,0:T(8,128)(2,1)} %constant.52.clone.o3) | copy-start | bytes 2359300
  11.2 10.5 %copy-start.3 = (bf16[2,768,256]{2,1,0:T(8,128)(2,1)S(1)}, bf16[2,768,256]{2,1,0:T(8,128)(2,1)}, u32[]{:S(2)}) copy-start(bf16[2,768,256]{2,1,0:T(8,128)(2,1)} %constant.50.clone.o2) | copy-start | bytes 2359300
  11.2 10.5 %copy-start.6 = (bf16[2,384,256]{2,1,0:T(8,128)(2,1)S(1)}, bf16[2,384,256]{2,1,0:T(8,128)(2,1)}, u32[]{:S(2)}) copy-start(bf16[2,384,256]{2,1,0:T(8,128)(2,1)} %constant.53.clone.e3) | copy-start | bytes 1179652
  11.3 10.5 %copy-start.7 = (bf16[2,384,256]{2,1,0:T(8,128)(2,1)S(1)}, bf16[2,384,256]{2,1,0:T(8,128)(2,1)}, u32[]{:S(2)}) copy-start(bf16[2,384,256]{2,1,0:T(8,128)(2,1)} %constant.51.clone.e2) | copy-start | bytes 1179652
  11.3 10.5 %copy-start.12 = (f32[256,128]{1,0:T(8,128)S(1)}, f32[256,128]{1,0:T(8,128)}, u32[]{:S(2)}) copy-start(f32[256,128]{1,0:T(8,128)} %constant.66.clone.k3) | copy-start | bytes 393220
  11.3 10.5 %copy-start.13 = (f32[256,128]{1,0:T(8,128)S(1)}, f32[256,128]{1,0:T(8,128)}, u32[]{:S(2)}) copy-start(f32[256,128]{1,0:T(8,128)} %constant.65.clone.k2) | copy-start | bytes 393220
  11.3 10.5 %copy-start.22 = (f32[8,128]{1,0:T(8,128)S(1)}, f32[8,128]{1,0:T(8,128)}, u32[]{:S(2)}) copy-start(f32[8,128]{1,0:T(8,128)} %constant.64.clone.k1) | copy-start | bytes 12292
  11.3 5.3 %collective-permute-start.1 = (f32[24,512]{1,0:T(8,128)S(1)}, f32[24,512]{1,0:T(8,128)S(1)}, u32[]{:S(2)}, u32[]{:S(2)}) collective-permute-start(f32[24,512]{1,0:T(8,128)S(1)} %get-tuple-element.31), channel_id=1, source_target_pairs={{0,4},{4,8},{8,12},{12,0},{1,5},{5,9},{9,13},{13,1},{2,6},{6,10},{... | collective-permute-start | bytes 147464 | tf_op jit(solution)/shard_map/ppermute | solution.py:873
  12.8 4.3 %collective-permute-start.2 = (f32[24,512]{1,0:T(8,128)S(1)}, f32[24,512]{1,0:T(8,128)S(1)}, u32[]{:S(2)}, u32[]{:S(2)}) collective-permute-start(f32[24,512]{1,0:T(8,128)S(1)} %get-tuple-element.32), channel_id=1, source_target_pairs={{4,0},{8,4},{12,8},{0,12},{5,1},{9,5},{13,9},{1,13},{6,2},{10,6},{... | collective-permute-start | bytes 147464 | tf_op jit(solution)/shard_map/ppermute | solution.py:873
  18.1 10.8 %collective-permute-start.5 = (f32[296,128]{1,0:T(8,128)S(1)}, f32[296,128]{1,0:T(8,128)S(1)}, u32[]{:S(2)}, u32[]{:S(2)}) collective-permute-start(f32[296,128]{1,0:T(8,128)S(1)} %get-tuple-element.41), channel_id=1, source_target_pairs={{1,0},{2,1},{3,2},{0,3},{5,4},{6,5},{7,6},{4,7},{9,8},{10,9},{11,1... | collective-permute-start | bytes 454664 | tf_op jit(solution)/shard_map/ppermute | solution.py:873
  21.7 7.2 %collective-permute-start.6 = (f32[296,128]{1,0:T(8,128)S(1)}, f32[296,128]{1,0:T(8,128)S(1)}, u32[]{:S(2)}, u32[]{:S(2)}) collective-permute-start(f32[296,128]{1,0:T(8,128)S(1)} %get-tuple-element.42), channel_id=1, source_target_pairs={{0,1},{1,2},{2,3},{3,0},{4,5},{5,6},{6,7},{7,4},{8,9},{9,10},{10,1... | collective-permute-start | bytes 454664 | tf_op jit(solution)/shard_map/ppermute | solution.py:873
  21.8 6.4 %copy-start.19 = (bf16[64,192]{1,0:T(8,128)(2,1)S(1)}, bf16[64,192]{1,0:T(8,128)(2,1)}, u32[]{:S(2)}) copy-start(bf16[64,192]{1,0:T(8,128)(2,1)} %constant.67.clone.xt) | copy-start | bytes 73732
  21.8 7.1 %copy-start.5 = (bf16[512,512]{1,0:T(8,128)(2,1)S(1)}, bf16[512,512]{1,0:T(8,128)(2,1)}, u32[]{:S(2)}) copy-start(bf16[512,512]{1,0:T(8,128)(2,1)} %constant.68.clone.t2) | copy-start | bytes 1572868
  21.8 7.1 %copy-start.9 = (bf16[256,512]{1,0:T(8,128)(2,1)S(1)}, bf16[256,512]{1,0:T(8,128)(2,1)}, u32[]{:S(2)}) copy-start(bf16[256,512]{1,0:T(8,128)(2,1)} %constant.69.clone.t3) | copy-start | bytes 786436
  21.8 7.1 %copy-start.11 = (bf16[128,512]{1,0:T(8,128)(2,1)S(1)}, bf16[128,512]{1,0:T(8,128)(2,1)}, u32[]{:S(2)}) copy-start(bf16[128,512]{1,0:T(8,128)(2,1)} %constant.71.clone.yf) | copy-start | bytes 393220
  21.8 7.1 %copy-start.17 = (bf16[256,48]{1,0:T(8,128)(2,1)S(1)}, bf16[256,48]{1,0:T(8,128)(2,1)}, u32[]{:S(2)}) copy-start(bf16[256,48]{1,0:T(8,128)(2,1)} %constant.70.clone.xf) | copy-start | bytes 73732

commit v5 on v4

--- a/solution.py
+++ b/solution.py
@@ -707,7 +707,7 @@
     nx, ny = below.shape[0] // 2, below.shape[1]
     _, _, maps = joint_sides(nx)
 
-    def kernel(a1, b1, o1, e1, xt, after_ref, w_ref):
+    def kernel(b1, a1, o1, e1, xt, after_ref, w_ref):
         del after_ref
         early = []
         for ref in (b1, a1):
@@ -725,7 +725,7 @@
         compiler_params=params(16),
         cost_estimate=SHORT,
         name="early_part",
-    )(above, below, *band, jnp.asarray(stack_lhs(maps[0][0])), after)
+    )(below, above, *band, jnp.asarray(stack_lhs(maps[0][0])), after)
 
 
 def z_apply(inner, partial, early, from_left, from_right):
@@ -752,6 +752,7 @@
 
     def kernel(in_ref, base_hbm, w_ref, fr, fl, t2, t3, xf, yf, out_hbm, s1, s2, s3, buf, sem):
         del base_hbm
+        s2[...] = jnp.zeros(s2.shape, F32)
         s3[...] = jnp.zeros(s3.shape, F32)
         halos = [
             jnp.concatenate([ref[at[2] + 8 * p : at[2] + 8 * p + 8, :] for p in range(groups)], axis=1)
@@ -788,14 +789,12 @@
                 start = c * n
                 for q in range(groups):
                     piece = got[start : start + n, 128 * q : 128 * q + 128]
-                    if level == 1:
-                        to[c, q] = piece
-                    else:
-                        to[c, q, pl.ds(0, n, stride=2), :] = piece
-
-        lanes = lax.broadcasted_iota(jnp.int32, (8, 128), 1)
-        even_lane = lanes % 2 == 0
-        third_cell = (lax.broadcasted_iota(jnp.int32, (8, 128), 0) % 2 + lanes % 4) == 0
+                    to[c, q, pl.ds(0, n, stride=1 << level), :] = piece
+
+        row_ids = lax.broadcasted_iota(jnp.int32, (8, 128), 0)
+        lane_ids = lax.broadcasted_iota(jnp.int32, (8, 128), 1)
+        second_cell = row_ids % 2 + lane_ids % 2 == 0
+        third_cell = row_ids % 4 + lane_ids % 4 == 0
 
         def summed(table_row, get):
             total = None
@@ -807,35 +806,24 @@
         copies = []
         for slot, z in enumerate(touched):
 
-            for t in range(nx // 16):
-                full, half = 16 * t, 8 * t
+            for row in range(0, nx, 8):
+                rows = slice(row, row + 8)
                 for q in range(groups):
-                    if z % 2:
-                        for more in (0, 8):
-                            rows = pl.ds(full + more, 8)
-                            extra = summed(maps[0][z], lambda c: s1[c, q, rows, :])
-                            buf[slot, q, rows, :] = add(in_ref[q, z, rows, :], extra)
-                        continue
-                    evens = pl.ds(16 * t, 8, stride=2)
-                    odds = pl.ds(16 * t + 1, 8, stride=2)
-                    extra = summed(maps[0][z], lambda c: s1[c, q, odds, :])
-                    buf[slot, q, odds, :] = add(in_ref[q, z, odds, :], extra)
-                    rows = pl.ds(half, 8)
-                    extra = summed(maps[1][z // 2], lambda c: s2[c, q, rows, :])
-                    if z % 4 == 0:
-                        third = summed(maps[2][z // 4], lambda c: s3[c, q, rows, :])
-                        third = 0.0 if third is None else third
-                        extra = jnp.where(third_cell, third, 0.0 if extra is None else extra)
-                    one = summed(maps[0][z], lambda c: s1[c, q, evens, :])
-                    if one is not None:
-                        extra = jnp.where(even_lane, 0.0 if extra is None else extra, one)
-                    buf[slot, q, evens, :] = add(in_ref[q, z, evens, :], extra)
-            for q in range(groups):
-                copy = pltpu.make_async_copy(
-                    buf.at[slot, q], out_hbm.at[z, :, 128 * q : 128 * q + 128], sem.at[slot]
-                )
-                copy.start()
-                copies.append(copy)
+                    extra = summed(maps[0][z], lambda c: s1[c, q, rows, :])
+                    if z % 2 == 0:
+                        inner = summed(maps[1][z // 2], lambda c: s2[c, q, rows, :])
+                        if z % 4 == 0:
+                            third = summed(maps[2][z // 4], lambda c: s3[c, q, rows, :])
+                            if third is not None:
+                                inner = jnp.where(third_cell, third, 0.0 if inner is None else inner)
+                        if extra is None:
+                            extra = inner
+                        else:
+                            extra = jnp.where(second_cell, 0.0 if inner is None else inner, extra)
+                    buf[slot, rows, 128 * q : 128 * q + 128] = add(in_ref[q, z, rows, :], extra)
+            copy = pltpu.make_async_copy(buf.at[slot], out_hbm.at[z], sem.at[slot])
+            copy.start()
+            copies.append(copy)
         for copy in copies:
             copy.wait()
 
@@ -847,9 +835,9 @@
         input_output_aliases={1: 0},
         scratch_shapes=[
             pltpu.VMEM((4, groups, nx, 128), F32),
-            pltpu.VMEM((maps[1].shape[1], groups, nx // 2, 128), F32),
-            pltpu.VMEM((maps[2].shape[1], groups, nx // 2, 128), F32),
-            pltpu.VMEM((len(touched), groups, nx, 128), F32),
+            pltpu.VMEM((maps[1].shape[1], groups, nx, 128), F32),
+            pltpu.VMEM((maps[2].shape[1], groups, nx, 128), F32),
+            pltpu.VMEM((len(touched), nx, ny), F32),
             pltpu.SemaphoreType.DMA((len(touched),)),
         ],
         compiler_params=params(24),

time: 31.4 us -> 30.6 us (0.975)
  starting transfers between devices: 11.8 us -> 10.5 us
  Pallas kernels: 18.4 us -> 19 us
    ppermute x3, starting transfers between devices: 9.72 us -> 5.62 us  [swap(): lax.ppermute(to_left, axis, left)]
    ppermute x3, starting transfers between devices: 1.55 us -> 4.32 us  [swap(): lax.ppermute(to_right, axis, right)]
    pallas_call x1, Pallas kernels: 2.31 us -> 2.92 us  [z_apply(): pl.pallas_call(kernel, in_specs=[VM, HB] + [VM] * 7, out_specs=HB, out_sh...]
  transfers between devices with their start and end apart: 7 -> 7, of which waited for: 1 -> 1; matrix products, arithmetic and copies ran while one was open for 0% -> 0% of each run, Pallas kernels for 41% -> 42%
where the time goes in v5:
time: 30.6 us; the launch traced here: 30.5 us
  Pallas kernels  19 us (62%)
  starting transfers between devices  10.5 us (34%)
  waiting for transfers between devices  0.47 us (2%)
  between operations  0.36 us (1%)
    pallas_call x1, Pallas kernels, main_part(): pl.pallas_call(kernel, in_specs=[VM] * 14, out_specs=[VM, VM, HB], out_sh...  6.31 us
    ppermute x3, starting transfers between devices, swap(): lax.ppermute(to_left, axis, left)  5.62 us
    ppermute x3, starting transfers between devices, swap(): lax.ppermute(to_right, axis, right)  4.32 us
    pallas_call x1, Pallas kernels, x_send(): pl.pallas_call(kernel, in_specs=[HB, HB], out_specs=[VM] * 4, out_shape=[...  3.25 us
    pallas_call x1, Pallas kernels, z_apply(): pl.pallas_call(kernel, in_specs=[VM, HB] + [VM] * 7, out_specs=HB, out_sh...  2.92 us
    pallas_call x1, Pallas kernels, x_apply(): pl.pallas_call(kernel, grid=(steps,), in_specs=[VM] * 4, out_specs=[VM] *...  2.64 us
    pallas_call x1, Pallas kernels, z_first(): pl.pallas_call(kernel, in_specs=[VM] * 3, out_specs=[VM] * 5, out_shape=[...  2.35 us
    pallas_call x1, Pallas kernels, y_messages(): pl.pallas_call(kernel, in_specs=[VM] * 14, out_specs=[VM] * 2, out_shape=...  0.86 us
  transfers between devices with their start and end apart: 7, of which 1 were waited for; matrix products, arithmetic and copies ran while one was open for 0% of the time, Pallas kernels for 42%

profile of v5, /device:TPU:0, one launch (start us, length us, event | category | flops | bytes accessed | tf_op | source)
XLA Modules:
  0.0 30.5 jit_solution(2580896393761299864)
XLA Ops:
  0.0 3.2 %x_send.1 = (f32[32,64,512]{2,1,0:T(8,128)S(1)}, f32[384,512]{1,0:T(8,128)S(1)}, f32[128,512]{1,0:T(8,128)S(1)}, f32[128,512]{1,0:T(8,128)S(1)}) custom-call(f32[32,64,512]{2,1,0:T(8,128)} %u_hbm.1, bf16[96,256]{1,0:T(8,128)(2,1)} %constant.54.clone.c_hbm), custom_call_target="tpu_custom_call" | custom-call | flops 1000 | bytes 1000 | tf_op jit(solution)/shard_map/x_send/pallas_call | solution.py:182
  3.3 0.5 %collective-permute-start = (f32[384,512]{1,0:T(8,128)S(1)}, f32[384,512]{1,0:T(8,128)S(1)}, u32[]{:S(2)}, u32[]{:S(2)}) collective-permute-start(f32[384,512]{1,0:T(8,128)S(1)} %get-tuple-element.25), channel_id=1, source_target_pairs={{0,16},{16,0},{1,17},{17,1},{2,18},{18,2},{3,19},{19,3},{4,20},{20... | collective-permute-start | bytes 2359304 | tf_op jit(solution)/shard_map/ppermute | solution.py:202
  3.8 2.6 %collective-permute-start.3 = (f32[128,512]{1,0:T(8,128)S(1)}, f32[128,512]{1,0:T(8,128)S(1)}, u32[]{:S(2)}, u32[]{:S(2)}) collective-permute-start(f32[128,512]{1,0:T(8,128)S(1)} %get-tuple-element.35), channel_id=1, source_target_pairs={{0,1},{1,2},{2,3},{3,0},{4,5},{5,6},{6,7},{7,4},{8,9},{9,10},{10,1... | collective-permute-start | bytes 786440 | tf_op jit(solution)/shard_map/ppermute | solution.py:861
  6.4 2.1 %collective-permute-start.4 = (f32[128,512]{1,0:T(8,128)S(1)}, f32[128,512]{1,0:T(8,128)S(1)}, u32[]{:S(2)}, u32[]{:S(2)}) collective-permute-start(f32[128,512]{1,0:T(8,128)S(1)} %get-tuple-element.36), channel_id=1, source_target_pairs={{1,0},{2,1},{3,2},{0,3},{5,4},{6,5},{7,6},{4,7},{9,8},{10,9},{11,1... | collective-permute-start | bytes 786440 | tf_op jit(solution)/shard_map/ppermute | solution.py:861
  8.5 0.0 collective-permute-done.r_ref
  8.5 0.0 copy-done.20
  8.5 0.0 copy-start
  8.6 0.0 copy-start.1
  8.6 0.0 copy-start.4
  8.6 0.0 copy-start.8
  8.6 0.0 copy-start.10
  8.6 0.0 copy-start.14
  8.6 0.0 copy-start.16
  8.6 0.0 copy-start.18
  8.6 0.0 copy-start.21
  8.7 2.6 %x_apply.1 = (f32[32,64,512]{2,1,0:T(8,128)S(1)}, f32[32,32,512]{2,1,0:T(8,128)S(1)}, f32[32,16,512]{2,1,0:T(8,128)S(1)}, f32[24,512]{1,0:T(8,128)S(1)}, f32[24,512]{1,0:T(8,128)S(1)}) custom-call(f32[32,64,512]{2,1,0:T(8,128)S(1)} %get-tuple-element.24.u_ref, f32[384,512]{1,0:T(8,128)S(1)} %collective-permute-done.r_ref, ...), custom_call_target="tpu_custom_call" | custom-call | flops 1000 | bytes 1000 | tf_op jit(solution)/shard_map/x_apply/pallas_call | solution.py:272
  11.3 0.0 copy-start.3
  11.3 0.0 copy-start.6
  11.3 0.0 copy-start.7
  11.3 0.0 copy-start.12
  11.4 0.0 copy-start.13
  11.4 0.0 copy-start.22
  11.4 1.7 %collective-permute-start.1 = (f32[24,512]{1,0:T(8,128)S(1)}, f32[24,512]{1,0:T(8,128)S(1)}, u32[]{:S(2)}, u32[]{:S(2)}) collective-permute-start(f32[24,512]{1,0:T(8,128)S(1)} %get-tuple-element.31), channel_id=1, source_target_pairs={{0,4},{4,8},{8,12},{12,0},{1,5},{5,9},{9,13},{13,1},{2,6},{6,10},{... | collective-permute-start | bytes 147464 | tf_op jit(solution)/shard_map/ppermute | solution.py:861
  13.1 1.3 %collective-permute-start.2 = (f32[24,512]{1,0:T(8,128)S(1)}, f32[24,512]{1,0:T(8,128)S(1)}, u32[]{:S(2)}, u32[]{:S(2)}) collective-permute-start(f32[24,512]{1,0:T(8,128)S(1)} %get-tuple-element.32), channel_id=1, source_target_pairs={{4,0},{8,4},{12,8},{0,12},{5,1},{9,5},{13,9},{1,13},{6,2},{10,6},{... | collective-permute-start | bytes 147464 | tf_op jit(solution)/shard_map/ppermute | solution.py:861
  14.4 2.4 %z_first.1 = (f32[192,512]{1,0:T(8,128)S(1)}, f32[112,512]{1,0:T(8,128)S(1)}, f32[16,512]{1,0:T(8,128)S(1)}, f32[16,32,512]{2,1,0:T(8,128)S(1)}, f32[8,16,512]{2,1,0:T(8,128)S(1)}) custom-call(f32[32,32,512]{2,1,0:T(8,128)S(1)} %get-tuple-element.27.x2, f32[32,16,512]{2,1,0:T(8,128)S(1)} %get-tuple-element.28.x3, f32[384,512]{1,0:T(8,128)S(1)} %collective-permute-done.r_ref), custom_call_target="tpu_custom_call" | custom-call | flops 1000 | bytes 1000 | tf_op jit(solution)/shard_map/z_first/pallas_call | solution.py:375
  16.7 0.0 collective-permute-done.1.fl
  16.7 0.4 %collective-permute-done.2.fr = f32[24,512]{1,0:T(8,128)S(1)} collective-permute-done((f32[24,512]{1,0:T(8,128)S(1)}, f32[24,512]{1,0:T(8,128)S(1)}, u32[]{:S(2)}, u32[]{:S(2)}) %collective-permute-start.2) | collective-permute-done | bytes 49184 | tf_op jit(solution)/shard_map/ppermute | solution.py:861
  17.2 0.0 copy-done
  17.2 0.9 %y_messages.1 = (f32[296,128]{1,0:T(8,128)S(1)}, f32[296,128]{1,0:T(8,128)S(1)}) custom-call(f32[192,512]{1,0:T(8,128)S(1)} %get-tuple-element.38.c2, f32[112,512]{1,0:T(8,128)S(1)} %get-tuple-element.39.c3, f32[16,512]{1,0:T(8,128)S(1)} %get-tuple-element.40.cf, f32[24,512]{1,0:T(8,128)S(1)} %collective-permute-done.1.fl, ...), custom_call_target="tpu_custom_call" | custom-call | flops 1000 | bytes 1000 | tf_op jit(solution)/shard_map/y_messages/pallas_call | solution.py:548
  18.1 2.2 %collective-permute-start.5 = (f32[296,128]{1,0:T(8,128)S(1)}, f32[296,128]{1,0:T(8,128)S(1)}, u32[]{:S(2)}, u32[]{:S(2)}) collective-permute-start(f32[296,128]{1,0:T(8,128)S(1)} %get-tuple-element.41), channel_id=1, source_target_pairs={{1,0},{2,1},{3,2},{0,3},{5,4},{6,5},{7,6},{4,7},{9,8},{10,9},{11,1... | collective-permute-start | bytes 454664 | tf_op jit(solution)/shard_map/ppermute | solution.py:861
  20.3 0.0 collective-permute-start.6
  20.3 0.0 copy-done.6
  20.3 0.0 copy-done.7
  20.3 0.0 copy-done.12
  20.4 0.0 copy-done.13
  20.4 0.0 copy-done.22
  20.4 0.0 copy-start.19
  20.4 0.0 copy-start.5
  20.4 0.0 copy-start.9
  20.4 0.0 copy-start.11
  20.4 0.0 copy-start.17
  20.4 6.3 %main_part.1 = (f32[4,32,64,128]{3,2,1,0:T(8,128)S(1)}, f32[8,128]{1,0:T(8,128)S(1)}, f32[32,64,512]{2,1,0:T(8,128)}) custom-call(f32[32,64,512]{2,1,0:T(8,128)S(1)} %get-tuple-element.26.x1, f32[16,32,512]{2,1,0:T(8,128)S(1)} %get-tuple-element.29.x2, f32[8,16,512]{2,1,0:T(8,128)S(1)} %get-tuple-element.30.x3, f32[24,512]{1,0:T(8,128)S(1)} %collective-permute-done.1.fl, ...), custom_call_target="tpu_custom_call" | custom-call | flops 1000 | bytes 1000 | tf_op jit(solution)/shard_map/main_part/pallas_call | solution.py:686
  26.8 0.0 collective-permute-done.3.b1
  26.8 0.0 collective-permute-done.4.a1
  26.8 0.7 %early_part.1.w_ref = f32[256,512]{1,0:T(8,128)S(1)} custom-call(f32[128,512]{1,0:T(8,128)S(1)} %collective-permute-done.3.b1, f32[128,512]{1,0:T(8,128)S(1)} %collective-permute-done.4.a1, bf16[2,768,256]{2,1,0:T(8,128)(2,1)S(1)} %copy-done, bf16[2,384,256]{2,1,0:T(8,128)(2,1)S(1)} %copy-done.1, bf16[64,192]{1,0:T(8,128)(2,1)S(1)} %copy-done.19, ...), custom_call_target="tpu_custom_call" | custom-call | flops 1000 | bytes 1000 | tf_op jit(solution)/shard_map/early_part/pallas_call | solution.py:720
  27.5 0.0 collective-permute-done.5.fr
  27.5 0.0 collective-permute-done.6.fl
  27.5 2.9 %z_apply.1 = f32[32,64,512]{2,1,0:T(8,128)} custom-call(f32[4,32,64,128]{3,2,1,0:T(8,128)S(1)} %get-tuple-element.33.in_ref, f32[32,64,512]{2,1,0:T(8,128)} %get-tuple-element.34.base_hbm, f32[256,512]{1,0:T(8,128)S(1)} %early_part.1.w_ref, f32[296,128]{1,0:T(8,128)S(1)} %collective-permute-done.5.fr, ...), custom_call_target="tpu_custom_call", output_to_operand_aliasing={{}: (1, {})} | custom-call | tf_op jit(solution)/shard_map/z_apply/pallas_call | solution.py:830
  (19 shorter events, 0.0 us)
Async XLA Ops:
  0.0 8.5 %copy-start.20 = (bf16[3,8,384]{2,1,0:T(8,128)(2,1)S(1)}, bf16[3,8,384]{2,1,0:T(8,128)(2,1)}, u32[]{:S(2)}) copy-start(bf16[3,8,384]{2,1,0:T(8,128)(2,1)} %constant.56.clone.c_ref) | copy-start | bytes 55300
  0.0 8.5 %copy-start.15 = (bf16[2,112,240]{2,1,0:T(8,128)(2,1)S(1)}, bf16[2,112,240]{2,1,0:T(8,128)(2,1)}, u32[]{:S(2)}) copy-start(bf16[2,112,240]{2,1,0:T(8,128)(2,1)} %constant.55.clone.t_ref) | copy-start | bytes 322564
  3.3 5.3 %collective-permute-start = (f32[384,512]{1,0:T(8,128)S(1)}, f32[384,512]{1,0:T(8,128)S(1)}, u32[]{:S(2)}, u32[]{:S(2)}) collective-permute-start(f32[384,512]{1,0:T(8,128)S(1)} %get-tuple-element.25), channel_id=1, source_target_pairs={{0,16},{16,0},{1,17},{17,1},{2,18},{18,2},{3,19},{19,3},{4,20},{20... | collective-permute-start | bytes 2359304 | tf_op jit(solution)/shard_map/ppermute | solution.py:202
  3.8 23.0 %collective-permute-start.3 = (f32[128,512]{1,0:T(8,128)S(1)}, f32[128,512]{1,0:T(8,128)S(1)}, u32[]{:S(2)}, u32[]{:S(2)}) collective-permute-start(f32[128,512]{1,0:T(8,128)S(1)} %get-tuple-element.35), channel_id=1, source_target_pairs={{0,1},{1,2},{2,3},{3,0},{4,5},{5,6},{6,7},{7,4},{8,9},{9,10},{10,1... | collective-permute-start | bytes 786440 | tf_op jit(solution)/shard_map/ppermute | solution.py:861
  6.4 20.4 %collective-permute-start.4 = (f32[128,512]{1,0:T(8,128)S(1)}, f32[128,512]{1,0:T(8,128)S(1)}, u32[]{:S(2)}, u32[]{:S(2)}) collective-permute-start(f32[128,512]{1,0:T(8,128)S(1)} %get-tuple-element.36), channel_id=1, source_target_pairs={{1,0},{2,1},{3,2},{0,3},{5,4},{6,5},{7,6},{4,7},{9,8},{10,9},{11,1... | collective-permute-start | bytes 786440 | tf_op jit(solution)/shard_map/ppermute | solution.py:861
  8.5 8.6 %copy-start = (bf16[2,768,256]{2,1,0:T(8,128)(2,1)S(1)}, bf16[2,768,256]{2,1,0:T(8,128)(2,1)}, u32[]{:S(2)}) copy-start(bf16[2,768,256]{2,1,0:T(8,128)(2,1)} %constant.48.clone.o1.own1) | copy-start | bytes 2359300
  8.6 8.6 %copy-start.1 = (bf16[2,384,256]{2,1,0:T(8,128)(2,1)S(1)}, bf16[2,384,256]{2,1,0:T(8,128)(2,1)}, u32[]{:S(2)}) copy-start(bf16[2,384,256]{2,1,0:T(8,128)(2,1)} %constant.49.clone.e1.edge1) | copy-start | bytes 1179652
  8.6 8.6 %copy-start.4 = (bf16[1536,256]{1,0:T(8,128)(2,1)S(1)}, bf16[1536,256]{1,0:T(8,128)(2,1)}, u32[]{:S(2)}) copy-start(bf16[1536,256]{1,0:T(8,128)(2,1)} %constant.57.clone.m2) | copy-start | bytes 2359300
  8.6 8.6 %copy-start.8 = (bf16[1536,128]{1,0:T(8,128)(2,1)S(1)}, bf16[1536,128]{1,0:T(8,128)(2,1)}, u32[]{:S(2)}) copy-start(bf16[1536,128]{1,0:T(8,128)(2,1)} %constant.58.clone.m3) | copy-start | bytes 1179652
  8.6 8.6 %copy-start.10 = (bf16[384,256]{1,0:T(8,128)(2,1)S(1)}, bf16[384,256]{1,0:T(8,128)(2,1)}, u32[]{:S(2)}) copy-start(bf16[384,256]{1,0:T(8,128)(2,1)} %constant.59.clone.h2) | copy-start | bytes 589828
  8.6 8.6 %copy-start.14 = (f32[224,128]{1,0:T(8,128)S(1)}, f32[224,128]{1,0:T(8,128)}, u32[]{:S(2)}) copy-start(f32[224,128]{1,0:T(8,128)} %constant.63.clone.k3) | copy-start | bytes 344068
  8.6 8.6 %copy-start.16 = (bf16[384,128]{1,0:T(8,128)(2,1)S(1)}, bf16[384,128]{1,0:T(8,128)(2,1)}, u32[]{:S(2)}) copy-start(bf16[384,128]{1,0:T(8,128)(2,1)} %constant.60.clone.h3) | copy-start | bytes 294916
  8.6 8.6 %copy-start.18 = (f32[96,128]{1,0:T(8,128)S(1)}, f32[96,128]{1,0:T(8,128)}, u32[]{:S(2)}) copy-start(f32[96,128]{1,0:T(8,128)} %constant.62.clone.k2) | copy-start | bytes 147460
  8.6 8.6 %copy-start.21 = (f32[32,128]{1,0:T(8,128)S(1)}, f32[32,128]{1,0:T(8,128)}, u32[]{:S(2)}) copy-start(f32[32,128]{1,0:T(8,128)} %constant.61.clone.k1) | copy-start | bytes 49156
  11.3 9.0 %copy-start.2 = (bf16[2,768,256]{2,1,0:T(8,128)(2,1)S(1)}, bf16[2,768,256]{2,1,0:T(8,128)(2,1)}, u32[]{:S(2)}) copy-start(bf16[2,768,256]{2,1,0:T(8,128)(2,1)} %constant.52.clone.o3) | copy-start | bytes 2359300
  11.3 9.0 %copy-start.3 = (bf16[2,768,256]{2,1,0:T(8,128)(2,1)S(1)}, bf16[2,768,256]{2,1,0:T(8,128)(2,1)}, u32[]{:S(2)}) copy-start(bf16[2,768,256]{2,1,0:T(8,128)(2,1)} %constant.50.clone.o2) | copy-start | bytes 2359300
  11.3 9.0 %copy-start.6 = (bf16[2,384,256]{2,1,0:T(8,128)(2,1)S(1)}, bf16[2,384,256]{2,1,0:T(8,128)(2,1)}, u32[]{:S(2)}) copy-start(bf16[2,384,256]{2,1,0:T(8,128)(2,1)} %constant.53.clone.e3) | copy-start | bytes 1179652
  11.3 9.0 %copy-start.7 = (bf16[2,384,256]{2,1,0:T(8,128)(2,1)S(1)}, bf16[2,384,256]{2,1,0:T(8,128)(2,1)}, u32[]{:S(2)}) copy-start(bf16[2,384,256]{2,1,0:T(8,128)(2,1)} %constant.51.clone.e2) | copy-start | bytes 1179652
  11.3 9.0 %copy-start.12 = (f32[256,128]{1,0:T(8,128)S(1)}, f32[256,128]{1,0:T(8,128)}, u32[]{:S(2)}) copy-start(f32[256,128]{1,0:T(8,128)} %constant.66.clone.k3) | copy-start | bytes 393220
  11.4 9.0 %copy-start.13 = (f32[256,128]{1,0:T(8,128)S(1)}, f32[256,128]{1,0:T(8,128)}, u32[]{:S(2)}) copy-start(f32[256,128]{1,0:T(8,128)} %constant.65.clone.k2) | copy-start | bytes 393220
  11.4 9.0 %copy-start.22 = (f32[8,128]{1,0:T(8,128)S(1)}, f32[8,128]{1,0:T(8,128)}, u32[]{:S(2)}) copy-start(f32[8,128]{1,0:T(8,128)} %constant.64.clone.k1) | copy-start | bytes 12292
  11.4 5.3 %collective-permute-start.1 = (f32[24,512]{1,0:T(8,128)S(1)}, f32[24,512]{1,0:T(8,128)S(1)}, u32[]{:S(2)}, u32[]{:S(2)}) collective-permute-start(f32[24,512]{1,0:T(8,128)S(1)} %get-tuple-element.31), channel_id=1, source_target_pairs={{0,4},{4,8},{8,12},{12,0},{1,5},{5,9},{9,13},{13,1},{2,6},{6,10},{... | collective-permute-start | bytes 147464 | tf_op jit(solution)/shard_map/ppermute | solution.py:861
  13.1 4.1 %collective-permute-start.2 = (f32[24,512]{1,0:T(8,128)S(1)}, f32[24,512]{1,0:T(8,128)S(1)}, u32[]{:S(2)}, u32[]{:S(2)}) collective-permute-start(f32[24,512]{1,0:T(8,128)S(1)} %get-tuple-element.32), channel_id=1, source_target_pairs={{4,0},{8,4},{12,8},{0,12},{5,1},{9,5},{13,9},{1,13},{6,2},{10,6},{... | collective-permute-start | bytes 147464 | tf_op jit(solution)/shard_map/ppermute | solution.py:861
  18.1 9.4 %collective-permute-start.5 = (f32[296,128]{1,0:T(8,128)S(1)}, f32[296,128]{1,0:T(8,128)S(1)}, u32[]{:S(2)}, u32[]{:S(2)}) collective-permute-start(f32[296,128]{1,0:T(8,128)S(1)} %get-tuple-element.41), channel_id=1, source_target_pairs={{1,0},{2,1},{3,2},{0,3},{5,4},{6,5},{7,6},{4,7},{9,8},{10,9},{11,1... | collective-permute-start | bytes 454664 | tf_op jit(solution)/shard_map/ppermute | solution.py:861
  20.3 7.2 %collective-permute-start.6 = (f32[296,128]{1,0:T(8,128)S(1)}, f32[296,128]{1,0:T(8,128)S(1)}, u32[]{:S(2)}, u32[]{:S(2)}) collective-permute-start(f32[296,128]{1,0:T(8,128)S(1)} %get-tuple-element.42), channel_id=1, source_target_pairs={{0,1},{1,2},{2,3},{3,0},{4,5},{5,6},{6,7},{7,4},{8,9},{9,10},{10,1... | collective-permute-start | bytes 454664 | tf_op jit(solution)/shard_map/ppermute | solution.py:861
  20.4 6.4 %copy-start.19 = (bf16[64,192]{1,0:T(8,128)(2,1)S(1)}, bf16[64,192]{1,0:T(8,128)(2,1)}, u32[]{:S(2)}) copy-start(bf16[64,192]{1,0:T(8,128)(2,1)} %constant.67.clone.xt) | copy-start | bytes 73732
  20.4 7.1 %copy-start.5 = (bf16[512,512]{1,0:T(8,128)(2,1)S(1)}, bf16[512,512]{1,0:T(8,128)(2,1)}, u32[]{:S(2)}) copy-start(bf16[512,512]{1,0:T(8,128)(2,1)} %constant.68.clone.t2) | copy-start | bytes 1572868
  20.4 7.1 %copy-start.9 = (bf16[256,512]{1,0:T(8,128)(2,1)S(1)}, bf16[256,512]{1,0:T(8,128)(2,1)}, u32[]{:S(2)}) copy-start(bf16[256,512]{1,0:T(8,128)(2,1)} %constant.69.clone.t3) | copy-start | bytes 786436
  20.4 7.1 %copy-start.11 = (bf16[128,512]{1,0:T(8,128)(2,1)S(1)}, bf16[128,512]{1,0:T(8,128)(2,1)}, u32[]{:S(2)}) copy-start(bf16[128,512]{1,0:T(8,128)(2,1)} %constant.71.clone.yf) | copy-start | bytes 393220
  20.4 7.1 %copy-start.17 = (bf16[256,48]{1,0:T(8,128)(2,1)S(1)}, bf16[256,48]{1,0:T(8,128)(2,1)}, u32[]{:S(2)}) copy-start(bf16[256,48]{1,0:T(8,128)(2,1)} %constant.70.clone.xf) | copy-start | bytes 73732

commit v6 on v4

--- a/solution.py
+++ b/solution.py
@@ -707,7 +707,7 @@
     nx, ny = below.shape[0] // 2, below.shape[1]
     _, _, maps = joint_sides(nx)
 
-    def kernel(a1, b1, o1, e1, xt, after_ref, w_ref):
+    def kernel(b1, a1, o1, e1, xt, after_ref, w_ref):
         del after_ref
         early = []
         for ref in (b1, a1):
@@ -725,7 +725,7 @@
         compiler_params=params(16),
         cost_estimate=SHORT,
         name="early_part",
-    )(above, below, *band, jnp.asarray(stack_lhs(maps[0][0])), after)
+    )(below, above, *band, jnp.asarray(stack_lhs(maps[0][0])), after)
 
 
 def z_apply(inner, partial, early, from_left, from_right):
@@ -750,7 +750,7 @@
     side_rows = np.concatenate([side_hi, side_hi, side_lo, np.zeros((104, ny), side_hi.dtype)])
     touched = sorted(touched_layers(nz), key=lambda z: np.abs(maps[0][z]).max() > 1e-12)
 
-    def kernel(in_ref, base_hbm, w_ref, fr, fl, t2, t3, xf, yf, out_hbm, s1, s2, s3, buf, sem):
+    def kernel(in_ref, base_hbm, w_ref, fr, fl, t2, t3, xf, yf, io_ref, out_hbm, s1, s2, s3, sem):
         del base_hbm
         s3[...] = jnp.zeros(s3.shape, F32)
         halos = [
@@ -814,12 +814,13 @@
                         for more in (0, 8):
                             rows = pl.ds(full + more, 8)
                             extra = summed(maps[0][z], lambda c: s1[c, q, rows, :])
-                            buf[slot, q, rows, :] = add(in_ref[q, z, rows, :], extra)
+                            io_ref[q, z, rows, :] = add(in_ref[q, z, rows, :], extra)
                         continue
                     evens = pl.ds(16 * t, 8, stride=2)
                     odds = pl.ds(16 * t + 1, 8, stride=2)
                     extra = summed(maps[0][z], lambda c: s1[c, q, odds, :])
-                    buf[slot, q, odds, :] = add(in_ref[q, z, odds, :], extra)
+                    if extra is not None:
+                        io_ref[q, z, odds, :] = add(in_ref[q, z, odds, :], extra)
                     rows = pl.ds(half, 8)
                     extra = summed(maps[1][z // 2], lambda c: s2[c, q, rows, :])
                     if z % 4 == 0:
@@ -829,10 +830,10 @@
                     one = summed(maps[0][z], lambda c: s1[c, q, evens, :])
                     if one is not None:
                         extra = jnp.where(even_lane, 0.0 if extra is None else extra, one)
-                    buf[slot, q, evens, :] = add(in_ref[q, z, evens, :], extra)
+                    io_ref[q, z, evens, :] = add(in_ref[q, z, evens, :], extra)
             for q in range(groups):
                 copy = pltpu.make_async_copy(
-                    buf.at[slot, q], out_hbm.at[z, :, 128 * q : 128 * q + 128], sem.at[slot]
+                    io_ref.at[q, z], out_hbm.at[z, :, 128 * q : 128 * q + 128], sem.at[slot]
                 )
                 copy.start()
                 copies.append(copy)
@@ -842,14 +843,13 @@
     return pl.pallas_call(
         kernel,
         in_specs=[VM, HB] + [VM] * 7,
-        out_specs=HB,
-        out_shape=jax.ShapeDtypeStruct((nz, nx, ny), F32),
-        input_output_aliases={1: 0},
+        out_specs=[VM, HB],
+        out_shape=[vmem(inner.shape), jax.ShapeDtypeStruct((nz, nx, ny), F32)],
+        input_output_aliases={0: 0, 1: 1},
         scratch_shapes=[
             pltpu.VMEM((4, groups, nx, 128), F32),
             pltpu.VMEM((maps[1].shape[1], groups, nx // 2, 128), F32),
             pltpu.VMEM((maps[2].shape[1], groups, nx // 2, 128), F32),
-            pltpu.VMEM((len(touched), groups, nx, 128), F32),
             pltpu.SemaphoreType.DMA((len(touched),)),
         ],
         compiler_params=params(24),
@@ -887,7 +887,7 @@
     late_below, late_above = swap(up, down, "gz")
     inner, done, partial = main_part((x1, own2, own3), from_left, from_right, bands)
     early = early_part(below, above, bands[0], done)
-    return z_apply(inner, partial, early, late_below, late_above)
+    return z_apply(inner, partial, early, late_below, late_above)[1]
 
 
 def solution(mesh):

time: 31.4 us -> 30 us (0.955)
  starting transfers between devices: 11.8 us -> 10.5 us
    ppermute x3, starting transfers between devices: 9.72 us -> 5.62 us  [swap(): lax.ppermute(to_left, axis, left)]
    ppermute x3, starting transfers between devices: 1.55 us -> 4.32 us  [swap(): lax.ppermute(to_right, axis, right)]
  transfers between devices with their start and end apart: 7 -> 7, of which waited for: 1 -> 1; matrix products, arithmetic and copies ran while one was open for 0% -> 0% of each run, Pallas kernels for 41% -> 43%
where the time goes in v6:
time: 30 us; the launch traced here: 29.8 us
  Pallas kernels  18.4 us (61%)
  starting transfers between devices  10.5 us (35%)
  waiting for transfers between devices  0.46 us (2%)
  between operations  0.37 us (1%)
    pallas_call x1, Pallas kernels, main_part(): pl.pallas_call(kernel, in_specs=[VM] * 14, out_specs=[VM, VM, HB], out_sh...  6.34 us
    ppermute x3, starting transfers between devices, swap(): lax.ppermute(to_left, axis, left)  5.62 us
    ppermute x3, starting transfers between devices, swap(): lax.ppermute(to_right, axis, right)  4.32 us
    pallas_call x1, Pallas kernels, x_send(): pl.pallas_call(kernel, in_specs=[HB, HB], out_specs=[VM] * 4, out_shape=[...  3.25 us
    pallas_call x1, Pallas kernels, x_apply(): pl.pallas_call(kernel, grid=(steps,), in_specs=[VM] * 4, out_specs=[VM] *...  2.64 us
    pallas_call x1, Pallas kernels, z_first(): pl.pallas_call(kernel, in_specs=[VM] * 3, out_specs=[VM] * 5, out_shape=[...  2.35 us
    pallas_call x1, Pallas kernels, z_apply(): pl.pallas_call(kernel, in_specs=[VM, HB] + [VM] * 7, out_specs=[VM, HB],...  2.27 us
    pallas_call x1, Pallas kernels, y_messages(): pl.pallas_call(kernel, in_specs=[VM] * 14, out_specs=[VM] * 2, out_shape=...  0.86 us
  transfers between devices with their start and end apart: 7, of which 1 were waited for; matrix products, arithmetic and copies ran while one was open for 0% of the time, Pallas kernels for 43%

profile of v6, /device:TPU:0, one launch (start us, length us, event | category | flops | bytes accessed | tf_op | source)
XLA Modules:
  0.0 29.8 jit_solution(10601270090718287724)
XLA Ops:
  0.0 3.2 %x_send.1 = (f32[32,64,512]{2,1,0:T(8,128)S(1)}, f32[384,512]{1,0:T(8,128)S(1)}, f32[128,512]{1,0:T(8,128)S(1)}, f32[128,512]{1,0:T(8,128)S(1)}) custom-call(f32[32,64,512]{2,1,0:T(8,128)} %u_hbm.1, bf16[96,256]{1,0:T(8,128)(2,1)} %constant.54.clone.c_hbm), custom_call_target="tpu_custom_call" | custom-call | flops 1000 | bytes 1000 | tf_op jit(solution)/shard_map/x_send/pallas_call | solution.py:182
  3.3 0.5 %collective-permute-start = (f32[384,512]{1,0:T(8,128)S(1)}, f32[384,512]{1,0:T(8,128)S(1)}, u32[]{:S(2)}, u32[]{:S(2)}) collective-permute-start(f32[384,512]{1,0:T(8,128)S(1)} %get-tuple-element.26), channel_id=1, source_target_pairs={{0,16},{16,0},{1,17},{17,1},{2,18},{18,2},{3,19},{19,3},{4,20},{20... | collective-permute-start | bytes 2359304 | tf_op jit(solution)/shard_map/ppermute | solution.py:202
  3.8 2.6 %collective-permute-start.3 = (f32[128,512]{1,0:T(8,128)S(1)}, f32[128,512]{1,0:T(8,128)S(1)}, u32[]{:S(2)}, u32[]{:S(2)}) collective-permute-start(f32[128,512]{1,0:T(8,128)S(1)} %get-tuple-element.36), channel_id=1, source_target_pairs={{0,1},{1,2},{2,3},{3,0},{4,5},{5,6},{6,7},{7,4},{8,9},{9,10},{10,1... | collective-permute-start | bytes 786440 | tf_op jit(solution)/shard_map/ppermute | solution.py:873
  6.4 2.1 %collective-permute-start.4 = (f32[128,512]{1,0:T(8,128)S(1)}, f32[128,512]{1,0:T(8,128)S(1)}, u32[]{:S(2)}, u32[]{:S(2)}) collective-permute-start(f32[128,512]{1,0:T(8,128)S(1)} %get-tuple-element.37), channel_id=1, source_target_pairs={{1,0},{2,1},{3,2},{0,3},{5,4},{6,5},{7,6},{4,7},{9,8},{10,9},{11,1... | collective-permute-start | bytes 786440 | tf_op jit(solution)/shard_map/ppermute | solution.py:873
  8.5 0.0 collective-permute-done.r_ref
  8.5 0.0 copy-done.20
  8.5 0.0 copy-start
  8.6 0.0 copy-start.1
  8.6 0.0 copy-start.4
  8.6 0.0 copy-start.8
  8.6 0.0 copy-start.10
  8.6 0.0 copy-start.14
  8.6 0.0 copy-start.16
  8.6 0.0 copy-start.18
  8.6 0.0 copy-start.21
  8.7 2.6 %x_apply.1 = (f32[32,64,512]{2,1,0:T(8,128)S(1)}, f32[32,32,512]{2,1,0:T(8,128)S(1)}, f32[32,16,512]{2,1,0:T(8,128)S(1)}, f32[24,512]{1,0:T(8,128)S(1)}, f32[24,512]{1,0:T(8,128)S(1)}) custom-call(f32[32,64,512]{2,1,0:T(8,128)S(1)} %get-tuple-element.25.u_ref, f32[384,512]{1,0:T(8,128)S(1)} %collective-permute-done.r_ref, ...), custom_call_target="tpu_custom_call" | custom-call | flops 1000 | bytes 1000 | tf_op jit(solution)/shard_map/x_apply/pallas_call | solution.py:272
  11.3 0.0 copy-start.3
  11.3 0.0 copy-start.6
  11.3 0.0 copy-start.7
  11.3 0.0 copy-start.12
  11.4 0.0 copy-start.13
  11.4 0.0 copy-start.22
  11.4 1.7 %collective-permute-start.1 = (f32[24,512]{1,0:T(8,128)S(1)}, f32[24,512]{1,0:T(8,128)S(1)}, u32[]{:S(2)}, u32[]{:S(2)}) collective-permute-start(f32[24,512]{1,0:T(8,128)S(1)} %get-tuple-element.32), channel_id=1, source_target_pairs={{0,4},{4,8},{8,12},{12,0},{1,5},{5,9},{9,13},{13,1},{2,6},{6,10},{... | collective-permute-start | bytes 147464 | tf_op jit(solution)/shard_map/ppermute | solution.py:873
  13.1 1.3 %collective-permute-start.2 = (f32[24,512]{1,0:T(8,128)S(1)}, f32[24,512]{1,0:T(8,128)S(1)}, u32[]{:S(2)}, u32[]{:S(2)}) collective-permute-start(f32[24,512]{1,0:T(8,128)S(1)} %get-tuple-element.33), channel_id=1, source_target_pairs={{4,0},{8,4},{12,8},{0,12},{5,1},{9,5},{13,9},{1,13},{6,2},{10,6},{... | collective-permute-start | bytes 147464 | tf_op jit(solution)/shard_map/ppermute | solution.py:873
  14.4 2.4 %z_first.1 = (f32[192,512]{1,0:T(8,128)S(1)}, f32[112,512]{1,0:T(8,128)S(1)}, f32[16,512]{1,0:T(8,128)S(1)}, f32[16,32,512]{2,1,0:T(8,128)S(1)}, f32[8,16,512]{2,1,0:T(8,128)S(1)}) custom-call(f32[32,32,512]{2,1,0:T(8,128)S(1)} %get-tuple-element.28.x2, f32[32,16,512]{2,1,0:T(8,128)S(1)} %get-tuple-element.29.x3, f32[384,512]{1,0:T(8,128)S(1)} %collective-permute-done.r_ref), custom_call_target="tpu_custom_call" | custom-call | flops 1000 | bytes 1000 | tf_op jit(solution)/shard_map/z_first/pallas_call | solution.py:375
  16.7 0.0 collective-permute-done.1.fl
  16.7 0.4 %collective-permute-done.2.fr = f32[24,512]{1,0:T(8,128)S(1)} collective-permute-done((f32[24,512]{1,0:T(8,128)S(1)}, f32[24,512]{1,0:T(8,128)S(1)}, u32[]{:S(2)}, u32[]{:S(2)}) %collective-permute-start.2) | collective-permute-done | bytes 49184 | tf_op jit(solution)/shard_map/ppermute | solution.py:873
  17.2 0.0 copy-done
  17.2 0.9 %y_messages.1 = (f32[296,128]{1,0:T(8,128)S(1)}, f32[296,128]{1,0:T(8,128)S(1)}) custom-call(f32[192,512]{1,0:T(8,128)S(1)} %get-tuple-element.39.c2, f32[112,512]{1,0:T(8,128)S(1)} %get-tuple-element.40.c3, f32[16,512]{1,0:T(8,128)S(1)} %get-tuple-element.41.cf, f32[24,512]{1,0:T(8,128)S(1)} %collective-permute-done.1.fl, ...), custom_call_target="tpu_custom_call" | custom-call | flops 1000 | bytes 1000 | tf_op jit(solution)/shard_map/y_messages/pallas_call | solution.py:548
  18.1 2.2 %collective-permute-start.5 = (f32[296,128]{1,0:T(8,128)S(1)}, f32[296,128]{1,0:T(8,128)S(1)}, u32[]{:S(2)}, u32[]{:S(2)}) collective-permute-start(f32[296,128]{1,0:T(8,128)S(1)} %get-tuple-element.42), channel_id=1, source_target_pairs={{1,0},{2,1},{3,2},{0,3},{5,4},{6,5},{7,6},{4,7},{9,8},{10,9},{11,1... | collective-permute-start | bytes 454664 | tf_op jit(solution)/shard_map/ppermute | solution.py:873
  20.3 0.0 collective-permute-start.6
  20.3 0.0 copy-done.3
  20.3 0.0 copy-done.6
  20.3 0.0 copy-done.7
  20.3 0.0 copy-done.12
  20.4 0.0 copy-done.13
  20.4 0.0 copy-start.19
  20.4 0.0 copy-start.5
  20.4 0.0 copy-start.9
  20.4 0.0 copy-start.11
  20.4 0.0 copy-start.17
  20.4 6.3 %main_part.1 = (f32[4,32,64,128]{3,2,1,0:T(8,128)S(1)}, f32[8,128]{1,0:T(8,128)S(1)}, f32[32,64,512]{2,1,0:T(8,128)}) custom-call(f32[32,64,512]{2,1,0:T(8,128)S(1)} %get-tuple-element.27.x1, f32[16,32,512]{2,1,0:T(8,128)S(1)} %get-tuple-element.30.x2, f32[8,16,512]{2,1,0:T(8,128)S(1)} %get-tuple-element.31.x3, f32[24,512]{1,0:T(8,128)S(1)} %collective-permute-done.1.fl, ...), custom_call_target="tpu_custom_call" | custom-call | flops 1000 | bytes 1000 | tf_op jit(solution)/shard_map/main_part/pallas_call | solution.py:686
  26.8 0.0 collective-permute-done.3.b1
  26.8 0.0 collective-permute-done.4.a1
  26.8 0.7 %early_part.1.w_ref = f32[256,512]{1,0:T(8,128)S(1)} custom-call(f32[128,512]{1,0:T(8,128)S(1)} %collective-permute-done.3.b1, f32[128,512]{1,0:T(8,128)S(1)} %collective-permute-done.4.a1, bf16[2,768,256]{2,1,0:T(8,128)(2,1)S(1)} %copy-done, bf16[2,384,256]{2,1,0:T(8,128)(2,1)S(1)} %copy-done.1, bf16[64,192]{1,0:T(8,128)(2,1)S(1)} %copy-done.19, ...), custom_call_target="tpu_custom_call" | custom-call | flops 1000 | bytes 1000 | tf_op jit(solution)/shard_map/early_part/pallas_call | solution.py:720
  27.5 0.0 collective-permute-done.5.fr
  27.5 0.0 collective-permute-done.6.fl
  27.6 2.3 %z_apply.1 = (f32[4,32,64,128]{3,2,1,0:T(8,128)S(1)}, f32[32,64,512]{2,1,0:T(8,128)}) custom-call(f32[4,32,64,128]{3,2,1,0:T(8,128)S(1)} %get-tuple-element.34.in_ref, f32[32,64,512]{2,1,0:T(8,128)} %get-tuple-element.35.base_hbm, f32[256,512]{1,0:T(8,128)S(1)} %early_part.1.w_ref, ...), custom_call_target="tpu_custom_call", output_to_operand_aliasing={{0}: (0, {}), {1}: (1, {})} | custom-call | tf_op jit(solution)/shard_map/z_apply/pallas_call | solution.py:843
  (19 shorter events, 0.0 us)
Async XLA Ops:
  0.0 8.5 %copy-start.20 = (bf16[3,8,384]{2,1,0:T(8,128)(2,1)S(1)}, bf16[3,8,384]{2,1,0:T(8,128)(2,1)}, u32[]{:S(2)}) copy-start(bf16[3,8,384]{2,1,0:T(8,128)(2,1)} %constant.56.clone.c_ref) | copy-start | bytes 55300
  0.0 8.5 %copy-start.15 = (bf16[2,112,240]{2,1,0:T(8,128)(2,1)S(1)}, bf16[2,112,240]{2,1,0:T(8,128)(2,1)}, u32[]{:S(2)}) copy-start(bf16[2,112,240]{2,1,0:T(8,128)(2,1)} %constant.55.clone.t_ref) | copy-start | bytes 322564
  3.3 5.3 %collective-permute-start = (f32[384,512]{1,0:T(8,128)S(1)}, f32[384,512]{1,0:T(8,128)S(1)}, u32[]{:S(2)}, u32[]{:S(2)}) collective-permute-start(f32[384,512]{1,0:T(8,128)S(1)} %get-tuple-element.26), channel_id=1, source_target_pairs={{0,16},{16,0},{1,17},{17,1},{2,18},{18,2},{3,19},{19,3},{4,20},{20... | collective-permute-start | bytes 2359304 | tf_op jit(solution)/shard_map/ppermute | solution.py:202
  3.8 23.0 %collective-permute-start.3 = (f32[128,512]{1,0:T(8,128)S(1)}, f32[128,512]{1,0:T(8,128)S(1)}, u32[]{:S(2)}, u32[]{:S(2)}) collective-permute-start(f32[128,512]{1,0:T(8,128)S(1)} %get-tuple-element.36), channel_id=1, source_target_pairs={{0,1},{1,2},{2,3},{3,0},{4,5},{5,6},{6,7},{7,4},{8,9},{9,10},{10,1... | collective-permute-start | bytes 786440 | tf_op jit(solution)/shard_map/ppermute | solution.py:873
  6.4 20.4 %collective-permute-start.4 = (f32[128,512]{1,0:T(8,128)S(1)}, f32[128,512]{1,0:T(8,128)S(1)}, u32[]{:S(2)}, u32[]{:S(2)}) collective-permute-start(f32[128,512]{1,0:T(8,128)S(1)} %get-tuple-element.37), channel_id=1, source_target_pairs={{1,0},{2,1},{3,2},{0,3},{5,4},{6,5},{7,6},{4,7},{9,8},{10,9},{11,1... | collective-permute-start | bytes 786440 | tf_op jit(solution)/shard_map/ppermute | solution.py:873
  8.5 8.6 %copy-start = (bf16[2,768,256]{2,1,0:T(8,128)(2,1)S(1)}, bf16[2,768,256]{2,1,0:T(8,128)(2,1)}, u32[]{:S(2)}) copy-start(bf16[2,768,256]{2,1,0:T(8,128)(2,1)} %constant.48.clone.o1.own1) | copy-start | bytes 2359300
  8.6 8.6 %copy-start.1 = (bf16[2,384,256]{2,1,0:T(8,128)(2,1)S(1)}, bf16[2,384,256]{2,1,0:T(8,128)(2,1)}, u32[]{:S(2)}) copy-start(bf16[2,384,256]{2,1,0:T(8,128)(2,1)} %constant.49.clone.e1.edge1) | copy-start | bytes 1179652
  8.6 8.6 %copy-start.4 = (bf16[1536,256]{1,0:T(8,128)(2,1)S(1)}, bf16[1536,256]{1,0:T(8,128)(2,1)}, u32[]{:S(2)}) copy-start(bf16[1536,256]{1,0:T(8,128)(2,1)} %constant.57.clone.m2) | copy-start | bytes 2359300
  8.6 8.6 %copy-start.8 = (bf16[1536,128]{1,0:T(8,128)(2,1)S(1)}, bf16[1536,128]{1,0:T(8,128)(2,1)}, u32[]{:S(2)}) copy-start(bf16[1536,128]{1,0:T(8,128)(2,1)} %constant.58.clone.m3) | copy-start | bytes 1179652
  8.6 8.6 %copy-start.10 = (bf16[384,256]{1,0:T(8,128)(2,1)S(1)}, bf16[384,256]{1,0:T(8,128)(2,1)}, u32[]{:S(2)}) copy-start(bf16[384,256]{1,0:T(8,128)(2,1)} %constant.59.clone.h2) | copy-start | bytes 589828
  8.6 8.6 %copy-start.14 = (f32[224,128]{1,0:T(8,128)S(1)}, f32[224,128]{1,0:T(8,128)}, u32[]{:S(2)}) copy-start(f32[224,128]{1,0:T(8,128)} %constant.63.clone.k3) | copy-start | bytes 344068
  8.6 8.6 %copy-start.16 = (bf16[384,128]{1,0:T(8,128)(2,1)S(1)}, bf16[384,128]{1,0:T(8,128)(2,1)}, u32[]{:S(2)}) copy-start(bf16[384,128]{1,0:T(8,128)(2,1)} %constant.60.clone.h3) | copy-start | bytes 294916
  8.6 8.6 %copy-start.18 = (f32[96,128]{1,0:T(8,128)S(1)}, f32[96,128]{1,0:T(8,128)}, u32[]{:S(2)}) copy-start(f32[96,128]{1,0:T(8,128)} %constant.62.clone.k2) | copy-start | bytes 147460
  8.6 8.6 %copy-start.21 = (f32[32,128]{1,0:T(8,128)S(1)}, f32[32,128]{1,0:T(8,128)}, u32[]{:S(2)}) copy-start(f32[32,128]{1,0:T(8,128)} %constant.61.clone.k1) | copy-start | bytes 49156
  11.3 9.0 %copy-start.2 = (bf16[2,768,256]{2,1,0:T(8,128)(2,1)S(1)}, bf16[2,768,256]{2,1,0:T(8,128)(2,1)}, u32[]{:S(2)}) copy-start(bf16[2,768,256]{2,1,0:T(8,128)(2,1)} %constant.52.clone.o3) | copy-start | bytes 2359300
  11.3 9.0 %copy-start.3 = (bf16[2,768,256]{2,1,0:T(8,128)(2,1)S(1)}, bf16[2,768,256]{2,1,0:T(8,128)(2,1)}, u32[]{:S(2)}) copy-start(bf16[2,768,256]{2,1,0:T(8,128)(2,1)} %constant.50.clone.o2) | copy-start | bytes 2359300
  11.3 9.0 %copy-start.6 = (bf16[2,384,256]{2,1,0:T(8,128)(2,1)S(1)}, bf16[2,384,256]{2,1,0:T(8,128)(2,1)}, u32[]{:S(2)}) copy-start(bf16[2,384,256]{2,1,0:T(8,128)(2,1)} %constant.53.clone.e3) | copy-start | bytes 1179652
  11.3 9.0 %copy-start.7 = (bf16[2,384,256]{2,1,0:T(8,128)(2,1)S(1)}, bf16[2,384,256]{2,1,0:T(8,128)(2,1)}, u32[]{:S(2)}) copy-start(bf16[2,384,256]{2,1,0:T(8,128)(2,1)} %constant.51.clone.e2) | copy-start | bytes 1179652
  11.3 9.0 %copy-start.12 = (f32[256,128]{1,0:T(8,128)S(1)}, f32[256,128]{1,0:T(8,128)}, u32[]{:S(2)}) copy-start(f32[256,128]{1,0:T(8,128)} %constant.66.clone.k3) | copy-start | bytes 393220
  11.4 9.0 %copy-start.13 = (f32[256,128]{1,0:T(8,128)S(1)}, f32[256,128]{1,0:T(8,128)}, u32[]{:S(2)}) copy-start(f32[256,128]{1,0:T(8,128)} %constant.65.clone.k2) | copy-start | bytes 393220
  11.4 9.0 %copy-start.22 = (f32[8,128]{1,0:T(8,128)S(1)}, f32[8,128]{1,0:T(8,128)}, u32[]{:S(2)}) copy-start(f32[8,128]{1,0:T(8,128)} %constant.64.clone.k1) | copy-start | bytes 12292
  11.4 5.3 %collective-permute-start.1 = (f32[24,512]{1,0:T(8,128)S(1)}, f32[24,512]{1,0:T(8,128)S(1)}, u32[]{:S(2)}, u32[]{:S(2)}) collective-permute-start(f32[24,512]{1,0:T(8,128)S(1)} %get-tuple-element.32), channel_id=1, source_target_pairs={{0,4},{4,8},{8,12},{12,0},{1,5},{5,9},{9,13},{13,1},{2,6},{6,10},{... | collective-permute-start | bytes 147464 | tf_op jit(solution)/shard_map/ppermute | solution.py:873
  13.1 4.1 %collective-permute-start.2 = (f32[24,512]{1,0:T(8,128)S(1)}, f32[24,512]{1,0:T(8,128)S(1)}, u32[]{:S(2)}, u32[]{:S(2)}) collective-permute-start(f32[24,512]{1,0:T(8,128)S(1)} %get-tuple-element.33), channel_id=1, source_target_pairs={{4,0},{8,4},{12,8},{0,12},{5,1},{9,5},{13,9},{1,13},{6,2},{10,6},{... | collective-permute-start | bytes 147464 | tf_op jit(solution)/shard_map/ppermute | solution.py:873
  18.1 9.4 %collective-permute-start.5 = (f32[296,128]{1,0:T(8,128)S(1)}, f32[296,128]{1,0:T(8,128)S(1)}, u32[]{:S(2)}, u32[]{:S(2)}) collective-permute-start(f32[296,128]{1,0:T(8,128)S(1)} %get-tuple-element.42), channel_id=1, source_target_pairs={{1,0},{2,1},{3,2},{0,3},{5,4},{6,5},{7,6},{4,7},{9,8},{10,9},{11,1... | collective-permute-start | bytes 454664 | tf_op jit(solution)/shard_map/ppermute | solution.py:873
  20.3 7.2 %collective-permute-start.6 = (f32[296,128]{1,0:T(8,128)S(1)}, f32[296,128]{1,0:T(8,128)S(1)}, u32[]{:S(2)}, u32[]{:S(2)}) collective-permute-start(f32[296,128]{1,0:T(8,128)S(1)} %get-tuple-element.43), channel_id=1, source_target_pairs={{0,1},{1,2},{2,3},{3,0},{4,5},{5,6},{6,7},{7,4},{8,9},{9,10},{10,1... | collective-permute-start | bytes 454664 | tf_op jit(solution)/shard_map/ppermute | solution.py:873
  20.4 6.4 %copy-start.19 = (bf16[64,192]{1,0:T(8,128)(2,1)S(1)}, bf16[64,192]{1,0:T(8,128)(2,1)}, u32[]{:S(2)}) copy-start(bf16[64,192]{1,0:T(8,128)(2,1)} %constant.67.clone.xt) | copy-start | bytes 73732
  20.4 7.1 %copy-start.5 = (bf16[512,512]{1,0:T(8,128)(2,1)S(1)}, bf16[512,512]{1,0:T(8,128)(2,1)}, u32[]{:S(2)}) copy-start(bf16[512,512]{1,0:T(8,128)(2,1)} %constant.68.clone.t2) | copy-start | bytes 1572868
  20.4 7.1 %copy-start.9 = (bf16[256,512]{1,0:T(8,128)(2,1)S(1)}, bf16[256,512]{1,0:T(8,128)(2,1)}, u32[]{:S(2)}) copy-start(bf16[256,512]{1,0:T(8,128)(2,1)} %constant.69.clone.t3) | copy-start | bytes 786436
  20.4 7.1 %copy-start.11 = (bf16[128,512]{1,0:T(8,128)(2,1)S(1)}, bf16[128,512]{1,0:T(8,128)(2,1)}, u32[]{:S(2)}) copy-start(bf16[128,512]{1,0:T(8,128)(2,1)} %constant.71.clone.yf) | copy-start | bytes 393220
  20.4 7.1 %copy-start.17 = (bf16[256,48]{1,0:T(8,128)(2,1)S(1)}, bf16[256,48]{1,0:T(8,128)(2,1)}, u32[]{:S(2)}) copy-start(bf16[256,48]{1,0:T(8,128)(2,1)} %constant.70.clone.xf) | copy-start | bytes 73732

commit v7 on v6

--- a/solution.py
+++ b/solution.py
@@ -674,12 +674,8 @@
             return 0
 
         lax.fori_loop(0, (counts[1] // 8) * groups, merge, 0)
-        more = leaving([z for z in untouched if z % 2 == 0])
-        for copy in more:
-            copy.start()
-
         done_ref[...] = jnp.zeros((8, 128), F32)
-        for copy in copies + more:
+        for copy in copies:
             copy.wait()
 
     flat = [t for band in bands for t in band]
@@ -749,9 +745,18 @@
     side_hi, side_lo = hi_lo(np.concatenate([left, right, np.zeros((4, ny))]))
     side_rows = np.concatenate([side_hi, side_hi, side_lo, np.zeros((104, ny), side_hi.dtype)])
     touched = sorted(touched_layers(nz), key=lambda z: np.abs(maps[0][z]).max() > 1e-12)
+    left_over = [z for z in range(0, nz, 2) if z not in touched]
 
     def kernel(in_ref, base_hbm, w_ref, fr, fl, t2, t3, xf, yf, io_ref, out_hbm, s1, s2, s3, sem):
         del base_hbm
+        copies = []
+        for slot, z in enumerate(left_over):
+            for q in range(groups):
+                copy = pltpu.make_async_copy(
+                    io_ref.at[q, z], out_hbm.at[z, :, 128 * q : 128 * q + 128], sem.at[len(touched) + slot]
+                )
+                copy.start()
+                copies.append(copy)
         s3[...] = jnp.zeros(s3.shape, F32)
         halos = [
             jnp.concatenate([ref[at[2] + 8 * p : at[2] + 8 * p + 8, :] for p in range(groups)], axis=1)
@@ -804,7 +809,6 @@
                     total = add(total, get(c) * np.float32(scalar))
             return total
 
-        copies = []
         for slot, z in enumerate(touched):
 
             for t in range(nx // 16):
@@ -850,7 +854,7 @@
             pltpu.VMEM((4, groups, nx, 128), F32),
             pltpu.VMEM((maps[1].shape[1], groups, nx // 2, 128), F32),
             pltpu.VMEM((maps[2].shape[1], groups, nx // 2, 128), F32),
-            pltpu.SemaphoreType.DMA((len(touched),)),
+            pltpu.SemaphoreType.DMA((len(touched) + len(left_over),)),
         ],
         compiler_params=params(24),
         name="z_apply",

time: 30 us -> 30 us (level)
  transfers between devices with their start and end apart: 7 -> 7, of which waited for: 1 -> 2; matrix products, arithmetic and copies ran while one was open for 0% -> 0% of each run, Pallas kernels for 43% -> 43%
where the time goes in v7:
time: 30 us; the launch traced here: 29.8 us
  Pallas kernels  18.2 us (61%)
  starting transfers between devices  10.5 us (35%)
  waiting for transfers between devices  0.62 us (2%)
  between operations  0.35 us (1%)
    pallas_call x1, Pallas kernels, main_part(): pl.pallas_call(kernel, in_specs=[VM] * 14, out_specs=[VM, VM, HB], out_sh...  6.17 us
    ppermute x3, starting transfers between devices, swap(): lax.ppermute(to_left, axis, left)  5.62 us
    ppermute x3, starting transfers between devices, swap(): lax.ppermute(to_right, axis, right)  4.32 us
    pallas_call x1, Pallas kernels, x_send(): pl.pallas_call(kernel, in_specs=[HB, HB], out_specs=[VM] * 4, out_shape=[...  3.25 us
    pallas_call x1, Pallas kernels, x_apply(): pl.pallas_call(kernel, grid=(steps,), in_specs=[VM] * 4, out_specs=[VM] *...  2.64 us
    pallas_call x1, Pallas kernels, z_first(): pl.pallas_call(kernel, in_specs=[VM] * 3, out_specs=[VM] * 5, out_shape=[...  2.35 us
    pallas_call x1, Pallas kernels, z_apply(): pl.pallas_call(kernel, in_specs=[VM, HB] + [VM] * 7, out_specs=[VM, HB],...  2.3 us
    pallas_call x1, Pallas kernels, y_messages(): pl.pallas_call(kernel, in_specs=[VM] * 14, out_specs=[VM] * 2, out_shape=...  0.86 us
  transfers between devices with their start and end apart: 7, of which 2 were waited for; matrix products, arithmetic and copies ran while one was open for 0% of the time, Pallas kernels for 43%

profile of v7, /device:TPU:0, one launch (start us, length us, event | category | flops | bytes accessed | tf_op | source)
XLA Modules:
  0.0 29.8 jit_solution(111666275937244336)
XLA Ops:
  0.0 3.2 %x_send.1 = (f32[32,64,512]{2,1,0:T(8,128)S(1)}, f32[384,512]{1,0:T(8,128)S(1)}, f32[128,512]{1,0:T(8,128)S(1)}, f32[128,512]{1,0:T(8,128)S(1)}) custom-call(f32[32,64,512]{2,1,0:T(8,128)} %u_hbm.1, bf16[96,256]{1,0:T(8,128)(2,1)} %constant.54.clone.c_hbm), custom_call_target="tpu_custom_call" | custom-call | flops 1000 | bytes 1000 | tf_op jit(solution)/shard_map/x_send/pallas_call | solution.py:182
  3.3 0.5 %collective-permute-start = (f32[384,512]{1,0:T(8,128)S(1)}, f32[384,512]{1,0:T(8,128)S(1)}, u32[]{:S(2)}, u32[]{:S(2)}) collective-permute-start(f32[384,512]{1,0:T(8,128)S(1)} %get-tuple-element.26), channel_id=1, source_target_pairs={{0,16},{16,0},{1,17},{17,1},{2,18},{18,2},{3,19},{19,3},{4,20},{20... | collective-permute-start | bytes 2359304 | tf_op jit(solution)/shard_map/ppermute | solution.py:202
  3.8 2.6 %collective-permute-start.3 = (f32[128,512]{1,0:T(8,128)S(1)}, f32[128,512]{1,0:T(8,128)S(1)}, u32[]{:S(2)}, u32[]{:S(2)}) collective-permute-start(f32[128,512]{1,0:T(8,128)S(1)} %get-tuple-element.36), channel_id=1, source_target_pairs={{0,1},{1,2},{2,3},{3,0},{4,5},{5,6},{6,7},{7,4},{8,9},{9,10},{10,1... | collective-permute-start | bytes 786440 | tf_op jit(solution)/shard_map/ppermute | solution.py:877
  6.4 2.1 %collective-permute-start.4 = (f32[128,512]{1,0:T(8,128)S(1)}, f32[128,512]{1,0:T(8,128)S(1)}, u32[]{:S(2)}, u32[]{:S(2)}) collective-permute-start(f32[128,512]{1,0:T(8,128)S(1)} %get-tuple-element.37), channel_id=1, source_target_pairs={{1,0},{2,1},{3,2},{0,3},{5,4},{6,5},{7,6},{4,7},{9,8},{10,9},{11,1... | collective-permute-start | bytes 786440 | tf_op jit(solution)/shard_map/ppermute | solution.py:877
  8.5 0.0 collective-permute-done.r_ref
  8.5 0.0 copy-done.20
  8.5 0.0 copy-done.15
  8.5 0.0 copy-start
  8.6 0.0 copy-start.1
  8.6 0.0 copy-start.4
  8.6 0.0 copy-start.8
  8.6 0.0 copy-start.10
  8.6 0.0 copy-start.14
  8.6 0.0 copy-start.16
  8.6 0.0 copy-start.18
  8.6 0.0 copy-start.21
  8.7 2.6 %x_apply.1 = (f32[32,64,512]{2,1,0:T(8,128)S(1)}, f32[32,32,512]{2,1,0:T(8,128)S(1)}, f32[32,16,512]{2,1,0:T(8,128)S(1)}, f32[24,512]{1,0:T(8,128)S(1)}, f32[24,512]{1,0:T(8,128)S(1)}) custom-call(f32[32,64,512]{2,1,0:T(8,128)S(1)} %get-tuple-element.25.u_ref, f32[384,512]{1,0:T(8,128)S(1)} %collective-permute-done.r_ref, ...), custom_call_target="tpu_custom_call" | custom-call | flops 1000 | bytes 1000 | tf_op jit(solution)/shard_map/x_apply/pallas_call | solution.py:272
  11.3 0.0 copy-start.3
  11.3 0.0 copy-start.6
  11.3 0.0 copy-start.7
  11.3 0.0 copy-start.12
  11.4 0.0 copy-start.13
  11.4 0.0 copy-start.22
  11.4 1.7 %collective-permute-start.1 = (f32[24,512]{1,0:T(8,128)S(1)}, f32[24,512]{1,0:T(8,128)S(1)}, u32[]{:S(2)}, u32[]{:S(2)}) collective-permute-start(f32[24,512]{1,0:T(8,128)S(1)} %get-tuple-element.32), channel_id=1, source_target_pairs={{0,4},{4,8},{8,12},{12,0},{1,5},{5,9},{9,13},{13,1},{2,6},{6,10},{... | collective-permute-start | bytes 147464 | tf_op jit(solution)/shard_map/ppermute | solution.py:877
  13.1 1.3 %collective-permute-start.2 = (f32[24,512]{1,0:T(8,128)S(1)}, f32[24,512]{1,0:T(8,128)S(1)}, u32[]{:S(2)}, u32[]{:S(2)}) collective-permute-start(f32[24,512]{1,0:T(8,128)S(1)} %get-tuple-element.33), channel_id=1, source_target_pairs={{4,0},{8,4},{12,8},{0,12},{5,1},{9,5},{13,9},{1,13},{6,2},{10,6},{... | collective-permute-start | bytes 147464 | tf_op jit(solution)/shard_map/ppermute | solution.py:877
  14.4 2.4 %z_first.1 = (f32[192,512]{1,0:T(8,128)S(1)}, f32[112,512]{1,0:T(8,128)S(1)}, f32[16,512]{1,0:T(8,128)S(1)}, f32[16,32,512]{2,1,0:T(8,128)S(1)}, f32[8,16,512]{2,1,0:T(8,128)S(1)}) custom-call(f32[32,32,512]{2,1,0:T(8,128)S(1)} %get-tuple-element.28.x2, f32[32,16,512]{2,1,0:T(8,128)S(1)} %get-tuple-element.29.x3, f32[384,512]{1,0:T(8,128)S(1)} %collective-permute-done.r_ref), custom_call_target="tpu_custom_call" | custom-call | flops 1000 | bytes 1000 | tf_op jit(solution)/shard_map/z_first/pallas_call | solution.py:375
  16.7 0.0 collective-permute-done.1.fl
  16.7 0.4 %collective-permute-done.2.fr = f32[24,512]{1,0:T(8,128)S(1)} collective-permute-done((f32[24,512]{1,0:T(8,128)S(1)}, f32[24,512]{1,0:T(8,128)S(1)}, u32[]{:S(2)}, u32[]{:S(2)}) %collective-permute-start.2) | collective-permute-done | bytes 49184 | tf_op jit(solution)/shard_map/ppermute | solution.py:877
  17.2 0.0 copy-done
  17.2 0.0 copy-done.1
  17.2 0.0 copy-done.4
  17.2 0.0 copy-done.8
  17.2 0.9 %y_messages.1 = (f32[296,128]{1,0:T(8,128)S(1)}, f32[296,128]{1,0:T(8,128)S(1)}) custom-call(f32[192,512]{1,0:T(8,128)S(1)} %get-tuple-element.39.c2, f32[112,512]{1,0:T(8,128)S(1)} %get-tuple-element.40.c3, f32[16,512]{1,0:T(8,128)S(1)} %get-tuple-element.41.cf, f32[24,512]{1,0:T(8,128)S(1)} %collective-permute-done.1.fl, ...), custom_call_target="tpu_custom_call" | custom-call | flops 1000 | bytes 1000 | tf_op jit(solution)/shard_map/y_messages/pallas_call | solution.py:548
  18.1 2.2 %collective-permute-start.5 = (f32[296,128]{1,0:T(8,128)S(1)}, f32[296,128]{1,0:T(8,128)S(1)}, u32[]{:S(2)}, u32[]{:S(2)}) collective-permute-start(f32[296,128]{1,0:T(8,128)S(1)} %get-tuple-element.42), channel_id=1, source_target_pairs={{1,0},{2,1},{3,2},{0,3},{5,4},{6,5},{7,6},{4,7},{9,8},{10,9},{11,1... | collective-permute-start | bytes 454664 | tf_op jit(solution)/shard_map/ppermute | solution.py:877
  20.3 0.0 collective-permute-start.6
  20.4 0.0 copy-start.19
  20.4 0.0 copy-start.5
  20.4 0.0 copy-start.9
  20.4 0.0 copy-start.11
  20.4 0.0 copy-start.17
  20.4 6.2 %main_part.1 = (f32[4,32,64,128]{3,2,1,0:T(8,128)S(1)}, f32[8,128]{1,0:T(8,128)S(1)}, f32[32,64,512]{2,1,0:T(8,128)}) custom-call(f32[32,64,512]{2,1,0:T(8,128)S(1)} %get-tuple-element.27.x1, f32[16,32,512]{2,1,0:T(8,128)S(1)} %get-tuple-element.30.x2, f32[8,16,512]{2,1,0:T(8,128)S(1)} %get-tuple-element.31.x3, f32[24,512]{1,0:T(8,128)S(1)} %collective-permute-done.1.fl, ...), custom_call_target="tpu_custom_call" | custom-call | flops 1000 | bytes 1000 | tf_op jit(solution)/shard_map/main_part/pallas_call | solution.py:682
  26.6 0.0 collective-permute-done.3.b1
  26.6 0.0 collective-permute-done.4.a1
  26.6 0.7 %early_part.1.w_ref = f32[256,512]{1,0:T(8,128)S(1)} custom-call(f32[128,512]{1,0:T(8,128)S(1)} %collective-permute-done.3.b1, f32[128,512]{1,0:T(8,128)S(1)} %collective-permute-done.4.a1, bf16[2,768,256]{2,1,0:T(8,128)(2,1)S(1)} %copy-done, bf16[2,384,256]{2,1,0:T(8,128)(2,1)S(1)} %copy-done.1, bf16[64,192]{1,0:T(8,128)(2,1)S(1)} %copy-done.19, ...), custom_call_target="tpu_custom_call" | custom-call | flops 1000 | bytes 1000 | tf_op jit(solution)/shard_map/early_part/pallas_call | solution.py:716
  27.3 0.0 collective-permute-done.5.fr
  27.3 0.2 collective-permute-done.6.fl
  27.5 0.0 copy-done.5
  27.5 2.3 %z_apply.1 = (f32[4,32,64,128]{3,2,1,0:T(8,128)S(1)}, f32[32,64,512]{2,1,0:T(8,128)}) custom-call(f32[4,32,64,128]{3,2,1,0:T(8,128)S(1)} %get-tuple-element.34.in_ref, f32[32,64,512]{2,1,0:T(8,128)} %get-tuple-element.35.base_hbm, f32[256,512]{1,0:T(8,128)S(1)} %early_part.1.w_ref, ...), custom_call_target="tpu_custom_call", output_to_operand_aliasing={{0}: (0, {}), {1}: (1, {})} | custom-call | tf_op jit(solution)/shard_map/z_apply/pallas_call | solution.py:847
  (19 shorter events, 0.0 us)
Async XLA Ops:
  0.0 8.5 %copy-start.20 = (bf16[3,8,384]{2,1,0:T(8,128)(2,1)S(1)}, bf16[3,8,384]{2,1,0:T(8,128)(2,1)}, u32[]{:S(2)}) copy-start(bf16[3,8,384]{2,1,0:T(8,128)(2,1)} %constant.56.clone.c_ref) | copy-start | bytes 55300
  0.0 8.5 %copy-start.15 = (bf16[2,112,240]{2,1,0:T(8,128)(2,1)S(1)}, bf16[2,112,240]{2,1,0:T(8,128)(2,1)}, u32[]{:S(2)}) copy-start(bf16[2,112,240]{2,1,0:T(8,128)(2,1)} %constant.55.clone.t_ref) | copy-start | bytes 322564
  3.3 5.3 %collective-permute-start = (f32[384,512]{1,0:T(8,128)S(1)}, f32[384,512]{1,0:T(8,128)S(1)}, u32[]{:S(2)}, u32[]{:S(2)}) collective-permute-start(f32[384,512]{1,0:T(8,128)S(1)} %get-tuple-element.26), channel_id=1, source_target_pairs={{0,16},{16,0},{1,17},{17,1},{2,18},{18,2},{3,19},{19,3},{4,20},{20... | collective-permute-start | bytes 2359304 | tf_op jit(solution)/shard_map/ppermute | solution.py:202
  3.8 22.8 %collective-permute-start.3 = (f32[128,512]{1,0:T(8,128)S(1)}, f32[128,512]{1,0:T(8,128)S(1)}, u32[]{:S(2)}, u32[]{:S(2)}) collective-permute-start(f32[128,512]{1,0:T(8,128)S(1)} %get-tuple-element.36), channel_id=1, source_target_pairs={{0,1},{1,2},{2,3},{3,0},{4,5},{5,6},{6,7},{7,4},{8,9},{9,10},{10,1... | collective-permute-start | bytes 786440 | tf_op jit(solution)/shard_map/ppermute | solution.py:877
  6.4 20.2 %collective-permute-start.4 = (f32[128,512]{1,0:T(8,128)S(1)}, f32[128,512]{1,0:T(8,128)S(1)}, u32[]{:S(2)}, u32[]{:S(2)}) collective-permute-start(f32[128,512]{1,0:T(8,128)S(1)} %get-tuple-element.37), channel_id=1, source_target_pairs={{1,0},{2,1},{3,2},{0,3},{5,4},{6,5},{7,6},{4,7},{9,8},{10,9},{11,1... | collective-permute-start | bytes 786440 | tf_op jit(solution)/shard_map/ppermute | solution.py:877
  8.5 8.6 %copy-start = (bf16[2,768,256]{2,1,0:T(8,128)(2,1)S(1)}, bf16[2,768,256]{2,1,0:T(8,128)(2,1)}, u32[]{:S(2)}) copy-start(bf16[2,768,256]{2,1,0:T(8,128)(2,1)} %constant.48.clone.o1.own1) | copy-start | bytes 2359300
  8.6 8.6 %copy-start.1 = (bf16[2,384,256]{2,1,0:T(8,128)(2,1)S(1)}, bf16[2,384,256]{2,1,0:T(8,128)(2,1)}, u32[]{:S(2)}) copy-start(bf16[2,384,256]{2,1,0:T(8,128)(2,1)} %constant.49.clone.e1.edge1) | copy-start | bytes 1179652
  8.6 8.6 %copy-start.4 = (bf16[1536,256]{1,0:T(8,128)(2,1)S(1)}, bf16[1536,256]{1,0:T(8,128)(2,1)}, u32[]{:S(2)}) copy-start(bf16[1536,256]{1,0:T(8,128)(2,1)} %constant.57.clone.m2) | copy-start | bytes 2359300
  8.6 8.6 %copy-start.8 = (bf16[1536,128]{1,0:T(8,128)(2,1)S(1)}, bf16[1536,128]{1,0:T(8,128)(2,1)}, u32[]{:S(2)}) copy-start(bf16[1536,128]{1,0:T(8,128)(2,1)} %constant.58.clone.m3) | copy-start | bytes 1179652
  8.6 8.6 %copy-start.10 = (bf16[384,256]{1,0:T(8,128)(2,1)S(1)}, bf16[384,256]{1,0:T(8,128)(2,1)}, u32[]{:S(2)}) copy-start(bf16[384,256]{1,0:T(8,128)(2,1)} %constant.59.clone.h2) | copy-start | bytes 589828
  8.6 8.6 %copy-start.14 = (f32[224,128]{1,0:T(8,128)S(1)}, f32[224,128]{1,0:T(8,128)}, u32[]{:S(2)}) copy-start(f32[224,128]{1,0:T(8,128)} %constant.63.clone.k3) | copy-start | bytes 344068
  8.6 8.6 %copy-start.16 = (bf16[384,128]{1,0:T(8,128)(2,1)S(1)}, bf16[384,128]{1,0:T(8,128)(2,1)}, u32[]{:S(2)}) copy-start(bf16[384,128]{1,0:T(8,128)(2,1)} %constant.60.clone.h3) | copy-start | bytes 294916
  8.6 8.6 %copy-start.18 = (f32[96,128]{1,0:T(8,128)S(1)}, f32[96,128]{1,0:T(8,128)}, u32[]{:S(2)}) copy-start(f32[96,128]{1,0:T(8,128)} %constant.62.clone.k2) | copy-start | bytes 147460
  8.6 8.6 %copy-start.21 = (f32[32,128]{1,0:T(8,128)S(1)}, f32[32,128]{1,0:T(8,128)}, u32[]{:S(2)}) copy-start(f32[32,128]{1,0:T(8,128)} %constant.61.clone.k1) | copy-start | bytes 49156
  11.3 9.0 %copy-start.2 = (bf16[2,768,256]{2,1,0:T(8,128)(2,1)S(1)}, bf16[2,768,256]{2,1,0:T(8,128)(2,1)}, u32[]{:S(2)}) copy-start(bf16[2,768,256]{2,1,0:T(8,128)(2,1)} %constant.52.clone.o3) | copy-start | bytes 2359300
  11.3 9.0 %copy-start.3 = (bf16[2,768,256]{2,1,0:T(8,128)(2,1)S(1)}, bf16[2,768,256]{2,1,0:T(8,128)(2,1)}, u32[]{:S(2)}) copy-start(bf16[2,768,256]{2,1,0:T(8,128)(2,1)} %constant.50.clone.o2) | copy-start | bytes 2359300
  11.3 9.0 %copy-start.6 = (bf16[2,384,256]{2,1,0:T(8,128)(2,1)S(1)}, bf16[2,384,256]{2,1,0:T(8,128)(2,1)}, u32[]{:S(2)}) copy-start(bf16[2,384,256]{2,1,0:T(8,128)(2,1)} %constant.53.clone.e3) | copy-start | bytes 1179652
  11.3 9.0 %copy-start.7 = (bf16[2,384,256]{2,1,0:T(8,128)(2,1)S(1)}, bf16[2,384,256]{2,1,0:T(8,128)(2,1)}, u32[]{:S(2)}) copy-start(bf16[2,384,256]{2,1,0:T(8,128)(2,1)} %constant.51.clone.e2) | copy-start | bytes 1179652
  11.3 9.0 %copy-start.12 = (f32[256,128]{1,0:T(8,128)S(1)}, f32[256,128]{1,0:T(8,128)}, u32[]{:S(2)}) copy-start(f32[256,128]{1,0:T(8,128)} %constant.66.clone.k3) | copy-start | bytes 393220
  11.4 9.0 %copy-start.13 = (f32[256,128]{1,0:T(8,128)S(1)}, f32[256,128]{1,0:T(8,128)}, u32[]{:S(2)}) copy-start(f32[256,128]{1,0:T(8,128)} %constant.65.clone.k2) | copy-start | bytes 393220
  11.4 9.0 %copy-start.22 = (f32[8,128]{1,0:T(8,128)S(1)}, f32[8,128]{1,0:T(8,128)}, u32[]{:S(2)}) copy-start(f32[8,128]{1,0:T(8,128)} %constant.64.clone.k1) | copy-start | bytes 12292
  11.4 5.3 %collective-permute-start.1 = (f32[24,512]{1,0:T(8,128)S(1)}, f32[24,512]{1,0:T(8,128)S(1)}, u32[]{:S(2)}, u32[]{:S(2)}) collective-permute-start(f32[24,512]{1,0:T(8,128)S(1)} %get-tuple-element.32), channel_id=1, source_target_pairs={{0,4},{4,8},{8,12},{12,0},{1,5},{5,9},{9,13},{13,1},{2,6},{6,10},{... | collective-permute-start | bytes 147464 | tf_op jit(solution)/shard_map/ppermute | solution.py:877
  13.1 4.1 %collective-permute-start.2 = (f32[24,512]{1,0:T(8,128)S(1)}, f32[24,512]{1,0:T(8,128)S(1)}, u32[]{:S(2)}, u32[]{:S(2)}) collective-permute-start(f32[24,512]{1,0:T(8,128)S(1)} %get-tuple-element.33), channel_id=1, source_target_pairs={{4,0},{8,4},{12,8},{0,12},{5,1},{9,5},{13,9},{1,13},{6,2},{10,6},{... | collective-permute-start | bytes 147464 | tf_op jit(solution)/shard_map/ppermute | solution.py:877
  18.1 9.2 %collective-permute-start.5 = (f32[296,128]{1,0:T(8,128)S(1)}, f32[296,128]{1,0:T(8,128)S(1)}, u32[]{:S(2)}, u32[]{:S(2)}) collective-permute-start(f32[296,128]{1,0:T(8,128)S(1)} %get-tuple-element.42), channel_id=1, source_target_pairs={{1,0},{2,1},{3,2},{0,3},{5,4},{6,5},{7,6},{4,7},{9,8},{10,9},{11,1... | collective-permute-start | bytes 454664 | tf_op jit(solution)/shard_map/ppermute | solution.py:877
  20.3 7.2 %collective-permute-start.6 = (f32[296,128]{1,0:T(8,128)S(1)}, f32[296,128]{1,0:T(8,128)S(1)}, u32[]{:S(2)}, u32[]{:S(2)}) collective-permute-start(f32[296,128]{1,0:T(8,128)S(1)} %get-tuple-element.43), channel_id=1, source_target_pairs={{0,1},{1,2},{2,3},{3,0},{4,5},{5,6},{6,7},{7,4},{8,9},{9,10},{10,1... | collective-permute-start | bytes 454664 | tf_op jit(solution)/shard_map/ppermute | solution.py:877
  20.4 6.3 %copy-start.19 = (bf16[64,192]{1,0:T(8,128)(2,1)S(1)}, bf16[64,192]{1,0:T(8,128)(2,1)}, u32[]{:S(2)}) copy-start(bf16[64,192]{1,0:T(8,128)(2,1)} %constant.67.clone.xt) | copy-start | bytes 73732
  20.4 7.1 %copy-start.5 = (bf16[512,512]{1,0:T(8,128)(2,1)S(1)}, bf16[512,512]{1,0:T(8,128)(2,1)}, u32[]{:S(2)}) copy-start(bf16[512,512]{1,0:T(8,128)(2,1)} %constant.68.clone.t2) | copy-start | bytes 1572868
  20.4 7.1 %copy-start.9 = (bf16[256,512]{1,0:T(8,128)(2,1)S(1)}, bf16[256,512]{1,0:T(8,128)(2,1)}, u32[]{:S(2)}) copy-start(bf16[256,512]{1,0:T(8,128)(2,1)} %constant.69.clone.t3) | copy-start | bytes 786436
  20.4 7.1 %copy-start.11 = (bf16[128,512]{1,0:T(8,128)(2,1)S(1)}, bf16[128,512]{1,0:T(8,128)(2,1)}, u32[]{:S(2)}) copy-start(bf16[128,512]{1,0:T(8,128)(2,1)} %constant.71.clone.yf) | copy-start | bytes 393220
  20.4 7.1 %copy-start.17 = (bf16[256,48]{1,0:T(8,128)(2,1)S(1)}, bf16[256,48]{1,0:T(8,128)(2,1)}, u32[]{:S(2)}) copy-start(bf16[256,48]{1,0:T(8,128)(2,1)} %constant.70.clone.xf) | copy-start | bytes 73732
